TPU v7x, 32 devices: a whole 2x2x4 slice. The times are simulated.
32 devices in a mesh: parts: 2 (over y), dp: 4 (over x, core), tensor: 4 (over z).
Axes of the slice: x: 2, y: 2, z: 4, core: 2. Of those that a mesh axis runs over, the one named last changes fastest.
Arguments:
- acts: bfloat16 [4096, 4096], P(('parts', 'dp'), 'tensor'), parts along dimension 0, may hold values from -6 to 6
- out_grad: bfloat16 [4096, 4096], P(('parts', 'dp'), 'tensor'), parts along dimension 0, may hold values from -6 to 6
- lengths: int32 [16], P(('parts', 'dp')), parts along dimension 0, may hold values from 64 to 256, as said below
- w_gate: bfloat16 [4096, 14336], P('dp', 'tensor'), may hold values from -0.09375 to 0.09375
- w_up: bfloat16 [4096, 14336], P('dp', 'tensor'), may hold values from -0.09375 to 0.09375
- w_down_t: bfloat16 [4096, 14336], P('dp', 'tensor'), may hold values from -0.09375 to 0.09375
- d_proj: bfloat16 [3, 4096, 64], replicated, may hold values from -0.09375 to 0.09375
- ff_proj: bfloat16 [3, 14336, 64], P(None, 'tensor'), may hold values from -0.046875 to 0.046875
- queries: bfloat16 [128, 12288], P(('dp', 'tensor')), may hold values from -0.0068359375 to 0.0068359375
Outputs:
- scores: float32 [16, 4, 32], P(('parts', 'dp'), None, 'tensor'), parts along dimension 0
There are 2 independent parts, one for each index of `parts`. A program takes and returns all parts, laid end to end along the dimension named above; an argument that names none is the same for every part. Nothing has to cross between parts.
Inputs may be any that keep to these rules, and one draw needn't show every extreme that they name: `lengths`: every sequence has at least 64 valid tokens, and some sequence of each part has all 256.
All inputs are finite; a program needn't handle non-finite values.
Results may differ from a plain program's by a relative error of at most 0.0042.
Values may be sent and summed in bfloat16 or wider, within the bound.
No kernel may reach another device: no remote copies, remote signals or barrier semaphores. Data moves between devices by JAX's collectives and lax.ppermute only.
A program may use at most 256 MiB of HBM per device.

v0:
```python
import jax
import jax.numpy as jnp
from jax import lax
from jax.sharding import PartitionSpec as P


def outer_sum(left, right, seq_count, length, rank):
    left_seq = left.reshape(seq_count, length, rank)
    right_seq = right.reshape(seq_count, length, rank)
    return jnp.einsum("slr,slk->srk", left_seq, right_seq, precision=lax.Precision.HIGHEST)


def add_rows(source, shard_rows):
    return jnp.dot(source, shard_rows, preferred_element_type=jnp.float32)


def body(acts, out_grad, lengths, w_gate, w_up, w_down_t, d_proj, ff_proj, queries):
    seq_dev = lengths.shape[0]
    tokens = acts.shape[0]
    length = tokens // seq_dev
    rank = d_proj.shape[2]
    positions = jnp.arange(length, dtype=jnp.int32)
    keep_mask = (positions[None, :] < lengths[:, None]).astype(jnp.bfloat16).reshape(tokens, 1)
    full_acts, full_grad = (
        lax.all_gather(acts, "tensor", axis=1, tiled=True),
        lax.all_gather(out_grad, "tensor", axis=1, tiled=True),
    )
    masked_grad = full_grad * keep_mask
    gate_pre = add_rows(full_acts, lax.all_gather(w_gate, "dp", axis=0, tiled=True))
    up_pre = add_rows(full_acts, lax.all_gather(w_up, "dp", axis=0, tiled=True))
    back_grad = add_rows(masked_grad, lax.all_gather(w_down_t, "dp", axis=0, tiled=True))
    sigmoid_gate = jax.nn.sigmoid(gate_pre)
    silu_gate = gate_pre * sigmoid_gate
    hidden = (silu_gate * up_pre).astype(jnp.bfloat16)
    grad_gate = (
        back_grad * up_pre * sigmoid_gate * (1.0 + gate_pre * (1.0 - sigmoid_gate))
    ).astype(jnp.bfloat16)
    grad_up = (back_grad * silu_gate).astype(jnp.bfloat16)
    left_gate = jnp.dot(full_acts, d_proj[0], preferred_element_type=jnp.float32)
    left_up = jnp.dot(full_acts, d_proj[1], preferred_element_type=jnp.float32)
    right_down = jnp.dot(masked_grad, d_proj[2], preferred_element_type=jnp.float32)
    right_gate = jnp.dot(grad_gate, ff_proj[0], preferred_element_type=jnp.float32)
    right_up = jnp.dot(grad_up, ff_proj[1], preferred_element_type=jnp.float32)
    left_down = jnp.dot(hidden, ff_proj[2], preferred_element_type=jnp.float32)
    partial_proj = jnp.stack(
        [
            outer_sum(left_gate, right_gate, seq_dev, length, rank),
            outer_sum(left_up, right_up, seq_dev, length, rank),
            outer_sum(left_down, right_down, seq_dev, length, rank),
        ],
        axis=1,
    )
    partial_proj = partial_proj.reshape(seq_dev, 3 * rank * rank)
    seq_proj = lax.psum(partial_proj, "tensor")
    proj_b = seq_proj.astype(jnp.bfloat16)
    query_dev = queries.shape[0]
    dp_count = lax.axis_size("dp")
    flat_scores = lax.dot_general(
        proj_b,
        lax.all_gather(queries, "dp", axis=0, tiled=True),
        (((1,), (1,)), ((), ())),
        preferred_element_type=jnp.float32,
    )
    scores = flat_scores.reshape(seq_dev, dp_count, query_dev)
    return scores


def solution(mesh):
    in_specs = (
        P(("parts", "dp"), "tensor"),
        P(("parts", "dp"), "tensor"),
        P(("parts", "dp")),
        P("dp", "tensor"),
        P("dp", "tensor"),
        P("dp", "tensor"),
        P(),
        P(None, "tensor", None),
        P(("dp", "tensor"), None),
    )
    out_specs = P(("parts", "dp"), None, "tensor")
    return jax.shard_map(body, mesh=mesh, in_specs=in_specs, out_specs=out_specs, check_vma=False)
```

profile of v0, /device:TPU:0, one launch (start us, length us, event | category | flops | bytes accessed | tf_op | source)
XLA Modules:
  0.0 776.7 jit_solution(1040278988086690871)
XLA Ops:
  6.5 0.0 all-gather.6.cloned.1.call-start
  6.5 0.7 all-gather.6.cloned.1.call-update
  7.3 0.0 all-gather.8.cloned.1.call-start
  7.3 0.7 all-gather.8.cloned.1.call-update
  8.0 0.0 all-gather.12.cloned.1.call-start
  8.1 0.7 all-gather.12.cloned.1.call-update
  8.7 0.0 all-gather.10.cloned.1.call-start
  8.8 0.5 all-gather.10.cloned.1.call-update
  9.3 0.0 copy-start.7
  9.3 0.0 copy-start.6
  9.3 0.0 copy-start.4
  9.3 0.0 all-gather.14.cloned.1.call-start
  9.4 0.5 all-gather.14.cloned.1.call-update
  9.9 0.0 copy-done.7
  10.0 0.1 fusion.21
  10.1 0.2 copy-done.6
  10.3 10.0 %all_gather.23 = bf16[32,12288]{1,0:T(8,128)(2,1)S(1)} all-gather(bf16[8,12288]{1,0:T(8,128)(2,1)S(1)} %copy-done.6), channel_id=1, replica_groups=mesh['parts'=2,'dp'=4,'tensor'=4] {'dp'}, dimensions={0}, use_global_device_ids=true | all-gather | bytes 983040 | tf_op jit(solution)/shard_map/all_gather | solution.py:60
  20.3 72.1 %all-gather.6.cloned.1.call-done = bf16[512,4096]{1,0:T(8,128)(2,1)} async-done(((bf16[512,1024]{1,0:T(8,128)(2,1)}), bf16[512,4096]{1,0:T(8,128)(2,1)}) %all-gather.6.cloned.1.call-update) | async-done | bytes 4194320 | tf_op jit(solution)/shard_map/all_gather | solution.py:25
  92.4 0.0 copy-start
  92.4 0.0 copy-done.4
  92.4 3.7 fusion.3
  96.2 0.0 copy-done
  96.2 1.4 fusion.5
  97.6 75.7 %all-gather.8.cloned.1.call-done = bf16[512,4096]{1,0:T(8,128)(2,1)} async-done(((bf16[512,1024]{1,0:T(8,128)(2,1)}), bf16[512,4096]{1,0:T(8,128)(2,1)}) %all-gather.8.cloned.1.call-update) | async-done | bytes 4194320 | tf_op jit(solution)/shard_map/all_gather | solution.py:26
  173.3 2.5 broadcast_multiply_fusion
  175.8 0.0 copy-start.1
  175.9 2.0 copy-done.1
  177.8 1.4 fusion.1
  179.2 172.3 %all-gather.12.cloned.1.call-done = bf16[4096,3584]{1,0:T(8,128)(2,1)} async-done(((bf16[1024,3584]{1,0:T(8,128)(2,1)}), bf16[4096,3584]{1,0:T(8,128)(2,1)}) %all-gather.12.cloned.1.call-update) | async-done | bytes 29360144 | tf_op jit(solution)/shard_map/all_gather | solution.py:30
  351.5 23.7 %fusion.23 = f32[512,3584]{1,0:T(8,128)} fusion(bf16[512,4096]{1,0:T(8,128)(2,1)} %all-gather.6.cloned.1.call-done, bf16[4096,3584]{1,0:T(8,128)(2,1)} %all-gather.12.cloned.1.call-done), kind=kOutput, calls=%fused_computation.33 | convolution fusion | flops 15032385536 | bytes 40894464 | tf_op jit(solution)/shard_map/dot_general | solution.py:14
  375.2 155.7 %all-gather.10.cloned.1.call-done = bf16[4096,3584]{1,0:T(8,128)(2,1)} async-done(((bf16[1024,3584]{1,0:T(8,128)(2,1)}), bf16[4096,3584]{1,0:T(8,128)(2,1)}) %all-gather.10.cloned.1.call-update) | async-done | bytes 29360144 | tf_op jit(solution)/shard_map/all_gather | solution.py:31
  530.9 23.8 %fusion.22 = f32[512,3584]{1,0:T(8,128)} fusion(bf16[512,4096]{1,0:T(8,128)(2,1)} %copy-done.1, bf16[4096,3584]{1,0:T(8,128)(2,1)} %all-gather.10.cloned.1.call-done), kind=kOutput, calls=%fused_computation.32 | convolution fusion | flops 15032385536 | bytes 40894464 | tf_op jit(solution)/shard_map/dot_general | solution.py:14
  554.7 0.0 copy-start.5
  554.7 155.7 %all-gather.14.cloned.1.call-done = bf16[4096,3584]{1,0:T(8,128)(2,1)} async-done(((bf16[1024,3584]{1,0:T(8,128)(2,1)}), bf16[4096,3584]{1,0:T(8,128)(2,1)}) %all-gather.14.cloned.1.call-update) | async-done | bytes 29360144 | tf_op jit(solution)/shard_map/all_gather | solution.py:29
  710.4 31.7 %multiply_convert_fusion.2 = (bf16[512,3584]{1,0:T(8,128)(2,1)}, bf16[512,3584]{1,0:T(8,128)(2,1)}, bf16[512,3584]{1,0:T(8,128)(2,1)}) fusion(f32[512,3584]{1,0:T(8,128)} %fusion.22, f32[512,3584]{1,0:T(8,128)} %fusion.23, bf16[512,4096]{1,0:T(8,128)(2,1)} %all-gather.6.cloned.1.call-done, bf16[4096,3584]{1,0:T(8,128)(2,1)} %all-gather.14.cloned.1.call-done), kind=kOutput, calls=%fused_computation.2 | convolution fusion | flops 15059910656 | bytes 59244544 | tf_op jit(solution)/shard_map/dot_general | solution.py:14
  742.1 0.0 copy-start.3
  742.1 0.0 copy-done.5
  742.1 0.0 copy-start.2
  742.1 3.4 fusion.12
  745.5 0.0 copy-done.3
  745.5 1.2 fusion.14
  746.8 0.0 copy-done.2
  746.8 1.2 fusion.10
  748.0 0.3 convolution_bitcast_fusion.1
  748.3 0.3 convolution_bitcast_fusion.2
  748.5 0.3 convolution_bitcast_fusion
  748.8 0.1 reshape.37
  749.0 20.2 %psum.7 = bf16[2,12288]{1,0:T(2,128)(2,1)S(1)} all-reduce(f32[2,12288]{1,0:T(2,128)S(1)} %reshape.37), channel_id=1, replica_groups=mesh['parts'=2,'dp'=4,'tensor'=4] {'tensor'}, use_global_device_ids=true, to_apply=%region_0.0 | all-reduce | flops 24576 | bytes 147456 | tf_op jit(solution)/shard_map/psum | solution.py:54
  769.1 0.3 fusion.24
  769.4 0.7 reshape.38
  (3 shorter events, 0.0 us)
Async XLA Ops:
  6.5 85.9 %all-gather.6.cloned.1.call-start = ((), (), s32[]{:S(2)}) async-start(), calls=%async_computation | async-start | bytes 5242880 | tf_op jit(solution)/shard_map/all_gather | solution.py:25
  7.3 166.1 %all-gather.8.cloned.1.call-start = ((), (), s32[]{:S(2)}) async-start(), calls=%async_computation.1 | async-start | bytes 5242880 | tf_op jit(solution)/shard_map/all_gather | solution.py:26
  8.0 343.5 %all-gather.12.cloned.1.call-start = ((), (), s32[]{:S(2)}) async-start(), calls=%async_computation.3 | async-start | bytes 36700160 | tf_op jit(solution)/shard_map/all_gather | solution.py:30
  8.7 522.2 %all-gather.10.cloned.1.call-start = ((), (), s32[]{:S(2)}) async-start(), calls=%async_computation.2 | async-start | bytes 36700160 | tf_op jit(solution)/shard_map/all_gather | solution.py:31
  9.3 0.7 copy-start.7
  9.3 0.9 copy-start.6
  9.3 83.1 %copy-start.4 = (bf16[3,4096,64]{1,2,0:T(8,128)(2,1)S(1)}, bf16[3,4096,64]{1,2,0:T(8,128)(2,1)}, u32[]{:S(2)}) copy-start(bf16[3,4096,64]{1,2,0:T(8,128)(2,1)} %param.15) | copy-start | bytes 4718596
  9.3 701.1 %all-gather.14.cloned.1.call-start = ((), (), s32[]{:S(2)}) async-start(), calls=%async_computation.4 | async-start | bytes 36700160 | tf_op jit(solution)/shard_map/all_gather | solution.py:29
  92.4 3.7 copy-start
  175.8 2.0 copy-start.1
  554.7 187.4 %copy-start.5 = (bf16[3,3584,64]{1,2,0:T(8,128)(2,1)S(1)}, bf16[3,3584,64]{1,2,0:T(8,128)(2,1)}, u32[]{:S(2)}) copy-start(bf16[3,3584,64]{1,2,0:T(8,128)(2,1)} %param.16) | copy-start | bytes 4128772
  742.1 3.4 copy-start.3
  742.1 4.6 copy-start.2
Sparse Core Ops, SparseCore 0:
  8.9 83.4 all-gather.5
  94.0 79.2 all-gather.7
  174.9 176.5 all-gather.11
  352.9 177.9 all-gather.9
  532.4 177.9 all-gather.13
where the time goes:
time: 777 us
  waiting for transfers between devices  635 us (82%)
  matrix products  92.7 us (12%)
  blocking collectives  30.2 us (4%)
  between operations  13.3 us (2%)
    all_gather x1, waiting for transfers between devices, body(): up_pre = add_rows(full_acts, lax.all_gather(w_up, 'dp', axis=0, tiled=True))  172 us
    all_gather x1, waiting for transfers between devices, body(): lax.all_gather(w_down_t, 'dp', axis=0, tiled=True)  156 us
    all_gather x1, waiting for transfers between devices, body(): lax.all_gather(w_gate, 'dp', axis=0, tiled=True)  156 us
    dot_general x3, matrix products, add_rows(): return jnp.dot(source, shard_rows, preferred_element_type=jnp.float32)  79.2 us
    all_gather x1, waiting for transfers between devices, body(): lax.all_gather(out_grad, 'tensor', axis=1, tiled=True)  75.7 us
    all_gather x1, waiting for transfers between devices, body(): lax.all_gather(acts, 'tensor', axis=1, tiled=True)  72.1 us
    psum x1, blocking collectives, body(): seq_proj = lax.psum(partial_proj, 'tensor')  20.2 us
  transfers between devices with their start and end apart: 5, of which 5 were waited for; matrix products, arithmetic and copies ran while one was open for 7% of the time, Pallas kernels for 0%

commit v1 on v0

v1 whole, which is shorter than its diff:
```python
import jax
import jax.numpy as jnp
from jax import lax
from jax.experimental import pallas as pl
from jax.experimental.pallas import tpu as pltpu
from jax.sharding import PartitionSpec as P

HIGHEST = lax.Precision.HIGHEST


def dot(left, right):
    return jnp.dot(left, right, preferred_element_type=jnp.float32)


def activations(gate_pre, up_pre, back_grad):
    sigmoid_gate = jax.nn.sigmoid(gate_pre)
    silu_gate = gate_pre * sigmoid_gate
    hidden = (silu_gate * up_pre).astype(jnp.bfloat16)
    grad_gate = (
        back_grad * up_pre * sigmoid_gate * (1.0 + gate_pre * (1.0 - sigmoid_gate))
    ).astype(jnp.bfloat16)
    grad_up = (back_grad * silu_gate).astype(jnp.bfloat16)
    return hidden, grad_gate, grad_up


def outer_sum(left, right, length):
    rank = left.shape[1]
    left_seq = left.reshape(-1, length, rank)
    right_seq = right.reshape(-1, length, rank)
    return jnp.einsum("slr,slk->srk", left_seq, right_seq, precision=HIGHEST)


def mask_tokens(out_grad, lengths):
    length = out_grad.shape[0] // lengths.shape[0]
    positions = jnp.arange(length, dtype=jnp.int32)
    keep = positions[None, :] < lengths[:, None]
    return out_grad * keep.astype(out_grad.dtype).reshape(-1, 1)


def gathered_body(acts, out_grad, lengths, w_gate, w_up, w_down_t, d_proj, ff_proj, queries):
    seq_dev = lengths.shape[0]
    length = acts.shape[0] // seq_dev
    rank = d_proj.shape[2]
    full_acts = lax.all_gather(acts, "tensor", axis=1, tiled=True)
    masked_grad = lax.all_gather(mask_tokens(out_grad, lengths), "tensor", axis=1, tiled=True)
    gate_pre = dot(full_acts, lax.all_gather(w_gate, "dp", axis=0, tiled=True))
    up_pre = dot(full_acts, lax.all_gather(w_up, "dp", axis=0, tiled=True))
    back_grad = dot(masked_grad, lax.all_gather(w_down_t, "dp", axis=0, tiled=True))
    hidden, grad_gate, grad_up = activations(gate_pre, up_pre, back_grad)
    proj = jnp.stack(
        [
            outer_sum(dot(full_acts, d_proj[0]), dot(grad_gate, ff_proj[0]), length),
            outer_sum(dot(full_acts, d_proj[1]), dot(grad_up, ff_proj[1]), length),
            outer_sum(dot(hidden, ff_proj[2]), dot(masked_grad, d_proj[2]), length),
        ],
        axis=1,
    )
    proj_b = lax.psum(proj.reshape(seq_dev, 3 * rank * rank), "tensor").astype(jnp.bfloat16)
    flat_scores = lax.dot_general(
        proj_b,
        lax.all_gather(queries, "dp", axis=0, tiled=True),
        (((1,), (1,)), ((), ())),
        preferred_element_type=jnp.float32,
    )
    return flat_scores.reshape(seq_dev, lax.axis_size("dp"), queries.shape[0])


def permute_dp(value, flip):
    return lax.ppermute(value, "dp", [(i, i ^ flip) for i in range(lax.axis_size("dp"))])


def permute_parts(value):
    return lax.ppermute(value, "parts", [(0, 1), (1, 0)])


def hidden_units_kernel(
    places, acts_ref, grad_ref, w_gate, w_up, w_down, near_ref, far_ref, relayed_ref, ff_ref, sums_in, sums_ref
):
    half = far_ref.shape[1] // 2
    depth = w_gate.shape[0]

    def columns(ref, k, size):
        return ref[:, pl.ds(pl.multiple_of(places[k], half), size)]

    def pre(ref, own, m):
        total = dot(columns(ref, 1, depth), own[...])
        total += dot(columns(ref, 2, depth), near_ref[m])
        for k, held in ((3, far_ref), (5, relayed_ref)):
            total += dot(columns(ref, k, half), held[m, :half])
            total += dot(columns(ref, k + 1, half), held[m, half:])
        return total

    hidden, grad_gate, grad_up = activations(pre(acts_ref, w_gate, 0), pre(acts_ref, w_up, 1), pre(grad_ref, w_down, 2))
    rank = ff_ref.shape[2]
    for m, value in enumerate((grad_gate, grad_up, hidden)):
        at = slice(m * rank, (m + 1) * rank)
        sums_ref[:, at] = sums_in[:, at] + dot(value, ff_ref[m])


def add_hidden_units(places, acts, grad, weights, near_rows, far, relayed, ff_proj, sums, tile):
    tokens, model = acts.shape
    depth = weights[0].shape[0]
    chunk = near_rows.shape[2]
    by_tile = lambda i, places: (i, 0)
    own = pl.BlockSpec((depth, chunk), lambda i, places: (0, places[0]))
    whole = lambda v: pl.BlockSpec(v.shape, lambda i, places: (0, 0, 0))
    return pl.pallas_call(
        hidden_units_kernel,
        out_shape=jax.ShapeDtypeStruct(sums.shape, sums.dtype),
        grid_spec=pltpu.PrefetchScalarGridSpec(
            num_scalar_prefetch=1,
            grid=(tokens // tile,),
            in_specs=[
                pl.BlockSpec((tile, model), by_tile),
                pl.BlockSpec((tile, model), by_tile),
                own,
                own,
                own,
                whole(near_rows),
                whole(far),
                whole(relayed),
                pl.BlockSpec((3, chunk, ff_proj.shape[2]), lambda i, places: (0, places[0], 0)),
                pl.BlockSpec((tile, sums.shape[1]), by_tile),
            ],
            out_specs=pl.BlockSpec((tile, sums.shape[1]), by_tile),
        ),
        input_output_aliases={10: 0},
        compiler_params=pltpu.CompilerParams(vmem_limit_bytes=48 * 2**20),
        cost_estimate=pl.CostEstimate(flops=1000, bytes_accessed=1000, transcendentals=0),
    )(places, acts, grad, *weights, near_rows, far, relayed, ff_proj, sums)


def relayed_body(acts, out_grad, lengths, w_gate, w_up, w_down_t, d_proj, ff_proj, queries):
    seq_dev = lengths.shape[0]
    tokens, depth_acts = acts.shape
    length = tokens // seq_dev
    rank = d_proj.shape[2]
    depth = w_gate.shape[0]
    me = lax.axis_index("dp")
    near = lax.rem(me, 2)
    part = lax.axis_index("parts")
    half = w_gate.shape[1] // 2
    chunk = 256
    chunks = half // chunk
    row_half = depth // 2
    weights = (w_gate, w_up, w_down_t)

    def piece(side, j, row_at=0, rows=depth):
        start = side * half + j * chunk
        return jnp.stack([lax.dynamic_slice(w, (row_at, start), (rows, chunk)) for w in weights])

    near_rows, far, relayed = [], [], []
    for j in range(chunks):
        near_rows.append(permute_dp(piece(1 - near, j), 1))
        out = jnp.concatenate(
            [
                piece(near, j, part * row_half, row_half),
                lax.dynamic_slice_in_dim(near_rows[j], part * row_half, row_half, 1),
            ],
            axis=1,
        )
        if j >= 2:
            out, far[j - 2] = lax.optimization_barrier((out, far[j - 2]))
        far.append(permute_dp(out, 2))

    def gathered(value):
        own = lax.all_gather(value, "tensor", axis=1, tiled=True)
        return jnp.concatenate([own, permute_dp(own, 1)], axis=0)

    full_acts = gathered(acts)
    full_grad = gathered(mask_tokens(out_grad, lengths))
    left_both = dot(full_acts, jnp.concatenate([d_proj[0], d_proj[1]], axis=1))
    right_down = dot(full_grad, d_proj[2])
    sums = jnp.zeros((2 * tokens, 3 * rank), jnp.float32)

    def add(j, sums):
        starts = [near * chunks + j, me * depth, (me ^ 1) * depth]
        starts += [(me ^ flip) * depth + side * row_half for side in (part, 1 - part) for flip in (2, 3)]
        places = jnp.stack([jnp.asarray(s, jnp.int32) for s in starts])
        return add_hidden_units(
            places, full_acts, full_grad, weights, near_rows[j], far[j], relayed[j], ff_proj, sums, 256
        )

    gates = {chunks - 2: 2, chunks - 1: 5}
    done = 0
    for j in range(chunks):
        value = far[j]
        if j >= 1:
            value, relayed[j - 1] = lax.optimization_barrier((value, relayed[j - 1]))
        for k in range(done, gates.get(j, done)):
            sums = add(k, sums)
        if gates.get(j, done) > done:
            done = gates[j]
            value, sums = lax.optimization_barrier((value, sums))
        far[j] = value
        relayed.append(permute_parts(value))
    for k in range(done, chunks):
        sums = add(k, sums)
    right_gate, right_up, left_down = jnp.split(sums, 3, axis=1)
    proj = jnp.stack(
        [
            outer_sum(left_both[:, :rank], right_gate, length),
            outer_sum(left_both[:, rank:], right_up, length),
            outer_sum(left_down, right_down, length),
        ],
        axis=1,
    ).reshape(2 * seq_dev, 3 * rank * rank)
    proj = proj[:seq_dev] + permute_dp(proj[seq_dev:], 1)
    proj_b = lax.psum(proj, "tensor").astype(jnp.bfloat16)
    flat_scores = lax.dot_general(
        proj_b,
        lax.all_gather(queries, "dp", axis=0, tiled=True),
        (((1,), (1,)), ((), ())),
        preferred_element_type=jnp.float32,
    )
    return flat_scores.reshape(seq_dev, lax.axis_size("dp"), queries.shape[0])


def solution(mesh):
    in_specs = (
        P(("parts", "dp"), "tensor"),
        P(("parts", "dp"), "tensor"),
        P(("parts", "dp")),
        P("dp", "tensor"),
        P("dp", "tensor"),
        P("dp", "tensor"),
        P(),
        P(None, "tensor", None),
        P(("dp", "tensor"), None),
    )
    out_specs = P(("parts", "dp"), None, "tensor")
    relayed = mesh.shape["dp"] == 4 and mesh.shape["parts"] == 2
    body = relayed_body if relayed else gathered_body
    return jax.shard_map(body, mesh=mesh, in_specs=in_specs, out_specs=out_specs, check_vma=False)
```

time: 777 us -> 387 us (0.50)
  waiting for transfers between devices: 635 us -> 154 us
  Pallas kernels: 0 us -> 92.9 us
  matrix products: 92.7 us -> 14.6 us
  local copies, waits for them, and re-layouts: 3.07 us -> 43.2 us
  starting transfers between devices: 0.15 us -> 23.8 us
  other arithmetic: 2.62 us -> 17 us
    all_gather x5 -> x2, waiting for transfers between devices: 632 us -> 32.2 us  [gathered(): own = lax.all_gather(value, 'tensor', axis=1, tiled=True)]
    ppermute x0 -> x24, waiting for transfers between devices: none -> 122 us  [the longest x17 114 us: permute_dp(): lax.ppermute(value, 'dp', [(i, i ^ flip) for i in range(lax.axis_size('dp...]
    pallas_call x0 -> x7, Pallas kernels: none -> 92.9 us  [add_hidden_units(): pl.pallas_call(hidden_units_kernel, out_shape=jax.ShapeDtypeStruct(sums.s...]
    dot_general x13 -> x6, matrix products: 92.7 us -> 14.6 us  [the longest x2 12.4 us: dot(): return jnp.dot(left, right, preferred_element_type=jnp.float32)]
    ppermute x0 -> x24, starting transfers between devices: none -> 23.8 us  [the longest x17 13.2 us: permute_dp(): lax.ppermute(value, 'dp', [(i, i ^ flip) for i in range(lax.axis_size('dp...]
    another operation x1 -> x11, local copies, waits for them, and re-layouts: 0.01 us -> 14.1 us  [the longest x4 13.5 us: piece(): jnp.stack([lax.dynamic_slice(w, (row_at, start), (rows, chunk)) for w in...]
    unnamed x17 -> x74, local copies, waits for them, and re-layouts: 2.23 us -> 15.5 us
  transfers between devices with their start and end apart: 5 -> 26, of which waited for: 5 -> 8; matrix products, arithmetic and copies ran while one was open for 7% -> 15% of each run, Pallas kernels for 0% -> 21%
where the time goes in v1:
time: 387 us; the launch traced here: 386 us
  waiting for transfers between devices  154 us (40%)
  Pallas kernels  92.9 us (24%)
  local copies, waits for them, and re-layouts  43.2 us (11%)
  blocking collectives  26.6 us (7%)
  starting transfers between devices  23.8 us (6%)
  other arithmetic  17 us (4%)
  matrix products  14.6 us (4%)
  between operations  14.1 us (4%)
    ppermute x17, waiting for transfers between devices, permute_dp(): lax.ppermute(value, 'dp', [(i, i ^ flip) for i in range(lax.axis_size('dp...  114 us
    pallas_call x7, Pallas kernels, add_hidden_units(): pl.pallas_call(hidden_units_kernel, out_shape=jax.ShapeDtypeStruct(sums.s...  92.9 us
    all_gather x2, waiting for transfers between devices, gathered(): own = lax.all_gather(value, 'tensor', axis=1, tiled=True)  32.2 us
    psum x1, blocking collectives, relayed_body(): proj_b = lax.psum(proj, 'tensor').astype(jnp.bfloat16)  17.7 us
    unnamed x74, local copies, waits for them, and re-layouts  15.5 us
    another operation x4, local copies, waits for them, and re-layouts, piece(): jnp.stack([lax.dynamic_slice(w, (row_at, start), (rows, chunk)) for w in...  13.5 us
    ppermute x17, starting transfers between devices, permute_dp(): lax.ppermute(value, 'dp', [(i, i ^ flip) for i in range(lax.axis_size('dp...  13.2 us
    dot_general x2, matrix products, dot(): return jnp.dot(left, right, preferred_element_type=jnp.float32)  12.4 us
  transfers between devices with their start and end apart: 26, of which 8 were waited for; matrix products, arithmetic and copies ran while one was open for 15% of the time, Pallas kernels for 21%

profile of v1, /device:TPU:0, one launch (start us, length us, event | category | flops | bytes accessed | tf_op | source)
XLA Modules:
  0.0 386.2 jit_solution(7721086484735358061)
XLA Ops:
  6.5 0.7 fusion.13
  7.3 2.4 broadcast_multiply_fusion
  9.8 3.6 dynamic-slice_bitcast_fusion.2
  13.4 1.4 copy-done.10
  14.8 4.2 %dynamic-slice_bitcast_fusion = (bf16[1,1024,256]{2,1,0:T(8,128)(2,1)}, bf16[1,1024,256]{2,1,0:T(8,128)(2,1)}, bf16[1,1024,256]{2,1,0:T(8,128)(2,1)}, bf16[1,102...) fusion(bf16[1024,3584]{1,0:T(8,128)(2,1)} %w_down.13, ...), kind=kLoop, calls=%fused_computation.24 | loop fusion | bytes 14680092 | tf_op jit(solution)/shard_map/stack | solution.py:150
  19.0 1.4 pad_maximum_fusion.6
  20.8 1.4 pad_maximum_fusion.4
  22.8 1.3 pad_maximum_fusion.12
  24.3 2.4 dynamic-slice_bitcast_fusion.23
  26.6 3.3 dynamic-slice_bitcast_fusion.21
  29.9 1.2 constant_dynamic-slice_fusion.3
  31.2 3.0 collective-permute-start.6
  34.5 1.2 constant_dynamic-slice_fusion
  35.8 1.2 collective-permute-start.13
  37.1 1.3 pad_maximum_fusion.5
  38.5 31.0 %collective-permute-done.6.far_ref = bf16[3,1024,256]{2,1,0:T(8,128)(2,1)S(1)} collective-permute-done((bf16[3,1024,256]{2,1,0:T(8,128)(2,1)S(1)}, bf16[3,1024,256]{2,1,0:T(8,128)(2,1)S(1)}, u32[]{:S(2)}, u32[]{:S(2)}) %collective-permute-start.6) | collective-permute-done | bytes 1572896 | tf_op jit(solution)/shard_map/ppermute | solution.py:69
  69.4 2.1 collective-permute-start.16
  71.9 1.2 pad_maximum_fusion.11
  73.5 29.2 %collective-permute-done.13.far_ref = bf16[3,1024,256]{2,1,0:T(8,128)(2,1)} collective-permute-done((bf16[3,1024,256]{2,1,0:T(8,128)(2,1)S(1)}, bf16[3,1024,256]{2,1,0:T(8,128)(2,1)}, u32[]{:S(2)}, u32[]{:S(2)}) %collective-permute-start.13) | collective-permute-done | bytes 1572896 | tf_op jit(solution)/shard_map/ppermute | solution.py:69
  102.6 1.7 collective-permute-start.7
  104.7 1.5 collective-permute-start.17
  106.2 1.4 pad_maximum_fusion.8
  107.6 1.5 collective-permute-start.14
  109.4 1.2 constant_dynamic-slice_fusion.5
  110.6 1.3 pad_maximum_fusion.3
  111.9 28.4 %collective-permute-done.7.far_ref = bf16[3,1024,256]{2,1,0:T(8,128)(2,1)} collective-permute-done((bf16[3,1024,256]{2,1,0:T(8,128)(2,1)}, bf16[3,1024,256]{2,1,0:T(8,128)(2,1)}, u32[]{:S(2)}, u32[]{:S(2)}) %collective-permute-start.7) | collective-permute-done | bytes 1572896 | tf_op jit(solution)/shard_map/ppermute | solution.py:69
  140.3 1.8 collective-permute-start.18
  142.1 32.2 %all-gather.3.cloned.1.call-done = bf16[512,4096]{1,0:T(8,128)(2,1)} async-done(((bf16[512,1024]{1,0:T(8,128)(2,1)}), bf16[512,4096]{1,0:T(8,128)(2,1)}) %all-gather.3.cloned.1.call-update) | async-done | bytes 4194320 | tf_op jit(solution)/shard_map/all_gather | solution.py:167
  174.2 1.3 pad_maximum_fusion
  176.1 1.5 collective-permute-start.8
  177.6 1.2 constant_dynamic-slice_fusion.2
  178.8 1.2 pad_maximum_fusion.9
  180.1 1.5 collective-permute-start.19
  181.5 2.6 copy.45.ff_ref
  184.3 1.3 constant_dynamic-slice_fusion.6
  185.7 1.3 pad_maximum_fusion.1
  187.0 1.1 collective-permute-start.15
  188.1 25.6 %collective-permute-done.8.far_ref = bf16[3,1024,256]{2,1,0:T(8,128)(2,1)} collective-permute-done((bf16[3,1024,256]{2,1,0:T(8,128)(2,1)}, bf16[3,1024,256]{2,1,0:T(8,128)(2,1)}, u32[]{:S(2)}, u32[]{:S(2)}) %collective-permute-start.8) | collective-permute-done | bytes 1572896 | tf_op jit(solution)/shard_map/ppermute | solution.py:69
  213.7 1.5 collective-permute-start.9
  215.4 1.0 collective-permute-done.19.relayed_ref
  216.5 1.5 collective-permute-start.20
  218.0 2.5 constant_dynamic-update-slice_fusion.1
  220.4 2.7 constant_dynamic-update-slice_fusion.2.grad_ref
  223.1 3.3 copy-done.8
  226.4 2.6 constant_dynamic-update-slice_fusion.acts_ref
  229.1 3.3 copy-done.9
  232.4 12.7 %shard_map.91.sums_in = f32[1024,192]{1,0:T(8,128)S(1)} custom-call(s32[7]{0:T(128)S(1)} %stack.343.places, bf16[1024,4096]{1,0:T(8,128)(2,1)} %copy-done.9, bf16[1024,4096]{1,0:T(8,128)(2,1)} %copy-done.8, bf16[1024,3584]{1,0:T(8,128)(2,1)} %w_gate.13, bf16[1024,3584]{1,0:T(8,128)(2,1)} %w_up.13, ...), custom_call_target="tpu_custom_call", output_to_operand_aliasing={{}: (10, {})} | custom-call | flops 1000 | bytes 1000 | tf_op jit(solution)/shard_map/pallas_call | solution.py:107
  245.1 13.6 %shard_map.92.sums_in = f32[1024,192]{1,0:T(8,128)S(1)} custom-call(s32[7]{0:T(128)S(1)} %stack.341.places, bf16[1024,4096]{1,0:T(8,128)(2,1)} %copy-done.9, bf16[1024,4096]{1,0:T(8,128)(2,1)} %copy-done.8, bf16[1024,3584]{1,0:T(8,128)(2,1)} %w_gate.13, bf16[1024,3584]{1,0:T(8,128)(2,1)} %w_up.13, ...), custom_call_target="tpu_custom_call", output_to_operand_aliasing={{}: (10, {})} | custom-call | flops 1000 | bytes 1000 | tf_op jit(solution)/shard_map/pallas_call | solution.py:107
  258.8 1.2 copy-done.6
  260.0 0.7 collective-permute-start.21
  260.9 13.2 %shard_map.93.sums_in = f32[1024,192]{1,0:T(8,128)S(1)} custom-call(s32[7]{0:T(128)S(1)} %stack.349.places, bf16[1024,4096]{1,0:T(8,128)(2,1)} %copy-done.9, bf16[1024,4096]{1,0:T(8,128)(2,1)} %copy-done.8, bf16[1024,3584]{1,0:T(8,128)(2,1)} %w_gate.13, bf16[1024,3584]{1,0:T(8,128)(2,1)} %w_up.13, ...), custom_call_target="tpu_custom_call", output_to_operand_aliasing={{}: (10, {})} | custom-call | flops 1000 | bytes 1000 | tf_op jit(solution)/shard_map/pallas_call | solution.py:107
  274.1 13.2 %shard_map.94.sums_in = f32[1024,192]{1,0:T(8,128)S(1)} custom-call(s32[7]{0:T(128)S(1)} %stack.347.places, bf16[1024,4096]{1,0:T(8,128)(2,1)} %copy-done.9, bf16[1024,4096]{1,0:T(8,128)(2,1)} %copy-done.8, bf16[1024,3584]{1,0:T(8,128)(2,1)} %w_gate.13, bf16[1024,3584]{1,0:T(8,128)(2,1)} %w_up.13, ...), custom_call_target="tpu_custom_call", output_to_operand_aliasing={{}: (10, {})} | custom-call | flops 1000 | bytes 1000 | tf_op jit(solution)/shard_map/pallas_call | solution.py:107
  287.3 13.4 %shard_map.95.sums_in = f32[1024,192]{1,0:T(8,128)S(1)} custom-call(s32[7]{0:T(128)S(1)} %stack.345.places, bf16[1024,4096]{1,0:T(8,128)(2,1)} %copy-done.9, bf16[1024,4096]{1,0:T(8,128)(2,1)} %copy-done.8, bf16[1024,3584]{1,0:T(8,128)(2,1)} %w_gate.13, bf16[1024,3584]{1,0:T(8,128)(2,1)} %w_up.13, ...), custom_call_target="tpu_custom_call", output_to_operand_aliasing={{}: (10, {})} | custom-call | flops 1000 | bytes 1000 | tf_op jit(solution)/shard_map/pallas_call | solution.py:107
  300.7 1.7 collective-permute-start.22
  302.4 0.9 slice_bitcast_fusion.1
  303.4 6.3 %fusion = f32[1024,128]{0,1:T(8,128)S(1)} fusion(bf16[1024,4096]{1,0:T(8,128)(2,1)} %copy-done.9, bf16[4096,64]{0,1:T(8,128)(2,1)} %get-tuple-element.100, bf16[4096,64]{0,1:T(8,128)(2,1)S(1)} %get-tuple-element.99), kind=kOutput, calls=%fused_computation.17 | convolution fusion | flops 1075838976 | bytes 9961472 | tf_op jit(solution)/shard_map/dot_general | solution.py:12
  309.8 6.1 %fusion.4 = f32[4,256,64]{1,2,0:T(8,128)S(1)} fusion(bf16[4,256,4096]{2,1,0:T(8,128)(2,1)} %bitcast.138, bf16[3,4096,64]{1,2,0:T(8,128)(2,1)} %param.15), kind=kOutput, calls=%fused_computation.21 | convolution fusion | flops 536870912 | bytes 9175040 | tf_op jit(solution)/shard_map/dot_general | solution.py:12
  315.9 13.6 %shard_map.96.sums_in = f32[1024,192]{1,0:T(8,128)S(1)} custom-call(s32[7]{0:T(128)S(1)} %stack.351.places, bf16[1024,4096]{1,0:T(8,128)(2,1)} %copy-done.9, bf16[1024,4096]{1,0:T(8,128)(2,1)} %copy-done.8, bf16[1024,3584]{1,0:T(8,128)(2,1)} %w_gate.13, bf16[1024,3584]{1,0:T(8,128)(2,1)} %w_up.13, ...), custom_call_target="tpu_custom_call", output_to_operand_aliasing={{}: (10, {})} | custom-call | flops 1000 | bytes 1000 | tf_op jit(solution)/shard_map/pallas_call | solution.py:107
  329.6 6.4 %collective-permute-done.22.relayed_ref = bf16[3,1024,256]{2,1,0:T(8,128)(2,1)S(1)} collective-permute-done((bf16[3,1024,256]{2,1,0:T(8,128)(2,1)}, bf16[3,1024,256]{2,1,0:T(8,128)(2,1)S(1)}, u32[]{:S(2)}, u32[]{:S(2)}) %collective-permute-start.22) | collective-permute-done | bytes 1572896 | tf_op jit(solution)/shard_map/ppermute | solution.py:73
  335.9 13.2 %shard_map.97 = f32[1024,192]{1,0:T(8,128)S(1)} custom-call(s32[7]{0:T(128)S(1)} %stack.283.places, bf16[1024,4096]{1,0:T(8,128)(2,1)} %copy-done.9, bf16[1024,4096]{1,0:T(8,128)(2,1)} %copy-done.8, bf16[1024,3584]{1,0:T(8,128)(2,1)} %w_gate.13, bf16[1024,3584]{1,0:T(8,128)(2,1)} %w_up.13, ...), custom_call_target="tpu_custom_call", output_to_operand_aliasing={{}: (10, {})} | custom-call | flops 1000 | bytes 1000 | tf_op jit(solution)/shard_map/pallas_call | solution.py:107
  350.2 1.0 convolution_bitcast_fusion
  351.6 8.8 %all_gather.11 = bf16[32,12288]{1,0:T(8,128)(2,1)S(1)} all-gather(bf16[8,12288]{1,0:T(8,128)(2,1)S(1)} %copy-done.34), channel_id=1, replica_groups=mesh['parts'=2,'dp'=4,'tensor'=4] {'dp'}, dimensions={0}, use_global_device_ids=true | all-gather | bytes 983040 | tf_op jit(solution)/shard_map/all_gather | solution.py:212
  360.6 17.7 %psum.7 = bf16[2,12288]{1,0:T(2,128)(2,1)S(1)} all-reduce(f32[2,12288]{1,0:T(2,128)S(1)} %add.256), channel_id=1, replica_groups=mesh['parts'=2,'dp'=4,'tensor'=4] {'tensor'}, use_global_device_ids=true, to_apply=%region_0.0 | all-reduce | flops 24576 | bytes 147456 | tf_op jit(solution)/shard_map/psum | solution.py:209
  378.7 0.7 reshape.47
  (127 shorter events, 6.6 us)
Async XLA Ops:
  6.5 102.5 %all-gather.5.cloned.1.call-start = ((), (), s32[]{:S(2)}) async-start(), calls=%async_computation.1 | async-start | bytes 5242880 | tf_op jit(solution)/shard_map/all_gather | solution.py:167
  9.7 164.5 %all-gather.3.cloned.1.call-start = ((), (), s32[]{:S(2)}) async-start(), calls=%async_computation | async-start | bytes 5242880 | tf_op jit(solution)/shard_map/all_gather | solution.py:167
  9.8 5.0 %copy-start.10 = (bf16[1024,3584]{1,0:T(8,128)(2,1)S(1)}, bf16[1024,3584]{1,0:T(8,128)(2,1)}, u32[]{:S(2)}) copy-start(bf16[1024,3584]{1,0:T(8,128)(2,1)} %w_up.13) | copy-start | bytes 22020100
  20.4 9.5 %collective-permute-start.5 = (bf16[3,1024,256]{2,1,0:T(8,128)(2,1)}, bf16[3,1024,256]{2,1,0:T(8,128)(2,1)}, u32[]{:S(2)}, u32[]{:S(2)}) collective-permute-start(bf16[3,1024,256]{2,1,0:T(8,128)(2,1)} %pad_maximum_fusion.6), channel_id=1, source_target_pairs={{0,4},{4,0},{8,12},{12,8},{1,5},{5,1},{9,13},{13,9},{2,6},{6,2},{1... | collective-permute-start | bytes 4718600 | tf_op jit(solution)/shard_map/ppermute | solution.py:69
  20.8 1.5 copy-start.21
  20.8 1.6 copy-start.22
  20.8 2.0 copy-start.23
  22.2 14.8 %collective-permute-start.4 = (bf16[3,1024,256]{2,1,0:T(8,128)(2,1)}, bf16[3,1024,256]{2,1,0:T(8,128)(2,1)S(1)}, u32[]{:S(2)}, u32[]{:S(2)}) collective-permute-start(bf16[3,1024,256]{2,1,0:T(8,128)(2,1)} %pad_maximum_fusion.4), channel_id=1, source_target_pairs={{0,4},{4,0},{8,12},{12,8},{1,5},{5,1},{9,13},{13,9},{2,6},{6,2},{1... | collective-permute-start | bytes 4718600 | tf_op jit(solution)/shard_map/ppermute | solution.py:69
  24.2 10.3 %collective-permute-start.12 = (bf16[3,1024,256]{2,1,0:T(8,128)(2,1)}, bf16[3,1024,256]{2,1,0:T(8,128)(2,1)}, u32[]{:S(2)}, u32[]{:S(2)}) collective-permute-start(bf16[3,1024,256]{2,1,0:T(8,128)(2,1)} %pad_maximum_fusion.12), channel_id=1, source_target_pairs={{0,4},{4,0},{8,12},{12,8},{1,5},{5,1},{9,13},{13,9},{2,6},{6,2},{1... | collective-permute-start | bytes 4718600 | tf_op jit(solution)/shard_map/ppermute | solution.py:69
  31.1 3.1 copy-start.18
  31.1 3.1 copy-start.19
  31.1 3.1 copy-start.20
  31.2 38.2 %collective-permute-start.6 = (bf16[3,1024,256]{2,1,0:T(8,128)(2,1)S(1)}, bf16[3,1024,256]{2,1,0:T(8,128)(2,1)S(1)}, u32[]{:S(2)}, u32[]{:S(2)}) collective-permute-start(bf16[3,1024,256]{2,1,0:T(8,128)(2,1)S(1)} %pad_maximum_fusion.7), channel_id=1, source_target_pairs={{0,8},{4,12},{8,0},{12,4},{1,9},{5,13},{9,1},{13,5},{2,10},{6,14},... | collective-permute-start | bytes 4718600 | tf_op jit(solution)/shard_map/ppermute | solution.py:69
  34.4 37.4 %collective-permute-start.11 = (bf16[3,1024,256]{2,1,0:T(8,128)(2,1)S(1)}, bf16[3,1024,256]{2,1,0:T(8,128)(2,1)S(1)}, u32[]{:S(2)}, u32[]{:S(2)}) collective-permute-start(bf16[3,1024,256]{2,1,0:T(8,128)(2,1)S(1)} %pad_maximum_fusion.10), channel_id=1, source_target_pairs={{0,4},{4,0},{8,12},{12,8},{1,5},{5,1},{9,13},{13,9},{2,6},{6,2},{1... | collective-permute-start | bytes 4718600 | tf_op jit(solution)/shard_map/ppermute | solution.py:69
  35.8 66.8 %collective-permute-start.13 = (bf16[3,1024,256]{2,1,0:T(8,128)(2,1)S(1)}, bf16[3,1024,256]{2,1,0:T(8,128)(2,1)}, u32[]{:S(2)}, u32[]{:S(2)}) collective-permute-start(bf16[3,1024,256]{2,1,0:T(8,128)(2,1)S(1)} %pad_maximum_fusion.13), channel_id=1, source_target_pairs={{0,8},{4,12},{8,0},{12,4},{1,9},{5,13},{9,1},{13,5},{2,10},{6,14},... | collective-permute-start | bytes 4718600 | tf_op jit(solution)/shard_map/ppermute | solution.py:69
  37.1 34.4 %copy-start.15 = (bf16[1,1024,256]{2,1,0:T(8,128)(2,1)S(1)}, bf16[1,1024,256]{2,1,0:T(8,128)(2,1)}, u32[]{:S(2)}) copy-start(bf16[1,1024,256]{2,1,0:T(8,128)(2,1)} %get-tuple-element.83) | copy-start | bytes 1572868
  37.1 34.4 %copy-start.16 = (bf16[1,1024,256]{2,1,0:T(8,128)(2,1)S(1)}, bf16[1,1024,256]{2,1,0:T(8,128)(2,1)}, u32[]{:S(2)}) copy-start(bf16[1,1024,256]{2,1,0:T(8,128)(2,1)} %get-tuple-element.97) | copy-start | bytes 1572868
  37.1 34.4 %copy-start.17 = (bf16[1,1024,256]{2,1,0:T(8,128)(2,1)S(1)}, bf16[1,1024,256]{2,1,0:T(8,128)(2,1)}, u32[]{:S(2)}) copy-start(bf16[1,1024,256]{2,1,0:T(8,128)(2,1)} %get-tuple-element.109) | copy-start | bytes 1572868
  69.4 2.3 copy-start.2
  69.4 35.3 %collective-permute-start.16 = (bf16[3,1024,256]{2,1,0:T(8,128)(2,1)S(1)}, bf16[3,1024,256]{2,1,0:T(8,128)(2,1)S(1)}, u32[]{:S(2)}, u32[]{:S(2)}) collective-permute-start(bf16[3,1024,256]{2,1,0:T(8,128)(2,1)S(1)} %collective-permute-done.6.far_ref), channel_id=1, source_target_pairs={{0,16},{16,0},{1,17},{17,1},{2,18},{18,2},{3,19},{19,3},{4,20},{20... | collective-permute-start | bytes 4718600 | tf_op jit(solution)/shard_map/ppermute | solution.py:73
  71.7 37.3 %collective-permute-start.3 = (bf16[3,1024,256]{2,1,0:T(8,128)(2,1)S(1)}, bf16[3,1024,256]{2,1,0:T(8,128)(2,1)}, u32[]{:S(2)}, u32[]{:S(2)}) collective-permute-start(bf16[3,1024,256]{2,1,0:T(8,128)(2,1)S(1)} %pad_maximum_fusion.2), channel_id=1, source_target_pairs={{0,4},{4,0},{8,12},{12,8},{1,5},{5,1},{9,13},{13,9},{2,6},{6,2},{1... | collective-permute-start | bytes 4718600 | tf_op jit(solution)/shard_map/ppermute | solution.py:69
  71.8 1.7 copy-start
  71.9 34.3 %copy-start.12 = (bf16[1,1024,256]{2,1,0:T(8,128)(2,1)S(1)}, bf16[1,1024,256]{2,1,0:T(8,128)(2,1)}, u32[]{:S(2)}) copy-start(bf16[1,1024,256]{2,1,0:T(8,128)(2,1)} %get-tuple-element.80) | copy-start | bytes 1572868
  71.9 34.3 %copy-start.13 = (bf16[1,1024,256]{2,1,0:T(8,128)(2,1)S(1)}, bf16[1,1024,256]{2,1,0:T(8,128)(2,1)}, u32[]{:S(2)}) copy-start(bf16[1,1024,256]{2,1,0:T(8,128)(2,1)} %get-tuple-element.94) | copy-start | bytes 1572868
  71.9 34.3 %copy-start.14 = (bf16[1,1024,256]{2,1,0:T(8,128)(2,1)S(1)}, bf16[1,1024,256]{2,1,0:T(8,128)(2,1)}, u32[]{:S(2)}) copy-start(bf16[1,1024,256]{2,1,0:T(8,128)(2,1)} %get-tuple-element.112) | copy-start | bytes 1572868
  102.6 37.6 %collective-permute-start.7 = (bf16[3,1024,256]{2,1,0:T(8,128)(2,1)}, bf16[3,1024,256]{2,1,0:T(8,128)(2,1)}, u32[]{:S(2)}, u32[]{:S(2)}) collective-permute-start(bf16[3,1024,256]{2,1,0:T(8,128)(2,1)} %pad_maximum_fusion.5), channel_id=1, source_target_pairs={{0,8},{4,12},{8,0},{12,4},{1,9},{5,13},{9,1},{13,5},{2,10},{6,14},... | collective-permute-start | bytes 4718600 | tf_op jit(solution)/shard_map/ppermute | solution.py:69
  104.7 2.8 copy-start.4
  104.7 35.6 %collective-permute-start.17 = (bf16[3,1024,256]{2,1,0:T(8,128)(2,1)}, bf16[3,1024,256]{2,1,0:T(8,128)(2,1)}, u32[]{:S(2)}, u32[]{:S(2)}) collective-permute-start(bf16[3,1024,256]{2,1,0:T(8,128)(2,1)} %collective-permute-done.13.far_ref), channel_id=1, source_target_pairs={{0,16},{16,0},{1,17},{17,1},{2,18},{18,2},{3,19},{19,3},{4,20},{20... | collective-permute-start | bytes 4718600 | tf_op jit(solution)/shard_map/ppermute | solution.py:73
  107.6 68.0 %collective-permute-start.10 = (bf16[3,1024,256]{2,1,0:T(8,128)(2,1)}, bf16[3,1024,256]{2,1,0:T(8,128)(2,1)}, u32[]{:S(2)}, u32[]{:S(2)}) collective-permute-start(bf16[3,1024,256]{2,1,0:T(8,128)(2,1)} %pad_maximum_fusion.8), channel_id=1, source_target_pairs={{0,4},{4,0},{8,12},{12,8},{1,5},{5,1},{9,13},{13,9},{2,6},{6,2},{1... | collective-permute-start | bytes 4718600 | tf_op jit(solution)/shard_map/ppermute | solution.py:69
  107.6 68.6 %collective-permute-start.14 = (bf16[3,1024,256]{2,1,0:T(8,128)(2,1)}, bf16[3,1024,256]{2,1,0:T(8,128)(2,1)}, u32[]{:S(2)}, u32[]{:S(2)}) collective-permute-start(bf16[3,1024,256]{2,1,0:T(8,128)(2,1)} %pad_maximum_fusion.11), channel_id=1, source_target_pairs={{0,8},{4,12},{8,0},{12,4},{1,9},{5,13},{9,1},{13,5},{2,10},{6,14},... | collective-permute-start | bytes 4718600 | tf_op jit(solution)/shard_map/ppermute | solution.py:69
  109.0 1.5 copy-start.31
  109.0 1.5 copy-start.32
  109.1 1.5 copy-start.33
  109.1 111.4 %collective-permute-start.1 = (bf16[512,4096]{1,0:T(8,128)(2,1)}, bf16[512,4096]{1,0:T(8,128)(2,1)}, u32[]{:S(2)}, u32[]{:S(2)}) collective-permute-start(bf16[512,4096]{1,0:T(8,128)(2,1)} %all-gather.5.cloned.1.call-done), channel_id=1, source_target_pairs={{0,4},{4,0},{8,12},{12,8},{1,5},{5,1},{9,13},{13,9},{2,6},{6,2},{1... | collective-permute-start | bytes 12582920 | tf_op jit(solution)/shard_map/ppermute | solution.py:69
  140.3 39.8 %collective-permute-start.18 = (bf16[3,1024,256]{2,1,0:T(8,128)(2,1)}, bf16[3,1024,256]{2,1,0:T(8,128)(2,1)}, u32[]{:S(2)}, u32[]{:S(2)}) collective-permute-start(bf16[3,1024,256]{2,1,0:T(8,128)(2,1)} %collective-permute-done.7.far_ref), channel_id=1, source_target_pairs={{0,16},{16,0},{1,17},{17,1},{2,18},{18,2},{3,19},{19,3},{4,20},{20... | collective-permute-start | bytes 4718600 | tf_op jit(solution)/shard_map/ppermute | solution.py:73
  174.2 52.2 %collective-permute-start = (bf16[512,4096]{1,0:T(8,128)(2,1)}, bf16[512,4096]{1,0:T(8,128)(2,1)}, u32[]{:S(2)}, u32[]{:S(2)}) collective-permute-start(bf16[512,4096]{1,0:T(8,128)(2,1)} %all-gather.3.cloned.1.call-done), channel_id=1, source_target_pairs={{0,4},{4,0},{8,12},{12,8},{1,5},{5,1},{9,13},{13,9},{2,6},{6,2},{1... | collective-permute-start | bytes 12582920 | tf_op jit(solution)/shard_map/ppermute | solution.py:69
  175.5 3.2 copy-start.28
  175.5 3.3 copy-start.29
  175.5 3.3 copy-start.30
  175.5 8.8 %collective-permute-start.2 = (bf16[3,1024,256]{2,1,0:T(8,128)(2,1)}, bf16[3,1024,256]{2,1,0:T(8,128)(2,1)}, u32[]{:S(2)}, u32[]{:S(2)}) collective-permute-start(bf16[3,1024,256]{2,1,0:T(8,128)(2,1)} %pad_maximum_fusion), channel_id=1, source_target_pairs={{0,4},{4,0},{8,12},{12,8},{1,5},{5,1},{9,13},{13,9},{2,6},{6,2},{1... | collective-permute-start | bytes 4718600 | tf_op jit(solution)/shard_map/ppermute | solution.py:69
  176.1 37.6 %collective-permute-start.8 = (bf16[3,1024,256]{2,1,0:T(8,128)(2,1)}, bf16[3,1024,256]{2,1,0:T(8,128)(2,1)}, u32[]{:S(2)}, u32[]{:S(2)}) collective-permute-start(bf16[3,1024,256]{2,1,0:T(8,128)(2,1)} %pad_maximum_fusion.3), channel_id=1, source_target_pairs={{0,8},{4,12},{8,0},{12,4},{1,9},{5,13},{9,1},{13,5},{2,10},{6,14},... | collective-permute-start | bytes 4718600 | tf_op jit(solution)/shard_map/ppermute | solution.py:69
  178.8 2.7 copy-start.25
  180.1 36.4 %collective-permute-start.19 = (bf16[3,1024,256]{2,1,0:T(8,128)(2,1)}, bf16[3,1024,256]{2,1,0:T(8,128)(2,1)}, u32[]{:S(2)}, u32[]{:S(2)}) collective-permute-start(bf16[3,1024,256]{2,1,0:T(8,128)(2,1)} %collective-permute-done.14.far_ref), channel_id=1, source_target_pairs={{0,16},{16,0},{1,17},{17,1},{2,18},{18,2},{3,19},{19,3},{4,20},{20... | collective-permute-start | bytes 4718600 | tf_op jit(solution)/shard_map/ppermute | solution.py:73
  184.2 1.5 copy-start.26
  184.2 1.5 copy-start.27
  184.3 30.8 %copy-start.11 = (bf16[512,4096]{1,0:T(8,128)(2,1)S(1)}, bf16[512,4096]{1,0:T(8,128)(2,1)}, u32[]{:S(2)}) copy-start(bf16[512,4096]{1,0:T(8,128)(2,1)} %all-gather.5.cloned.1.call-done) | copy-start | bytes 12582916
  187.0 71.8 %collective-permute-start.15 = (bf16[3,1024,256]{2,1,0:T(8,128)(2,1)}, bf16[3,1024,256]{2,1,0:T(8,128)(2,1)}, u32[]{:S(2)}, u32[]{:S(2)}) collective-permute-start(bf16[3,1024,256]{2,1,0:T(8,128)(2,1)} %pad_maximum_fusion.9), channel_id=1, source_target_pairs={{0,8},{4,12},{8,0},{12,4},{1,9},{5,13},{9,1},{13,5},{2,10},{6,14},... | collective-permute-start | bytes 4718600 | tf_op jit(solution)/shard_map/ppermute | solution.py:69
  213.7 87.0 %collective-permute-start.9 = (bf16[3,1024,256]{2,1,0:T(8,128)(2,1)}, bf16[3,1024,256]{2,1,0:T(8,128)(2,1)}, u32[]{:S(2)}, u32[]{:S(2)}) collective-permute-start(bf16[3,1024,256]{2,1,0:T(8,128)(2,1)} %pad_maximum_fusion.1), channel_id=1, source_target_pairs={{0,8},{4,12},{8,0},{12,4},{1,9},{5,13},{9,1},{13,5},{2,10},{6,14},... | collective-permute-start | bytes 4718600 | tf_op jit(solution)/shard_map/ppermute | solution.py:69
  216.5 42.3 %collective-permute-start.20 = (bf16[3,1024,256]{2,1,0:T(8,128)(2,1)}, bf16[3,1024,256]{2,1,0:T(8,128)(2,1)S(1)}, u32[]{:S(2)}, u32[]{:S(2)}) collective-permute-start(bf16[3,1024,256]{2,1,0:T(8,128)(2,1)} %collective-permute-done.8.far_ref), channel_id=1, source_target_pairs={{0,16},{16,0},{1,17},{17,1},{2,18},{18,2},{3,19},{19,3},{4,20},{20... | collective-permute-start | bytes 4718600 | tf_op jit(solution)/shard_map/ppermute | solution.py:73
  223.1 3.3 copy-start.8
  226.4 6.0 %copy-start.3 = (bf16[3,1024,256]{2,1,0:T(8,128)(2,1)S(1)}, bf16[3,1024,256]{2,1,0:T(8,128)(2,1)}, u32[]{:S(2)}) copy-start(bf16[3,1024,256]{2,1,0:T(8,128)(2,1)} %copy-done.2) | copy-start | bytes 4718596
  226.4 6.0 %copy-start.5 = (bf16[3,1024,256]{2,1,0:T(8,128)(2,1)S(1)}, bf16[3,1024,256]{2,1,0:T(8,128)(2,1)}, u32[]{:S(2)}) copy-start(bf16[3,1024,256]{2,1,0:T(8,128)(2,1)} %copy-done.4) | copy-start | bytes 4718596
  229.0 3.3 copy-start.9
  258.8 1.2 copy-start.6
  260.0 40.7 %collective-permute-start.21 = (bf16[3,1024,256]{2,1,0:T(8,128)(2,1)}, bf16[3,1024,256]{2,1,0:T(8,128)(2,1)}, u32[]{:S(2)}, u32[]{:S(2)}) collective-permute-start(bf16[3,1024,256]{2,1,0:T(8,128)(2,1)} %collective-permute-done.15.far_ref), channel_id=1, source_target_pairs={{0,16},{16,0},{1,17},{17,1},{2,18},{18,2},{3,19},{19,3},{4,20},{20... | collective-permute-start | bytes 4718600 | tf_op jit(solution)/shard_map/ppermute | solution.py:73
  260.9 13.2 %copy-start.1 = (bf16[3,1024,256]{2,1,0:T(8,128)(2,1)S(1)}, bf16[3,1024,256]{2,1,0:T(8,128)(2,1)}, u32[]{:S(2)}) copy-start(bf16[3,1024,256]{2,1,0:T(8,128)(2,1)} %copy-done) | copy-start | bytes 4718596
  274.1 13.2 %copy-start.7 = (bf16[3,1024,256]{2,1,0:T(8,128)(2,1)S(1)}, bf16[3,1024,256]{2,1,0:T(8,128)(2,1)}, u32[]{:S(2)}) copy-start(bf16[3,1024,256]{2,1,0:T(8,128)(2,1)} %copy-done.6) | copy-start | bytes 4718596
  287.3 15.1 %copy-start.24 = (bf16[3,4096,64]{1,2,0:T(8,128)(2,1)S(1)}, bf16[3,4096,64]{1,2,0:T(8,128)(2,1)}, u32[]{:S(2)}) copy-start(bf16[3,4096,64]{1,2,0:T(8,128)(2,1)} %param.15) | copy-start | bytes 4718596
  300.7 35.2 %collective-permute-start.22 = (bf16[3,1024,256]{2,1,0:T(8,128)(2,1)}, bf16[3,1024,256]{2,1,0:T(8,128)(2,1)S(1)}, u32[]{:S(2)}, u32[]{:S(2)}) collective-permute-start(bf16[3,1024,256]{2,1,0:T(8,128)(2,1)} %collective-permute-done.9.far_ref), channel_id=1, source_target_pairs={{0,16},{16,0},{1,17},{17,1},{2,18},{18,2},{3,19},{19,3},{4,20},{20... | collective-permute-start | bytes 4718600 | tf_op jit(solution)/shard_map/ppermute | solution.py:73
  350.2 1.3 copy-start.34
  351.5 9.1 %collective-permute-start.23 = (f32[2,12288]{1,0:T(2,128)S(1)}, f32[2,12288]{1,0:T(2,128)S(1)}, u32[]{:S(2)}, u32[]{:S(2)}) collective-permute-start(f32[2,12288]{1,0:T(2,128)S(1)} %slice.35), channel_id=1, source_target_pairs={{0,4},{4,0},{8,12},{12,8},{1,5},{5,1},{9,13},{13,9},{2,6},{6,2},{1... | collective-permute-start | bytes 294920 | tf_op jit(solution)/shard_map/ppermute | solution.py:69
Sparse Core Ops, SparseCore 0:
  9.8 83.4 all-gather.4
  94.9 79.2 all-gather.2

commit v2 on v1

v2 whole, which is shorter than its diff:
```python
import jax
import jax.numpy as jnp
from jax import lax
from jax.experimental import pallas as pl
from jax.experimental.pallas import tpu as pltpu
from jax.sharding import Mesh, PartitionSpec as P

HIGHEST = lax.Precision.HIGHEST


def dot(left, right):
    return jnp.dot(left, right, preferred_element_type=jnp.float32)


def activations(gate_pre, up_pre, back_grad):
    sigmoid_gate = jax.nn.sigmoid(gate_pre)
    silu_gate = gate_pre * sigmoid_gate
    hidden = (silu_gate * up_pre).astype(jnp.bfloat16)
    grad_gate = (
        back_grad * up_pre * sigmoid_gate * (1.0 + gate_pre * (1.0 - sigmoid_gate))
    ).astype(jnp.bfloat16)
    grad_up = (back_grad * silu_gate).astype(jnp.bfloat16)
    return hidden, grad_gate, grad_up


def outer_sum(left, right, length):
    rank = left.shape[1]
    left_seq = left.reshape(-1, length, rank)
    right_seq = right.reshape(-1, length, rank)
    return jnp.einsum("slr,slk->srk", left_seq, right_seq, precision=HIGHEST)


def mask_tokens(out_grad, lengths):
    length = out_grad.shape[0] // lengths.shape[0]
    positions = jnp.arange(length, dtype=jnp.int32)
    keep = positions[None, :] < lengths[:, None]
    return out_grad * keep.astype(out_grad.dtype).reshape(-1, 1)


def gathered_body(acts, out_grad, lengths, w_gate, w_up, w_down_t, d_proj, ff_proj, queries):
    seq_dev = lengths.shape[0]
    length = acts.shape[0] // seq_dev
    rank = d_proj.shape[2]
    full_acts = lax.all_gather(acts, "tensor", axis=1, tiled=True)
    masked_grad = lax.all_gather(mask_tokens(out_grad, lengths), "tensor", axis=1, tiled=True)
    gate_pre = dot(full_acts, lax.all_gather(w_gate, "dp", axis=0, tiled=True))
    up_pre = dot(full_acts, lax.all_gather(w_up, "dp", axis=0, tiled=True))
    back_grad = dot(masked_grad, lax.all_gather(w_down_t, "dp", axis=0, tiled=True))
    hidden, grad_gate, grad_up = activations(gate_pre, up_pre, back_grad)
    proj = jnp.stack(
        [
            outer_sum(dot(full_acts, d_proj[0]), dot(grad_gate, ff_proj[0]), length),
            outer_sum(dot(full_acts, d_proj[1]), dot(grad_up, ff_proj[1]), length),
            outer_sum(dot(hidden, ff_proj[2]), dot(masked_grad, d_proj[2]), length),
        ],
        axis=1,
    )
    proj_b = lax.psum(proj.reshape(seq_dev, 3 * rank * rank), "tensor").astype(jnp.bfloat16)
    flat_scores = lax.dot_general(
        proj_b,
        lax.all_gather(queries, "dp", axis=0, tiled=True),
        (((1,), (1,)), ((), ())),
        preferred_element_type=jnp.float32,
    )
    return flat_scores.reshape(seq_dev, lax.axis_size("dp"), queries.shape[0])


DP = ("far", "near")


def permute_dp(value, flip):
    return lax.ppermute(value, DP, [(i, i ^ flip) for i in range(4)])


def permute_tensor(value, flip):
    return lax.ppermute(value, "tensor", [(i, i ^ flip) for i in range(lax.axis_size("tensor"))])


def permute_parts(value):
    return lax.ppermute(value, "parts", [(0, 1), (1, 0)])


def pre_activation(places, tokens_ref, own, pieces):
    depth = own.shape[0]
    rows = depth // 2

    def columns(k, size):
        at = pl.multiple_of(lax.rem(places[k], depth), rows)
        return tokens_ref[places[k] // depth, :, pl.ds(at, size)]

    total = dot(tokens_ref[places[1] // depth], own[...])
    for k, (ref, plane) in enumerate(pieces):
        total += dot(columns(2 + k, rows), ref[plane])
    return total


def add_projected(sums_in, sums_ref, values, ff_ref):
    rank = ff_ref.shape[1]
    for m, value in enumerate(values):
        at = slice(m * rank, (m + 1) * rank)
        if value is None:
            sums_ref[:, at] = sums_in[:, at]
        else:
            product = lax.dot_general(value, ff_ref[m], (((1,), (1,)), ((), ())), preferred_element_type=jnp.float32)
            sums_ref[:, at] = sums_in[:, at] + product


def direct_kernel(tokens_ref, d_ref, out):
    depth = tokens_ref.shape[2]
    out[...] = sum(dot(tokens_ref[q], d_ref[q * depth : (q + 1) * depth]) for q in range(tokens_ref.shape[0]))


def token_tiles(tokens, near_count, tile):
    per_near = tokens.shape[1] // tile
    shape = (tokens.shape[0] // near_count, tile, tokens.shape[2])
    return pl.BlockSpec(shape, lambda i, *_: (i // per_near, i % per_near, 0)), near_count * per_near


def direct(tokens, d):
    tile = 256
    spec, tiles = token_tiles(tokens, 2, tile)
    return pl.pallas_call(
        direct_kernel,
        out_shape=jax.ShapeDtypeStruct((tiles * tile, d.shape[1]), jnp.float32),
        grid=(tiles,),
        in_specs=[spec, pl.BlockSpec(d.shape, lambda i: (0, 0))],
        out_specs=pl.BlockSpec((tile, d.shape[1]), lambda i: (i, 0)),
        compiler_params=pltpu.CompilerParams(vmem_limit_bytes=48 * 2**20),
        cost_estimate=pl.CostEstimate(flops=1000, bytes_accessed=1000, transcendentals=0),
    )(tokens, d)


def planes(pieces, m):
    return [(ref, m) for ref in pieces]


def both_kernel(places, acts_ref, grad_ref, w_gate, w_up, w_down, *refs):
    *pieces, ff_ref, sums_in, sums_ref = refs
    gate_pre = pre_activation(places, acts_ref, w_gate, planes(pieces, 0))
    up_pre = pre_activation(places, acts_ref, w_up, planes(pieces, 1))
    back_grad = pre_activation(places, grad_ref, w_down, planes(pieces, 2))
    hidden, grad_gate, grad_up = activations(gate_pre, up_pre, back_grad)
    add_projected(sums_in, sums_ref, (grad_gate, grad_up, hidden), ff_ref)


def forward_kernel(places, acts_ref, w_gate, w_up, *refs):
    *pieces, ff_ref, sums_in, sums_ref, gate_factor, up_factor = refs
    gate_pre = pre_activation(places, acts_ref, w_gate, planes(pieces, 0))
    up_pre = pre_activation(places, acts_ref, w_up, planes(pieces, 1))
    sigmoid_gate = jax.nn.sigmoid(gate_pre)
    silu_gate = gate_pre * sigmoid_gate
    gate_factor[...] = up_pre * sigmoid_gate * (1.0 + gate_pre * (1.0 - sigmoid_gate))
    up_factor[...] = silu_gate
    add_projected(sums_in, sums_ref, (None, None, (silu_gate * up_pre).astype(jnp.bfloat16)), ff_ref)


def backward_kernel(places, grad_ref, w_down, *refs):
    *pieces, gate_factor, up_factor, ff_ref, sums_in, sums_ref = refs
    back_grad = pre_activation(places, grad_ref, w_down, planes(pieces, 0))
    grad_gate = (back_grad * gate_factor[...]).astype(jnp.bfloat16)
    grad_up = (back_grad * up_factor[...]).astype(jnp.bfloat16)
    add_projected(sums_in, sums_ref, (grad_gate, grad_up, None), ff_ref)


def add_hidden_units(kernel, places, tokens, weights, pieces, factors, ff_proj, sums):
    tile = 256
    token_spec, tiles = token_tiles(tokens[0], 2, tile)
    rows = tiles * tile
    depth = weights[0].shape[0]
    chunk = pieces[0][0].shape[2]
    by_tile = lambda i, places: (i, 0)
    own = pl.BlockSpec((depth, chunk), lambda i, places: (0, places[0]))
    piece = lambda v, count, block: pl.BlockSpec((count, *v.shape[1:]), lambda i, places: (block, 0, 0))
    factor = pl.BlockSpec((tile, chunk), by_tile)
    total = pl.BlockSpec((tile, sums.shape[1]), by_tile)
    out_shape, out_specs = [jax.ShapeDtypeStruct(sums.shape, sums.dtype)], [total]
    if kernel is forward_kernel:
        out_shape += [jax.ShapeDtypeStruct((rows, chunk), jnp.float32)] * 2
        out_specs += [factor] * 2
    operands = [*tokens, *weights, *(v for v, _, _ in pieces), *factors, ff_proj, sums]
    return pl.pallas_call(
        kernel,
        out_shape=out_shape,
        grid_spec=pltpu.PrefetchScalarGridSpec(
            num_scalar_prefetch=1,
            grid=(tiles,),
            in_specs=[token_spec] * len(tokens)
            + [own] * len(weights)
            + [piece(*p) for p in pieces]
            + [factor] * len(factors)
            + [pl.BlockSpec((3, ff_proj.shape[1], chunk), lambda i, places: (0, 0, places[0])), total],
            out_specs=out_specs,
        ),
        input_output_aliases={len(operands): 0},
        compiler_params=pltpu.CompilerParams(vmem_limit_bytes=48 * 2**20),
        cost_estimate=pl.CostEstimate(flops=1000, bytes_accessed=1000, transcendentals=0),
    )(places, *operands)


def cut_kernel(at, *refs):
    *sources, mine, kept, left = refs
    for m in range(3):
        mine[m] = sources[m][...]
        kept[m] = sources[3 + m][...]
        left[m] = sources[6 + m][...]


def cut(weights, side, mine_at, other_at, rows, chunk):
    tile = 256
    at = jnp.stack([jnp.asarray(v, jnp.int32) for v in (side * rows // tile, (1 - side) * rows // tile, mine_at, other_at)])
    block = lambda r, c: pl.BlockSpec((tile, chunk), lambda i, at: (at[r] + i, at[c]))
    out = pl.BlockSpec((3, tile, chunk), lambda i, at: (0, i, 0))
    return pl.pallas_call(
        cut_kernel,
        out_shape=[jax.ShapeDtypeStruct((3, rows, chunk), weights[0].dtype)] * 3,
        grid_spec=pltpu.PrefetchScalarGridSpec(
            num_scalar_prefetch=1,
            grid=(rows // tile,),
            in_specs=[block(0, 2)] * 3 + [block(0, 3)] * 3 + [block(1, 3)] * 3,
            out_specs=[out] * 3,
        ),
        cost_estimate=pl.CostEstimate(flops=1000, bytes_accessed=1000, transcendentals=0),
    )(at, *weights, *weights, *weights)


def token_kernel(value, out):
    out[...] = value[...]


def token(value):
    block = pl.BlockSpec((8, 128), lambda i: (0, 0))
    return pl.pallas_call(
        token_kernel,
        out_shape=jax.ShapeDtypeStruct((8, 128), value.dtype),
        grid=(1,),
        in_specs=[block],
        out_specs=block,
        cost_estimate=pl.CostEstimate(flops=600000000, bytes_accessed=1000, transcendentals=0),
    )(value)


def after(value, *others):
    return lax.optimization_barrier((value, *others))[0]


def relayed_body(acts, out_grad, lengths, w_gate, w_up, w_down_t, d_proj, ff_proj, queries):
    seq_dev = lengths.shape[0]
    tokens = acts.shape[0]
    length = tokens // seq_dev
    rank = d_proj.shape[2]
    depth = w_gate.shape[0]
    me = lax.axis_index(DP)
    near = lax.axis_index("near")
    part = lax.axis_index("parts")
    half = w_gate.shape[1] // 2
    chunk = 256
    chunks = half // chunk
    rows = depth // 2
    weights = (w_gate, w_up, w_down_t)
    blocks = 2 * chunks
    last = blocks - 1
    ticks, joined = [], {}

    def at(stage, value):
        return after(value, ticks[stage]) if stage >= 0 else value

    def join(stage, *values):
        joined.setdefault(min(stage, last), []).extend(values)

    def end(stage, value):
        ticks.append(after(token(value), *joined[stage]))

    pair = jnp.stack([queries, permute_dp(queries, 2)])
    join(0, pair)
    gathered_acts = lax.all_gather(acts, ("near", "tensor"))
    gathered_grad = lax.all_gather(mask_tokens(out_grad, lengths), ("near", "tensor"))
    sums = jnp.zeros((2 * tokens, 3 * rank), jnp.float32)
    ff_columns = jnp.swapaxes(ff_proj, 1, 2)
    far, relayed, near_rows, cuts = [], [], [], []
    factors = [None] * chunks

    def add(kernel, j, sums):
        starts = [near * chunks + j, me * depth]
        starts += [(me ^ 1) * depth + side * rows for side in (part, 1 - part)]
        starts += [(me ^ flip) * depth + side * rows for side in (part, 1 - part) for flip in (2, 3)]
        places = jnp.stack([jnp.asarray(s, jnp.int32) for s in starts])
        sources = near_rows[j] + far[2 * j : 2 * j + 2] + relayed[2 * j : 2 * j + 2]
        run = lambda *args: add_hidden_units(kernel, places, *args, ff_columns, sums)
        if kernel is forward_kernel:
            sums, *factors[j] = run([full_acts], weights[:2], [(v, 2, 0) for v in sources], [])
        elif kernel is backward_kernel:
            (sums,) = run([full_grad], weights[2:], [(v, 1, 2) for v in sources], factors[j])
        else:
            (sums,) = run([full_acts, full_grad], weights, [(v, 3, 0) for v in sources], [])
        return sums

    def send(g):
        j = g // 2
        if g % 2 == 0:
            sources = [at(g - 3, w) for w in weights]
            cuts.append(cut(sources, part, near * chunks + j, (1 - near) * chunks + j, rows, chunk))
        far.append(permute_dp(at(g - 2, cuts[j][g % 2]), 2 + g % 2))
        join(g, far[g])

    work = {
        6: [(forward_kernel, 0)],
        7: [(forward_kernel, 1)],
        8: [(forward_kernel, 2)],
        9: [(backward_kernel, 0)],
        10: [(forward_kernel, 3)],
        11: [(backward_kernel, 1), (backward_kernel, 2)],
        12: [(forward_kernel, 4)],
        13: [(backward_kernel, 3), (backward_kernel, 4)],
    }
    rest = [(both_kernel, 5), (both_kernel, 6)]
    send(0)
    send(1)
    for g in range(blocks):
        if g in work:
            sums = after(sums, token(ticks[g - 1]))
            for kernel, j in work[g]:
                sums = add(kernel, j, sums)
            end(g, sums)
        else:
            end(g, ticks[-1] if ticks else jnp.zeros((8, 128), jnp.float32))
        relayed.append(permute_parts(at(g, far[g])))
        join(g + 2, relayed[g])
        if g + 2 < blocks:
            send(g + 2)
        if g % 2 == 1:
            near_rows.append([permute_dp(at(g, v), 1) for v in cuts[g // 2][1:]])
            join(g + 2, *near_rows[-1])
        if g == 1:
            near_pair = permute_dp(at(1, pair), 1)
            join(3, near_pair)
        if g == 5:
            full_acts = at(5, gathered_acts)
        if g == 8:
            full_grad = at(8, gathered_grad)
    sums = at(last, sums)
    left_both = direct(at(last, full_acts), jnp.concatenate([d_proj[0], d_proj[1]], axis=1))
    right_down = direct(at(last, full_grad), d_proj[2])
    for kernel, j in rest:
        sums = add(kernel, j, sums)
    right_gate, right_up, left_down = jnp.split(sums, 3, axis=1)
    left_gate, left_up = jnp.split(left_both, 2, axis=1)
    proj = jnp.stack(
        [
            outer_sum(left_gate, right_gate, length),
            outer_sum(left_up, right_up, length),
            outer_sum(left_down, right_down, length),
        ],
        axis=1,
    ).reshape(2, seq_dev, 3 * rank * rank)
    near_proj = permute_dp(lax.dynamic_index_in_dim(proj, 1 - near, 0, False), 1)
    proj = lax.dynamic_index_in_dim(proj, near, 0, False) + near_proj
    sent = proj.astype(jnp.bfloat16)
    for flip in range(1, lax.axis_size("tensor")):
        proj += permute_tensor(sent, flip).astype(jnp.float32)
    flat_scores = lax.dot_general(
        proj.astype(jnp.bfloat16),
        jnp.stack([pair, near_pair]).reshape(4 * queries.shape[0], -1),
        (((1,), (1,)), ((), ())),
        preferred_element_type=jnp.float32,
    )
    blocks = flat_scores.reshape(seq_dev, 4, queries.shape[0])
    order = jnp.stack([me ^ flip for flip in (0, 2, 1, 3)])
    place = (jnp.arange(4)[:, None] == order[None, :]).astype(jnp.float32)
    return jnp.einsum("ak,skc->sac", place, blocks, precision=HIGHEST)


def solution(mesh):
    sizes = mesh.shape
    relayed = sizes["dp"] == 4 and sizes["parts"] == 2 and sizes["tensor"] == 4
    dp = DP if relayed else ("dp",)
    if relayed:
        mesh = Mesh(mesh.devices.reshape(2, 2, 2, 4), ("parts", *DP, "tensor"))
    in_specs = (
        P(("parts", *dp), "tensor"),
        P(("parts", *dp), "tensor"),
        P(("parts", *dp)),
        P(dp, "tensor"),
        P(dp, "tensor"),
        P(dp, "tensor"),
        P(),
        P(None, "tensor", None),
        P((*dp, "tensor"), None),
    )
    out_specs = P(("parts", *dp), None, "tensor")
    body = relayed_body if relayed else gathered_body
    return jax.shard_map(body, mesh=mesh, in_specs=in_specs, out_specs=out_specs, check_vma=False)
```

time: 387 us -> 344 us (0.89)
  Pallas kernels: 92.9 us -> 154 us
  waiting for transfers between devices: 154 us -> 95.3 us
  blocking collectives: 26.6 us -> 0 us
  local copies, waits for them, and re-layouts: 43.2 us -> 20.8 us
  starting transfers between devices: 23.8 us -> 44.2 us
  matrix products: 14.6 us -> 5.66 us
  other arithmetic: 17 us -> 8.51 us
    pallas_call x7 -> x21, Pallas kernels: 92.9 us -> 154 us  [the longest x12 117 us: add_hidden_units(): pl.pallas_call(kernel, out_shape=out_shape, grid_spec=pltpu.PrefetchScala...]
    all_gather x2, waiting for transfers between devices: 32.2 us -> 0.01 us  [the longest x1 0.01 us: relayed_body(): gathered_acts = lax.all_gather(acts, ('near', 'tensor'))]
    ppermute x17 -> x34, waiting for transfers between devices: 114 us -> 91.3 us  [the longest x31 88.1 us: permute_dp(): return lax.ppermute(value, DP, [(i, i ^ flip) for i in range(4)])]
    psum x1 -> x0, blocking collectives: 17.7 us -> none  [relayed_body(): proj_b = lax.psum(proj, 'tensor').astype(jnp.bfloat16)]
    another operation x4 -> x1, local copies, waits for them, and re-layouts: 13.5 us -> 0.03 us  [relayed_body(): jnp.stack([outer_sum(left_gate, right_gate, length), outer_sum(left_up, r...]
    ppermute x17 -> x34, starting transfers between devices: 13.2 us -> 24.5 us  [the longest x31 20 us: permute_dp(): return lax.ppermute(value, DP, [(i, i ^ flip) for i in range(4)])]
    dot_general x3 -> x2, matrix products: 12.7 us -> 2.57 us  [the longest x1 1.83 us: relayed_body(): lax.dot_general(proj.astype(jnp.bfloat16), jnp.stack([pair, near_pair]).r...]
    ppermute x7 -> x14, starting transfers between devices: 10.6 us -> 19.7 us  [permute_parts(): return lax.ppermute(value, 'parts', [(0, 1), (1, 0)])]
  transfers between devices with their start and end apart: 26 -> 50, of which waited for: 8 -> 14; matrix products, arithmetic and copies ran while one was open for 15% -> 5% of each run, Pallas kernels for 21% -> 41%
where the time goes in v2:
time: 344 us; the launch traced here: 342 us
  Pallas kernels  154 us (45%)
  waiting for transfers between devices  95.3 us (28%)
  starting transfers between devices  44.2 us (13%)
  local copies, waits for them, and re-layouts  20.8 us (6%)
  between operations  13.9 us (4%)
  other arithmetic  8.51 us (2%)
  matrix products  5.66 us (2%)
    pallas_call x12, Pallas kernels, add_hidden_units(): pl.pallas_call(kernel, out_shape=out_shape, grid_spec=pltpu.PrefetchScala...  117 us
    ppermute x31, waiting for transfers between devices, permute_dp(): return lax.ppermute(value, DP, [(i, i ^ flip) for i in range(4)])  88.1 us
    pallas_call x7, Pallas kernels, cut(): pl.pallas_call(cut_kernel, out_shape=[jax.ShapeDtypeStruct((3, rows, chun...  26 us
    ppermute x31, starting transfers between devices, permute_dp(): return lax.ppermute(value, DP, [(i, i ^ flip) for i in range(4)])  20 us
    ppermute x14, starting transfers between devices, permute_parts(): return lax.ppermute(value, 'parts', [(0, 1), (1, 0)])  19.7 us
    unnamed x50, local copies, waits for them, and re-layouts  18.3 us
    pallas_call x2, Pallas kernels, direct(): pl.pallas_call(direct_kernel, out_shape=jax.ShapeDtypeStruct((tiles * til...  11.1 us
  transfers between devices with their start and end apart: 50, of which 14 were waited for; matrix products, arithmetic and copies ran while one was open for 5% of the time, Pallas kernels for 41%

profile of v2, /device:TPU:0, one launch (start us, length us, event | category | flops | bytes accessed | tf_op | source)
XLA Modules:
  0.0 342.5 jit_solution(4260071637148817913)
XLA Ops:
  8.0 2.3 broadcast_multiply_fusion
  10.4 3.0 collective-permute-start
  14.7 3.6 %shard_map.91 = (bf16[3,512,256]{2,1,0:T(8,128)(2,1)}, bf16[3,512,256]{2,1,0:T(8,128)(2,1)}, bf16[3,512,256]{2,1,0:T(8,128)(2,1)}) custom-call(s32[4]{0:T(128)} %get-tuple-element.240.at, bf16[1024,3584]{1,0:T(8,128)(2,1)} %w_gate.13, bf16[1024,3584]{1,0:T(8,128)(2,1)} %w_up.13, bf16[1024,3584]{1,0:T(8,128)(2,1)} %w_down.13, bf16[1024,3584]{1,0:T(8,128)(2,1)} %w_gate.13, ...), custom_call_target="tpu_custom_call" | custom-call | flops 1000 | bytes 1000 | tf_op jit(solution)/shard_map/pallas_call | solution.py:213
  19.2 4.1 %shard_map.92 = (bf16[3,512,256]{2,1,0:T(8,128)(2,1)}, bf16[3,512,256]{2,1,0:T(8,128)(2,1)}, bf16[3,512,256]{2,1,0:T(8,128)(2,1)}) custom-call(s32[4]{0:T(128)} %get-tuple-element.239.at, bf16[1024,3584]{1,0:T(8,128)(2,1)} %w_gate.13, bf16[1024,3584]{1,0:T(8,128)(2,1)} %w_up.13, bf16[1024,3584]{1,0:T(8,128)(2,1)} %w_down.13, bf16[1024,3584]{1,0:T(8,128)(2,1)} %w_gate.13, ...), custom_call_target="tpu_custom_call" | custom-call | flops 1000 | bytes 1000 | tf_op jit(solution)/shard_map/pallas_call | solution.py:213
  24.1 14.8 %collective-permute-done.1.refs_2_ = bf16[3,512,256]{2,1,0:T(8,128)(2,1)S(1)} collective-permute-done((bf16[3,512,256]{2,1,0:T(8,128)(2,1)}, bf16[3,512,256]{2,1,0:T(8,128)(2,1)S(1)}, u32[]{:S(2)}, u32[]{:S(2)}) %collective-permute-start.1) | collective-permute-done | bytes 786464 | tf_op jit(solution)/shard_map/ppermute | solution.py:72
  39.0 1.5 collective-permute-start.3
  41.0 12.4 %collective-permute-done.2.refs_3_ = bf16[3,512,256]{2,1,0:T(8,128)(2,1)S(1)} collective-permute-done((bf16[3,512,256]{2,1,0:T(8,128)(2,1)}, bf16[3,512,256]{2,1,0:T(8,128)(2,1)S(1)}, u32[]{:S(2)}, u32[]{:S(2)}) %collective-permute-start.2) | collective-permute-done | bytes 786464 | tf_op jit(solution)/shard_map/ppermute | solution.py:72
  53.5 2.0 collective-permute-start.5
  55.5 1.8 collective-permute-start.9
  58.8 13.8 %collective-permute-done.4.refs_2_ = bf16[3,512,256]{2,1,0:T(8,128)(2,1)S(1)} collective-permute-done((bf16[3,512,256]{2,1,0:T(8,128)(2,1)}, bf16[3,512,256]{2,1,0:T(8,128)(2,1)S(1)}, u32[]{:S(2)}, u32[]{:S(2)}) %collective-permute-start.4) | collective-permute-done | bytes 786464 | tf_op jit(solution)/shard_map/ppermute | solution.py:72
  72.7 1.5 collective-permute-start.10
  74.2 3.6 %shard_map.93 = (bf16[3,512,256]{2,1,0:T(8,128)(2,1)}, bf16[3,512,256]{2,1,0:T(8,128)(2,1)}, bf16[3,512,256]{2,1,0:T(8,128)(2,1)}) custom-call(s32[4]{0:T(128)} %get-tuple-element.238.at, bf16[1024,3584]{1,0:T(8,128)(2,1)} %w_gate.13, bf16[1024,3584]{1,0:T(8,128)(2,1)} %w_up.13, bf16[1024,3584]{1,0:T(8,128)(2,1)} %w_down.13, bf16[1024,3584]{1,0:T(8,128)(2,1)} %w_gate.13, ...), custom_call_target="tpu_custom_call" | custom-call | flops 1000 | bytes 1000 | tf_op jit(solution)/shard_map/pallas_call | solution.py:213
  78.4 8.7 %collective-permute-done.6.refs_3_ = bf16[3,512,256]{2,1,0:T(8,128)(2,1)S(1)} collective-permute-done((bf16[3,512,256]{2,1,0:T(8,128)(2,1)}, bf16[3,512,256]{2,1,0:T(8,128)(2,1)S(1)}, u32[]{:S(2)}, u32[]{:S(2)}) %collective-permute-start.6) | collective-permute-done | bytes 786464 | tf_op jit(solution)/shard_map/ppermute | solution.py:72
  87.2 2.0 collective-permute-start.12
  89.2 1.9 collective-permute-start.13
  91.1 1.8 collective-permute-done.10.refs_4_
  93.0 13.4 %collective-permute-done.11.refs_2_ = bf16[3,512,256]{2,1,0:T(8,128)(2,1)S(1)} collective-permute-done((bf16[3,512,256]{2,1,0:T(8,128)(2,1)}, bf16[3,512,256]{2,1,0:T(8,128)(2,1)S(1)}, u32[]{:S(2)}, u32[]{:S(2)}) %collective-permute-start.11) | collective-permute-done | bytes 786464 | tf_op jit(solution)/shard_map/ppermute | solution.py:72
  106.4 1.5 collective-permute-start.18
  107.9 3.7 %shard_map.97 = (bf16[3,512,256]{2,1,0:T(8,128)(2,1)}, bf16[3,512,256]{2,1,0:T(8,128)(2,1)}, bf16[3,512,256]{2,1,0:T(8,128)(2,1)}) custom-call(s32[4]{0:T(128)} %get-tuple-element.237.at, bf16[1024,3584]{1,0:T(8,128)(2,1)} %w_gate.13, bf16[1024,3584]{1,0:T(8,128)(2,1)} %w_up.13, bf16[1024,3584]{1,0:T(8,128)(2,1)} %w_down.13, bf16[1024,3584]{1,0:T(8,128)(2,1)} %w_gate.13, ...), custom_call_target="tpu_custom_call" | custom-call | flops 1000 | bytes 1000 | tf_op jit(solution)/shard_map/pallas_call | solution.py:213
  113.0 7.9 %collective-permute-done.13.refs_3_ = bf16[3,512,256]{2,1,0:T(8,128)(2,1)} collective-permute-done((bf16[3,512,256]{2,1,0:T(8,128)(2,1)}, bf16[3,512,256]{2,1,0:T(8,128)(2,1)}, u32[]{:S(2)}, u32[]{:S(2)}) %collective-permute-start.13) | collective-permute-done | bytes 786464 | tf_op jit(solution)/shard_map/ppermute | solution.py:72
  120.9 2.6 collective-permute-start.16
  123.5 1.5 collective-permute-start.19
  125.1 1.4 collective-permute-done.18.refs_4_
  126.6 1.1 copy-done.1
  128.9 1.1 copy-done.10
  130.0 9.9 %shard_map.94 = (f32[1024,192]{1,0:T(8,128)S(1)}, f32[1024,256]{1,0:T(8,128)}, f32[1024,256]{1,0:T(8,128)}) custom-call(s32[8]{0:T(128)S(1)} %stack.129.places, bf16[8,512,1024]{2,1,0:T(8,128)(2,1)} %bitcast.90, bf16[1024,3584]{1,0:T(8,128)(2,1)} %w_gate.13, bf16[1024,3584]{1,0:T(8,128)(2,1)} %w_up.13, ...), custom_call_target="tpu_custom_call", output_to_operand_aliasing={{0}: (11, {})} | custom-call | flops 1000 | bytes 1000 | tf_op jit(solution)/shard_map/pallas_call | solution.py:181
  140.1 1.5 collective-permute-start.21
  141.6 3.7 %shard_map.98 = (bf16[3,512,256]{2,1,0:T(8,128)(2,1)}, bf16[3,512,256]{2,1,0:T(8,128)(2,1)}, bf16[3,512,256]{2,1,0:T(8,128)(2,1)}) custom-call(s32[4]{0:T(128)} %get-tuple-element.236.at, bf16[1024,3584]{1,0:T(8,128)(2,1)} %w_gate.13, bf16[1024,3584]{1,0:T(8,128)(2,1)} %w_up.13, bf16[1024,3584]{1,0:T(8,128)(2,1)} %w_down.13, bf16[1024,3584]{1,0:T(8,128)(2,1)} %w_gate.13, ...), custom_call_target="tpu_custom_call" | custom-call | flops 1000 | bytes 1000 | tf_op jit(solution)/shard_map/pallas_call | solution.py:213
  145.3 1.1 collective-permute-start.22
  146.5 1.1 copy-done.13
  147.6 9.9 %shard_map.95 = (f32[1024,192]{1,0:T(8,128)S(1)}, f32[1024,256]{1,0:T(8,128)}, f32[1024,256]{1,0:T(8,128)}) custom-call(s32[8]{0:T(128)S(1)} %stack.128.places, bf16[8,512,1024]{2,1,0:T(8,128)(2,1)} %bitcast.91, bf16[1024,3584]{1,0:T(8,128)(2,1)} %w_gate.13, bf16[1024,3584]{1,0:T(8,128)(2,1)} %w_up.13, ...), custom_call_target="tpu_custom_call", output_to_operand_aliasing={{0}: (11, {})} | custom-call | flops 1000 | bytes 1000 | tf_op jit(solution)/shard_map/pallas_call | solution.py:181
  159.1 1.1 copy-done.7
  160.3 10.1 %shard_map.96 = (f32[1024,192]{1,0:T(8,128)S(1)}, f32[1024,256]{1,0:T(8,128)}, f32[1024,256]{1,0:T(8,128)}) custom-call(s32[8]{0:T(128)S(1)} %stack.127.places, bf16[8,512,1024]{2,1,0:T(8,128)(2,1)} %bitcast.92, bf16[1024,3584]{1,0:T(8,128)(2,1)} %w_gate.13, bf16[1024,3584]{1,0:T(8,128)(2,1)} %w_up.13, ...), custom_call_target="tpu_custom_call", output_to_operand_aliasing={{0}: (11, {})} | custom-call | flops 1000 | bytes 1000 | tf_op jit(solution)/shard_map/pallas_call | solution.py:181
  170.5 3.4 %collective-permute-done.22.refs_2_ = bf16[3,512,256]{2,1,0:T(8,128)(2,1)} collective-permute-done((bf16[3,512,256]{2,1,0:T(8,128)(2,1)}, bf16[3,512,256]{2,1,0:T(8,128)(2,1)}, u32[]{:S(2)}, u32[]{:S(2)}) %collective-permute-start.22) | collective-permute-done | bytes 786464 | tf_op jit(solution)/shard_map/ppermute | solution.py:72
  173.9 1.5 collective-permute-start.30
  175.4 3.6 %shard_map.106 = (bf16[3,512,256]{2,1,0:T(8,128)(2,1)}, bf16[3,512,256]{2,1,0:T(8,128)(2,1)}, bf16[3,512,256]{2,1,0:T(8,128)(2,1)}) custom-call(s32[4]{0:T(128)} %get-tuple-element.223.at, bf16[1024,3584]{1,0:T(8,128)(2,1)} %w_gate.13, bf16[1024,3584]{1,0:T(8,128)(2,1)} %w_up.13, bf16[1024,3584]{1,0:T(8,128)(2,1)} %w_down.13, bf16[1024,3584]{1,0:T(8,128)(2,1)} %w_gate.13, ...), custom_call_target="tpu_custom_call" | custom-call | flops 1000 | bytes 1000 | tf_op jit(solution)/shard_map/pallas_call | solution.py:213
  179.8 1.1 copy-done.2
  180.9 1.1 copy-done.5
  183.2 7.8 %shard_map.99.refs_7_ = f32[1024,192]{1,0:T(8,128)S(1)} custom-call(s32[8]{0:T(128)S(1)} %stack.129.places, bf16[8,512,1024]{2,1,0:T(8,128)(2,1)} %bitcast.82, bf16[1024,3584]{1,0:T(8,128)(2,1)} %w_down.13, bf16[3,512,256]{2,1,0:T(8,128)(2,1)} %collective-permute-done.7.refs_0_, ...), custom_call_target="tpu_custom_call", output_to_operand_aliasing={{}: (12, {})} | custom-call | flops 1000 | bytes 1000 | tf_op jit(solution)/shard_map/pallas_call | solution.py:181
  192.5 10.0 %shard_map.100 = (f32[1024,192]{1,0:T(8,128)S(1)}, f32[1024,256]{1,0:T(8,128)}, f32[1024,256]{1,0:T(8,128)}) custom-call(s32[8]{0:T(128)S(1)} %stack.135.places, bf16[8,512,1024]{2,1,0:T(8,128)(2,1)} %bitcast.93, bf16[1024,3584]{1,0:T(8,128)(2,1)} %w_gate.13, bf16[1024,3584]{1,0:T(8,128)(2,1)} %w_up.13, ...), custom_call_target="tpu_custom_call", output_to_operand_aliasing={{0}: (11, {})} | custom-call | flops 1000 | bytes 1000 | tf_op jit(solution)/shard_map/pallas_call | solution.py:181
  203.1 3.7 %shard_map.107 = (bf16[3,512,256]{2,1,0:T(8,128)(2,1)}, bf16[3,512,256]{2,1,0:T(8,128)(2,1)}, bf16[3,512,256]{2,1,0:T(8,128)(2,1)}) custom-call(s32[4]{0:T(128)} %get-tuple-element.235.at, bf16[1024,3584]{1,0:T(8,128)(2,1)} %w_gate.13, bf16[1024,3584]{1,0:T(8,128)(2,1)} %w_up.13, bf16[1024,3584]{1,0:T(8,128)(2,1)} %w_down.13, bf16[1024,3584]{1,0:T(8,128)(2,1)} %w_gate.13, ...), custom_call_target="tpu_custom_call" | custom-call | flops 1000 | bytes 1000 | tf_op jit(solution)/shard_map/pallas_call | solution.py:213
  206.8 1.3 collective-permute-start.38
  209.2 7.8 %shard_map.101.refs_9_ = f32[1024,192]{1,0:T(8,128)S(1)} custom-call(s32[8]{0:T(128)S(1)} %stack.128.places, bf16[8,512,1024]{2,1,0:T(8,128)(2,1)} %bitcast.83, bf16[1024,3584]{1,0:T(8,128)(2,1)} %w_down.13, bf16[3,512,256]{2,1,0:T(8,128)(2,1)} %collective-permute-done.14.refs_0_, ...), custom_call_target="tpu_custom_call", output_to_operand_aliasing={{}: (12, {})} | custom-call | flops 1000 | bytes 1000 | tf_op jit(solution)/shard_map/pallas_call | solution.py:181
  217.1 8.2 %shard_map.102.refs_7_ = f32[1024,192]{1,0:T(8,128)S(1)} custom-call(s32[8]{0:T(128)S(1)} %stack.127.places, bf16[8,512,1024]{2,1,0:T(8,128)(2,1)} %bitcast.84, bf16[1024,3584]{1,0:T(8,128)(2,1)} %w_down.13, bf16[3,512,256]{2,1,0:T(8,128)(2,1)} %collective-permute-done.16.refs_0_, ...), custom_call_target="tpu_custom_call", output_to_operand_aliasing={{}: (12, {})} | custom-call | flops 1000 | bytes 1000 | tf_op jit(solution)/shard_map/pallas_call | solution.py:181
  226.3 1.2 collective-permute-start.34
  227.9 12.1 %collective-permute-done.38.refs_2_ = bf16[3,512,256]{2,1,0:T(8,128)(2,1)} collective-permute-done((bf16[3,512,256]{2,1,0:T(8,128)(2,1)}, bf16[3,512,256]{2,1,0:T(8,128)(2,1)}, u32[]{:S(2)}, u32[]{:S(2)}) %collective-permute-start.38) | collective-permute-done | bytes 786464 | tf_op jit(solution)/shard_map/ppermute | solution.py:72
  240.1 1.9 collective-permute-start.39
  242.0 10.2 %shard_map.103 = (f32[1024,192]{1,0:T(8,128)S(1)}, f32[1024,256]{1,0:T(8,128)}, f32[1024,256]{1,0:T(8,128)}) custom-call(s32[8]{0:T(128)S(1)} %stack.126.places, bf16[8,512,1024]{2,1,0:T(8,128)(2,1)} %bitcast.94, bf16[1024,3584]{1,0:T(8,128)(2,1)} %w_gate.13, bf16[1024,3584]{1,0:T(8,128)(2,1)} %w_up.13, ...), custom_call_target="tpu_custom_call", output_to_operand_aliasing={{0}: (11, {})} | custom-call | flops 1000 | bytes 1000 | tf_op jit(solution)/shard_map/pallas_call | solution.py:181
  252.2 8.0 %shard_map.104.refs_9_ = f32[1024,192]{1,0:T(8,128)S(1)} custom-call(s32[8]{0:T(128)S(1)} %stack.135.places, bf16[8,512,1024]{2,1,0:T(8,128)(2,1)} %bitcast.85, bf16[1024,3584]{1,0:T(8,128)(2,1)} %w_down.13, bf16[3,512,256]{2,1,0:T(8,128)(2,1)} %collective-permute-done.26.refs_0_, ...), custom_call_target="tpu_custom_call", output_to_operand_aliasing={{}: (12, {})} | custom-call | flops 1000 | bytes 1000 | tf_op jit(solution)/shard_map/pallas_call | solution.py:181
  260.2 8.1 %shard_map.105.refs_7_ = f32[1024,192]{1,0:T(8,128)S(1)} custom-call(s32[8]{0:T(128)S(1)} %stack.126.places, bf16[8,512,1024]{2,1,0:T(8,128)(2,1)} %bitcast.86, bf16[1024,3584]{1,0:T(8,128)(2,1)} %w_down.13, bf16[3,512,256]{2,1,0:T(8,128)(2,1)} %collective-permute-done.28.refs_0_, ...), custom_call_target="tpu_custom_call", output_to_operand_aliasing={{}: (12, {})} | custom-call | flops 1000 | bytes 1000 | tf_op jit(solution)/shard_map/pallas_call | solution.py:181
  269.2 1.8 collective-permute-start.42
  271.0 1.2 fusion.10
  272.4 1.6 copy.50
  274.0 2.4 copy.49
  276.5 1.3 copy.48
  277.8 2.1 pad_maximum_fusion.d_ref
  279.9 5.5 %shard_map.111 = f32[1024,64]{1,0:T(8,128)S(1)} custom-call(bf16[8,512,1024]{2,1,0:T(8,128)(2,1)} %bitcast.87, bf16[4096,64]{1,0:T(8,128)(2,1)S(1)} %bitcast.80), custom_call_target="tpu_custom_call" | custom-call | flops 1000 | bytes 1000 | tf_op jit(solution)/shard_map/pallas_call | solution.py:122
  285.5 5.6 %shard_map.108 = f32[1024,128]{1,0:T(8,128)S(1)} custom-call(bf16[8,512,1024]{2,1,0:T(8,128)(2,1)} %bitcast.95, bf16[4096,128]{1,0:T(8,128)(2,1)S(1)} %pad_maximum_fusion.d_ref), custom_call_target="tpu_custom_call" | custom-call | flops 1000 | bytes 1000 | tf_op jit(solution)/shard_map/pallas_call | solution.py:122
  291.1 13.5 %shard_map.109.refs_7_ = f32[1024,192]{1,0:T(8,128)S(1)} custom-call(s32[8]{0:T(128)S(1)} %stack.143.places, bf16[8,512,1024]{2,1,0:T(8,128)(2,1)} %bitcast.96, bf16[8,512,1024]{2,1,0:T(8,128)(2,1)} %bitcast.88, bf16[1024,3584]{1,0:T(8,128)(2,1)} %w_gate.13, bf16[1024,3584]{1,0:T(8,128)(2,1)} %w_up.13, ...), custom_call_target="tpu_custom_call", output_to_operand_aliasing={{}: (13, {})} | custom-call | flops 1000 | bytes 1000 | tf_op jit(solution)/shard_map/pallas_call | solution.py:181
  305.8 13.5 %shard_map.110 = f32[1024,192]{1,0:T(8,128)S(1)} custom-call(s32[8]{0:T(128)S(1)} %stack.142.places, bf16[8,512,1024]{2,1,0:T(8,128)(2,1)} %bitcast.97, bf16[8,512,1024]{2,1,0:T(8,128)(2,1)} %bitcast.89, bf16[1024,3584]{1,0:T(8,128)(2,1)} %w_gate.13, bf16[1024,3584]{1,0:T(8,128)(2,1)} %w_up.13, ...), custom_call_target="tpu_custom_call", output_to_operand_aliasing={{}: (13, {})} | custom-call | flops 1000 | bytes 1000 | tf_op jit(solution)/shard_map/pallas_call | solution.py:181
  323.1 1.2 collective-permute-done.44
  324.4 3.7 %collective-permute-start.47 = (bf16[2,12288]{1,0:T(2,128)(2,1)S(1)}, bf16[2,12288]{1,0:T(2,128)(2,1)S(1)}, u32[]{:S(2)}, u32[]{:S(2)}) collective-permute-start(bf16[2,12288]{1,0:T(2,128)(2,1)S(1)} %fusion.3), channel_id=1, source_target_pairs={{0,3},{1,2},{2,1},{3,0},{4,7},{5,6},{6,5},{7,4},{8,11},{9,10},{10,... | collective-permute-start | bytes 147464 | tf_op jit(solution)/shard_map/ppermute | solution.py:76
  330.4 2.7 collective-permute-done.46
  333.1 1.8 fusion
  (138 shorter events, 27.5 us)
Async XLA Ops:
  6.5 3.9 %copy-start.22 = (bf16[8,12288]{1,0:T(8,128)(2,1)S(1)}, bf16[8,12288]{1,0:T(8,128)(2,1)}, u32[]{:S(2)}) copy-start(bf16[8,12288]{1,0:T(8,128)(2,1)} %param.17) | copy-start | bytes 589828
  6.5 120.0 %all-gather.5.cloned.1.call-start = ((), (), s32[]{:S(2)}) async-start(), calls=%async_computation | async-start | bytes 9437184 | tf_op jit(solution)/shard_map/all_gather | solution.py:275
  7.3 172.5 %all-gather.7.cloned.1.call-start = ((), (), s32[]{:S(2)}) async-start(), calls=%async_computation.1 | async-start | bytes 9437184 | tf_op jit(solution)/shard_map/all_gather | solution.py:276
  10.4 12.9 %collective-permute-start = (bf16[8,12288]{1,0:T(8,128)(2,1)S(1)}, bf16[8,12288]{1,0:T(8,128)(2,1)S(1)}, u32[]{:S(2)}, u32[]{:S(2)}) collective-permute-start(bf16[8,12288]{1,0:T(8,128)(2,1)S(1)} %copy-done.22), channel_id=1, source_target_pairs={{0,8},{4,12},{8,0},{12,4},{1,9},{5,13},{9,1},{13,5},{2,10},{6,14},... | collective-permute-start | bytes 589832 | tf_op jit(solution)/shard_map/ppermute | solution.py:72
  18.3 20.7 %collective-permute-start.1 = (bf16[3,512,256]{2,1,0:T(8,128)(2,1)}, bf16[3,512,256]{2,1,0:T(8,128)(2,1)S(1)}, u32[]{:S(2)}, u32[]{:S(2)}) collective-permute-start(bf16[3,512,256]{2,1,0:T(8,128)(2,1)} %get-tuple-element.114), channel_id=1, source_target_pairs={{0,8},{4,12},{8,0},{12,4},{1,9},{5,13},{9,1},{13,5},{2,10},{6,14},... | collective-permute-start | bytes 2359304 | tf_op jit(solution)/shard_map/ppermute | solution.py:72
  18.4 35.1 %collective-permute-start.2 = (bf16[3,512,256]{2,1,0:T(8,128)(2,1)}, bf16[3,512,256]{2,1,0:T(8,128)(2,1)S(1)}, u32[]{:S(2)}, u32[]{:S(2)}) collective-permute-start(bf16[3,512,256]{2,1,0:T(8,128)(2,1)} %get-tuple-element.125), channel_id=1, source_target_pairs={{0,12},{4,8},{8,4},{12,0},{1,13},{5,9},{9,5},{13,1},{2,14},{6,10},... | collective-permute-start | bytes 2359304 | tf_op jit(solution)/shard_map/ppermute | solution.py:72
  39.0 38.8 %copy-start = (bf16[3,512,256]{2,1,0:T(8,128)(2,1)}, bf16[3,512,256]{2,1,0:T(8,128)(2,1)S(1)}, u32[]{:S(2)}) copy-start(bf16[3,512,256]{2,1,0:T(8,128)(2,1)S(1)} %collective-permute-done.1.refs_2_) | copy-start | bytes 2359300
  39.0 18.5 %collective-permute-start.3 = (bf16[3,512,256]{2,1,0:T(8,128)(2,1)S(1)}, bf16[3,512,256]{2,1,0:T(8,128)(2,1)S(1)}, u32[]{:S(2)}, u32[]{:S(2)}) collective-permute-start(bf16[3,512,256]{2,1,0:T(8,128)(2,1)S(1)} %collective-permute-done.1.refs_2_), channel_id=1, source_target_pairs={{0,16},{16,0},{1,17},{17,1},{2,18},{18,2},{3,19},{19,3},{4,20},{20... | collective-permute-start | bytes 2359304 | tf_op jit(solution)/shard_map/ppermute | solution.py:80
  40.5 32.2 %collective-permute-start.4 = (bf16[3,512,256]{2,1,0:T(8,128)(2,1)}, bf16[3,512,256]{2,1,0:T(8,128)(2,1)S(1)}, u32[]{:S(2)}, u32[]{:S(2)}) collective-permute-start(bf16[3,512,256]{2,1,0:T(8,128)(2,1)} %get-tuple-element.120), channel_id=1, source_target_pairs={{0,8},{4,12},{8,0},{12,4},{1,9},{5,13},{9,1},{13,5},{2,10},{6,14},... | collective-permute-start | bytes 2359304 | tf_op jit(solution)/shard_map/ppermute | solution.py:72
  53.5 24.3 %copy-start.3 = (bf16[3,512,256]{2,1,0:T(8,128)(2,1)}, bf16[3,512,256]{2,1,0:T(8,128)(2,1)S(1)}, u32[]{:S(2)}) copy-start(bf16[3,512,256]{2,1,0:T(8,128)(2,1)S(1)} %collective-permute-done.2.refs_3_) | copy-start | bytes 2359300
  53.5 24.4 %collective-permute-start.5 = (bf16[3,512,256]{2,1,0:T(8,128)(2,1)S(1)}, bf16[3,512,256]{2,1,0:T(8,128)(2,1)}, u32[]{:S(2)}, u32[]{:S(2)}) collective-permute-start(bf16[3,512,256]{2,1,0:T(8,128)(2,1)S(1)} %collective-permute-done.2.refs_3_), channel_id=1, source_target_pairs={{0,16},{16,0},{1,17},{17,1},{2,18},{18,2},{3,19},{19,3},{4,20},{20... | collective-permute-start | bytes 2359304 | tf_op jit(solution)/shard_map/ppermute | solution.py:80
  55.5 17.2 %collective-permute-start.9 = (bf16[2,8,12288]{2,1,0:T(8,128)(2,1)S(1)}, bf16[2,8,12288]{2,1,0:T(8,128)(2,1)}, u32[]{:S(2)}, u32[]{:S(2)}) collective-permute-start(bf16[2,8,12288]{2,1,0:T(8,128)(2,1)S(1)} %get-tuple-element.128), channel_id=1, source_target_pairs={{0,4},{4,0},{8,12},{12,8},{1,5},{5,1},{9,13},{13,9},{2,6},{6,2},{1... | collective-permute-start | bytes 1179656 | tf_op jit(solution)/shard_map/ppermute | solution.py:72
  57.3 29.9 %collective-permute-start.6 = (bf16[3,512,256]{2,1,0:T(8,128)(2,1)}, bf16[3,512,256]{2,1,0:T(8,128)(2,1)S(1)}, u32[]{:S(2)}, u32[]{:S(2)}) collective-permute-start(bf16[3,512,256]{2,1,0:T(8,128)(2,1)} %get-tuple-element.140), channel_id=1, source_target_pairs={{0,12},{4,8},{8,4},{12,0},{1,13},{5,9},{9,5},{13,1},{2,14},{6,10},... | collective-permute-start | bytes 2359304 | tf_op jit(solution)/shard_map/ppermute | solution.py:72
  58.3 28.8 %collective-permute-start.7 = (bf16[3,512,256]{2,1,0:T(8,128)(2,1)}, bf16[3,512,256]{2,1,0:T(8,128)(2,1)}, u32[]{:S(2)}, u32[]{:S(2)}) collective-permute-start(bf16[3,512,256]{2,1,0:T(8,128)(2,1)} %get-tuple-element.125), channel_id=1, source_target_pairs={{0,4},{4,0},{8,12},{12,8},{1,5},{5,1},{9,13},{13,9},{2,6},{6,2},{1... | collective-permute-start | bytes 2359304 | tf_op jit(solution)/shard_map/ppermute | solution.py:72
  72.7 14.5 %collective-permute-start.8 = (bf16[3,512,256]{2,1,0:T(8,128)(2,1)}, bf16[3,512,256]{2,1,0:T(8,128)(2,1)}, u32[]{:S(2)}, u32[]{:S(2)}) collective-permute-start(bf16[3,512,256]{2,1,0:T(8,128)(2,1)} %get-tuple-element.127), channel_id=1, source_target_pairs={{0,4},{4,0},{8,12},{12,8},{1,5},{5,1},{9,13},{13,9},{2,6},{6,2},{1... | collective-permute-start | bytes 2359304 | tf_op jit(solution)/shard_map/ppermute | solution.py:72
  72.7 20.3 %collective-permute-start.10 = (bf16[3,512,256]{2,1,0:T(8,128)(2,1)S(1)}, bf16[3,512,256]{2,1,0:T(8,128)(2,1)}, u32[]{:S(2)}, u32[]{:S(2)}) collective-permute-start(bf16[3,512,256]{2,1,0:T(8,128)(2,1)S(1)} %collective-permute-done.4.refs_2_), channel_id=1, source_target_pairs={{0,16},{16,0},{1,17},{17,1},{2,18},{18,2},{3,19},{19,3},{4,20},{20... | collective-permute-start | bytes 2359304 | tf_op jit(solution)/shard_map/ppermute | solution.py:80
  77.8 28.6 %collective-permute-start.11 = (bf16[3,512,256]{2,1,0:T(8,128)(2,1)}, bf16[3,512,256]{2,1,0:T(8,128)(2,1)S(1)}, u32[]{:S(2)}, u32[]{:S(2)}) collective-permute-start(bf16[3,512,256]{2,1,0:T(8,128)(2,1)} %get-tuple-element.135), channel_id=1, source_target_pairs={{0,8},{4,12},{8,0},{12,4},{1,9},{5,13},{9,1},{13,5},{2,10},{6,14},... | collective-permute-start | bytes 2359304 | tf_op jit(solution)/shard_map/ppermute | solution.py:72
  87.2 24.4 %collective-permute-start.12 = (bf16[3,512,256]{2,1,0:T(8,128)(2,1)S(1)}, bf16[3,512,256]{2,1,0:T(8,128)(2,1)S(1)}, u32[]{:S(2)}, u32[]{:S(2)}) collective-permute-start(bf16[3,512,256]{2,1,0:T(8,128)(2,1)S(1)} %collective-permute-done.6.refs_3_), channel_id=1, source_target_pairs={{0,16},{16,0},{1,17},{17,1},{2,18},{18,2},{3,19},{19,3},{4,20},{20... | collective-permute-start | bytes 2359304 | tf_op jit(solution)/shard_map/ppermute | solution.py:80
  89.2 31.7 %collective-permute-start.13 = (bf16[3,512,256]{2,1,0:T(8,128)(2,1)}, bf16[3,512,256]{2,1,0:T(8,128)(2,1)}, u32[]{:S(2)}, u32[]{:S(2)}) collective-permute-start(bf16[3,512,256]{2,1,0:T(8,128)(2,1)} %get-tuple-element.145), channel_id=1, source_target_pairs={{0,12},{4,8},{8,4},{12,0},{1,13},{5,9},{9,5},{13,1},{2,14},{6,10},... | collective-permute-start | bytes 2359304 | tf_op jit(solution)/shard_map/ppermute | solution.py:72
  91.1 29.7 %collective-permute-start.14 = (bf16[3,512,256]{2,1,0:T(8,128)(2,1)}, bf16[3,512,256]{2,1,0:T(8,128)(2,1)}, u32[]{:S(2)}, u32[]{:S(2)}) collective-permute-start(bf16[3,512,256]{2,1,0:T(8,128)(2,1)} %get-tuple-element.140), channel_id=1, source_target_pairs={{0,4},{4,0},{8,12},{12,8},{1,5},{5,1},{9,13},{13,9},{2,6},{6,2},{1... | collective-permute-start | bytes 2359304 | tf_op jit(solution)/shard_map/ppermute | solution.py:72
  93.0 27.9 %collective-permute-start.15 = (bf16[3,512,256]{2,1,0:T(8,128)(2,1)}, bf16[3,512,256]{2,1,0:T(8,128)(2,1)}, u32[]{:S(2)}, u32[]{:S(2)}) collective-permute-start(bf16[3,512,256]{2,1,0:T(8,128)(2,1)} %get-tuple-element.142), channel_id=1, source_target_pairs={{0,4},{4,0},{8,12},{12,8},{1,5},{5,1},{9,13},{13,9},{2,6},{6,2},{1... | collective-permute-start | bytes 2359304 | tf_op jit(solution)/shard_map/ppermute | solution.py:72
  106.4 5.2 %copy-start.6 = (bf16[3,512,256]{2,1,0:T(8,128)(2,1)}, bf16[3,512,256]{2,1,0:T(8,128)(2,1)S(1)}, u32[]{:S(2)}) copy-start(bf16[3,512,256]{2,1,0:T(8,128)(2,1)S(1)} %collective-permute-done.11.refs_2_) | copy-start | bytes 2359300
  106.4 20.1 %collective-permute-start.18 = (bf16[3,512,256]{2,1,0:T(8,128)(2,1)S(1)}, bf16[3,512,256]{2,1,0:T(8,128)(2,1)}, u32[]{:S(2)}, u32[]{:S(2)}) collective-permute-start(bf16[3,512,256]{2,1,0:T(8,128)(2,1)S(1)} %collective-permute-done.11.refs_2_), channel_id=1, source_target_pairs={{0,16},{16,0},{1,17},{17,1},{2,18},{18,2},{3,19},{19,3},{4,20},{20... | collective-permute-start | bytes 2359304 | tf_op jit(solution)/shard_map/ppermute | solution.py:80
  112.5 27.6 %collective-permute-start.20 = (bf16[3,512,256]{2,1,0:T(8,128)(2,1)}, bf16[3,512,256]{2,1,0:T(8,128)(2,1)S(1)}, u32[]{:S(2)}, u32[]{:S(2)}) collective-permute-start(bf16[3,512,256]{2,1,0:T(8,128)(2,1)} %get-tuple-element.157), channel_id=1, source_target_pairs={{0,8},{4,12},{8,0},{12,4},{1,9},{5,13},{9,1},{13,5},{2,10},{6,14},... | collective-permute-start | bytes 2359304 | tf_op jit(solution)/shard_map/ppermute | solution.py:72
  120.9 24.4 %collective-permute-start.16 = (bf16[3,512,256]{2,1,0:T(8,128)(2,1)}, bf16[3,512,256]{2,1,0:T(8,128)(2,1)}, u32[]{:S(2)}, u32[]{:S(2)}) collective-permute-start(bf16[3,512,256]{2,1,0:T(8,128)(2,1)} %get-tuple-element.145), channel_id=1, source_target_pairs={{0,4},{4,0},{8,12},{12,8},{1,5},{5,1},{9,13},{13,9},{2,6},{6,2},{1... | collective-permute-start | bytes 2359304 | tf_op jit(solution)/shard_map/ppermute | solution.py:72
  123.5 34.0 %collective-permute-start.17 = (bf16[3,512,256]{2,1,0:T(8,128)(2,1)}, bf16[3,512,256]{2,1,0:T(8,128)(2,1)}, u32[]{:S(2)}, u32[]{:S(2)}) collective-permute-start(bf16[3,512,256]{2,1,0:T(8,128)(2,1)} %get-tuple-element.147), channel_id=1, source_target_pairs={{0,4},{4,0},{8,12},{12,8},{1,5},{5,1},{9,13},{13,9},{2,6},{6,2},{1... | collective-permute-start | bytes 2359304 | tf_op jit(solution)/shard_map/ppermute | solution.py:72
  123.5 34.0 %collective-permute-start.19 = (bf16[3,512,256]{2,1,0:T(8,128)(2,1)}, bf16[3,512,256]{2,1,0:T(8,128)(2,1)}, u32[]{:S(2)}, u32[]{:S(2)}) collective-permute-start(bf16[3,512,256]{2,1,0:T(8,128)(2,1)} %collective-permute-done.13.refs_3_), channel_id=1, source_target_pairs={{0,16},{16,0},{1,17},{17,1},{2,18},{18,2},{3,19},{19,3},{4,20},{20... | collective-permute-start | bytes 2359304 | tf_op jit(solution)/shard_map/ppermute | solution.py:80
  126.4 31.0 %collective-permute-start.23 = (bf16[3,512,256]{2,1,0:T(8,128)(2,1)}, bf16[3,512,256]{2,1,0:T(8,128)(2,1)}, u32[]{:S(2)}, u32[]{:S(2)}) collective-permute-start(bf16[3,512,256]{2,1,0:T(8,128)(2,1)} %get-tuple-element.175), channel_id=1, source_target_pairs={{0,12},{4,8},{8,4},{12,0},{1,13},{5,9},{9,5},{13,1},{2,14},{6,10},... | collective-permute-start | bytes 2359304 | tf_op jit(solution)/shard_map/ppermute | solution.py:72
  126.6 1.1 copy-start.1
  140.1 30.3 %collective-permute-start.21 = (bf16[3,512,256]{2,1,0:T(8,128)(2,1)S(1)}, bf16[3,512,256]{2,1,0:T(8,128)(2,1)}, u32[]{:S(2)}, u32[]{:S(2)}) collective-permute-start(bf16[3,512,256]{2,1,0:T(8,128)(2,1)S(1)} %collective-permute-done.20.refs_2_), channel_id=1, source_target_pairs={{0,16},{16,0},{1,17},{17,1},{2,18},{18,2},{3,19},{19,3},{4,20},{20... | collective-permute-start | bytes 2359304 | tf_op jit(solution)/shard_map/ppermute | solution.py:80
  145.3 28.6 %collective-permute-start.22 = (bf16[3,512,256]{2,1,0:T(8,128)(2,1)}, bf16[3,512,256]{2,1,0:T(8,128)(2,1)}, u32[]{:S(2)}, u32[]{:S(2)}) collective-permute-start(bf16[3,512,256]{2,1,0:T(8,128)(2,1)} %get-tuple-element.164), channel_id=1, source_target_pairs={{0,8},{4,12},{8,0},{12,4},{1,9},{5,13},{9,1},{13,5},{2,10},{6,14},... | collective-permute-start | bytes 2359304 | tf_op jit(solution)/shard_map/ppermute | solution.py:72
  146.5 1.1 copy-start.13
  157.5 21.5 %collective-permute-start.24 = (bf16[3,512,256]{2,1,0:T(8,128)(2,1)}, bf16[3,512,256]{2,1,0:T(8,128)(2,1)}, u32[]{:S(2)}, u32[]{:S(2)}) collective-permute-start(bf16[3,512,256]{2,1,0:T(8,128)(2,1)} %collective-permute-done.23.refs_3_), channel_id=1, source_target_pairs={{0,16},{16,0},{1,17},{17,1},{2,18},{18,2},{3,19},{19,3},{4,20},{20... | collective-permute-start | bytes 2359304 | tf_op jit(solution)/shard_map/ppermute | solution.py:80
  158.3 32.7 %collective-permute-start.25 = (bf16[3,512,256]{2,1,0:T(8,128)(2,1)}, bf16[3,512,256]{2,1,0:T(8,128)(2,1)}, u32[]{:S(2)}, u32[]{:S(2)}) collective-permute-start(bf16[3,512,256]{2,1,0:T(8,128)(2,1)} %get-tuple-element.179), channel_id=1, source_target_pairs={{0,12},{4,8},{8,4},{12,0},{1,13},{5,9},{9,5},{13,1},{2,14},{6,10},... | collective-permute-start | bytes 2359304 | tf_op jit(solution)/shard_map/ppermute | solution.py:72
  158.6 32.4 %collective-permute-start.26 = (bf16[3,512,256]{2,1,0:T(8,128)(2,1)}, bf16[3,512,256]{2,1,0:T(8,128)(2,1)}, u32[]{:S(2)}, u32[]{:S(2)}) collective-permute-start(bf16[3,512,256]{2,1,0:T(8,128)(2,1)} %get-tuple-element.175), channel_id=1, source_target_pairs={{0,4},{4,0},{8,12},{12,8},{1,5},{5,1},{9,13},{13,9},{2,6},{6,2},{1... | collective-permute-start | bytes 2359304 | tf_op jit(solution)/shard_map/ppermute | solution.py:72
  170.4 20.7 %collective-permute-start.27 = (bf16[3,512,256]{2,1,0:T(8,128)(2,1)}, bf16[3,512,256]{2,1,0:T(8,128)(2,1)}, u32[]{:S(2)}, u32[]{:S(2)}) collective-permute-start(bf16[3,512,256]{2,1,0:T(8,128)(2,1)} %get-tuple-element.177), channel_id=1, source_target_pairs={{0,4},{4,0},{8,12},{12,8},{1,5},{5,1},{9,13},{13,9},{2,6},{6,2},{1... | collective-permute-start | bytes 2359304 | tf_op jit(solution)/shard_map/ppermute | solution.py:72
  173.9 28.6 %collective-permute-start.30 = (bf16[3,512,256]{2,1,0:T(8,128)(2,1)}, bf16[3,512,256]{2,1,0:T(8,128)(2,1)}, u32[]{:S(2)}, u32[]{:S(2)}) collective-permute-start(bf16[3,512,256]{2,1,0:T(8,128)(2,1)} %collective-permute-done.22.refs_2_), channel_id=1, source_target_pairs={{0,16},{16,0},{1,17},{17,1},{2,18},{18,2},{3,19},{19,3},{4,20},{20... | collective-permute-start | bytes 2359304 | tf_op jit(solution)/shard_map/ppermute | solution.py:80
  179.0 27.7 %collective-permute-start.37 = (bf16[3,512,256]{2,1,0:T(8,128)(2,1)}, bf16[3,512,256]{2,1,0:T(8,128)(2,1)}, u32[]{:S(2)}, u32[]{:S(2)}) collective-permute-start(bf16[3,512,256]{2,1,0:T(8,128)(2,1)} %get-tuple-element.211), channel_id=1, source_target_pairs={{0,8},{4,12},{8,0},{12,4},{1,9},{5,13},{9,1},{13,5},{2,10},{6,14},... | collective-permute-start | bytes 2359304 | tf_op jit(solution)/shard_map/ppermute | solution.py:72
  179.8 1.1 copy-start.2
  191.0 34.2 %collective-permute-start.28 = (bf16[3,512,256]{2,1,0:T(8,128)(2,1)}, bf16[3,512,256]{2,1,0:T(8,128)(2,1)}, u32[]{:S(2)}, u32[]{:S(2)}) collective-permute-start(bf16[3,512,256]{2,1,0:T(8,128)(2,1)} %get-tuple-element.179), channel_id=1, source_target_pairs={{0,4},{4,0},{8,12},{12,8},{1,5},{5,1},{9,13},{13,9},{2,6},{6,2},{1... | collective-permute-start | bytes 2359304 | tf_op jit(solution)/shard_map/ppermute | solution.py:72
  191.1 34.1 %collective-permute-start.29 = (bf16[3,512,256]{2,1,0:T(8,128)(2,1)}, bf16[3,512,256]{2,1,0:T(8,128)(2,1)}, u32[]{:S(2)}, u32[]{:S(2)}) collective-permute-start(bf16[3,512,256]{2,1,0:T(8,128)(2,1)} %get-tuple-element.181), channel_id=1, source_target_pairs={{0,4},{4,0},{8,12},{12,8},{1,5},{5,1},{9,13},{13,9},{2,6},{6,2},{1... | collective-permute-start | bytes 2359304 | tf_op jit(solution)/shard_map/ppermute | solution.py:72
  191.6 33.7 %collective-permute-start.31 = (bf16[3,512,256]{2,1,0:T(8,128)(2,1)}, bf16[3,512,256]{2,1,0:T(8,128)(2,1)}, u32[]{:S(2)}, u32[]{:S(2)}) collective-permute-start(bf16[3,512,256]{2,1,0:T(8,128)(2,1)} %collective-permute-done.25.refs_3_), channel_id=1, source_target_pairs={{0,16},{16,0},{1,17},{17,1},{2,18},{18,2},{3,19},{19,3},{4,20},{20... | collective-permute-start | bytes 2359304 | tf_op jit(solution)/shard_map/ppermute | solution.py:80
  202.5 22.8 %collective-permute-start.32 = (bf16[3,512,256]{2,1,0:T(8,128)(2,1)}, bf16[3,512,256]{2,1,0:T(8,128)(2,1)}, u32[]{:S(2)}, u32[]{:S(2)}) collective-permute-start(bf16[3,512,256]{2,1,0:T(8,128)(2,1)} %get-tuple-element.206), channel_id=1, source_target_pairs={{0,12},{4,8},{8,4},{12,0},{1,13},{5,9},{9,5},{13,1},{2,14},{6,10},... | collective-permute-start | bytes 2359304 | tf_op jit(solution)/shard_map/ppermute | solution.py:72
  206.8 33.3 %collective-permute-start.38 = (bf16[3,512,256]{2,1,0:T(8,128)(2,1)}, bf16[3,512,256]{2,1,0:T(8,128)(2,1)}, u32[]{:S(2)}, u32[]{:S(2)}) collective-permute-start(bf16[3,512,256]{2,1,0:T(8,128)(2,1)} %get-tuple-element.213), channel_id=1, source_target_pairs={{0,8},{4,12},{8,0},{12,4},{1,9},{5,13},{9,1},{13,5},{2,10},{6,14},... | collective-permute-start | bytes 2359304 | tf_op jit(solution)/shard_map/ppermute | solution.py:72
  209.2 7.8 %copy-start.8 = (bf16[3,512,256]{2,1,0:T(8,128)(2,1)S(1)}, bf16[3,512,256]{2,1,0:T(8,128)(2,1)}, u32[]{:S(2)}) copy-start(bf16[3,512,256]{2,1,0:T(8,128)(2,1)} %copy-done.6) | copy-start | bytes 2359300
  225.3 43.0 %collective-permute-start.33 = (bf16[3,512,256]{2,1,0:T(8,128)(2,1)}, bf16[3,512,256]{2,1,0:T(8,128)(2,1)S(1)}, u32[]{:S(2)}, u32[]{:S(2)}) collective-permute-start(bf16[3,512,256]{2,1,0:T(8,128)(2,1)} %collective-permute-done.32.refs_3_), channel_id=1, source_target_pairs={{0,16},{16,0},{1,17},{17,1},{2,18},{18,2},{3,19},{19,3},{4,20},{20... | collective-permute-start | bytes 2359304 | tf_op jit(solution)/shard_map/ppermute | solution.py:80
  226.3 42.3 %collective-permute-start.34 = (bf16[3,512,256]{2,1,0:T(8,128)(2,1)}, bf16[3,512,256]{2,1,0:T(8,128)(2,1)}, u32[]{:S(2)}, u32[]{:S(2)}) collective-permute-start(bf16[3,512,256]{2,1,0:T(8,128)(2,1)} %get-tuple-element.216), channel_id=1, source_target_pairs={{0,12},{4,8},{8,4},{12,0},{1,13},{5,9},{9,5},{13,1},{2,14},{6,10},... | collective-permute-start | bytes 2359304 | tf_op jit(solution)/shard_map/ppermute | solution.py:72
  227.4 41.1 %collective-permute-start.35 = (bf16[3,512,256]{2,1,0:T(8,128)(2,1)}, bf16[3,512,256]{2,1,0:T(8,128)(2,1)}, u32[]{:S(2)}, u32[]{:S(2)}) collective-permute-start(bf16[3,512,256]{2,1,0:T(8,128)(2,1)} %get-tuple-element.206), channel_id=1, source_target_pairs={{0,4},{4,0},{8,12},{12,8},{1,5},{5,1},{9,13},{13,9},{2,6},{6,2},{1... | collective-permute-start | bytes 2359304 | tf_op jit(solution)/shard_map/ppermute | solution.py:72
  227.8 40.8 %collective-permute-start.36 = (bf16[3,512,256]{2,1,0:T(8,128)(2,1)}, bf16[3,512,256]{2,1,0:T(8,128)(2,1)}, u32[]{:S(2)}, u32[]{:S(2)}) collective-permute-start(bf16[3,512,256]{2,1,0:T(8,128)(2,1)} %get-tuple-element.208), channel_id=1, source_target_pairs={{0,4},{4,0},{8,12},{12,8},{1,5},{5,1},{9,13},{13,9},{2,6},{6,2},{1... | collective-permute-start | bytes 2359304 | tf_op jit(solution)/shard_map/ppermute | solution.py:72
  240.1 28.5 %collective-permute-start.39 = (bf16[3,512,256]{2,1,0:T(8,128)(2,1)}, bf16[3,512,256]{2,1,0:T(8,128)(2,1)S(1)}, u32[]{:S(2)}, u32[]{:S(2)}) collective-permute-start(bf16[3,512,256]{2,1,0:T(8,128)(2,1)} %collective-permute-done.38.refs_2_), channel_id=1, source_target_pairs={{0,16},{16,0},{1,17},{17,1},{2,18},{18,2},{3,19},{19,3},{4,20},{20... | collective-permute-start | bytes 2359304 | tf_op jit(solution)/shard_map/ppermute | solution.py:80
  260.2 10.8 %copy-start.20 = (bf16[3,4096,64]{1,2,0:T(8,128)(2,1)S(1)}, bf16[3,4096,64]{1,2,0:T(8,128)(2,1)}, u32[]{:S(2)}) copy-start(bf16[3,4096,64]{1,2,0:T(8,128)(2,1)} %param.15) | copy-start | bytes 4718596
  268.3 4.1 %copy-start.17 = (bf16[3,512,256]{2,1,0:T(8,128)(2,1)}, bf16[3,512,256]{2,1,0:T(8,128)(2,1)S(1)}, u32[]{:S(2)}) copy-start(bf16[3,512,256]{2,1,0:T(8,128)(2,1)S(1)} %collective-permute-done.33.refs_5_) | copy-start | bytes 2359300
  268.3 22.8 %collective-permute-start.43 = (bf16[3,512,256]{2,1,0:T(8,128)(2,1)}, bf16[3,512,256]{2,1,0:T(8,128)(2,1)}, u32[]{:S(2)}, u32[]{:S(2)}) collective-permute-start(bf16[3,512,256]{2,1,0:T(8,128)(2,1)} %collective-permute-done.37.refs_2_), channel_id=1, source_target_pairs={{0,16},{16,0},{1,17},{17,1},{2,18},{18,2},{3,19},{19,3},{4,20},{20... | collective-permute-start | bytes 2359304 | tf_op jit(solution)/shard_map/ppermute | solution.py:80
  268.6 3.8 %copy-start.15 = (bf16[3,512,256]{2,1,0:T(8,128)(2,1)}, bf16[3,512,256]{2,1,0:T(8,128)(2,1)S(1)}, u32[]{:S(2)}) copy-start(bf16[3,512,256]{2,1,0:T(8,128)(2,1)S(1)} %collective-permute-done.39.refs_4_) | copy-start | bytes 2359300
  268.6 36.2 %collective-permute-start.40 = (bf16[3,512,256]{2,1,0:T(8,128)(2,1)}, bf16[3,512,256]{2,1,0:T(8,128)(2,1)S(1)}, u32[]{:S(2)}, u32[]{:S(2)}) collective-permute-start(bf16[3,512,256]{2,1,0:T(8,128)(2,1)} %get-tuple-element.216), channel_id=1, source_target_pairs={{0,4},{4,0},{8,12},{12,8},{1,5},{5,1},{9,13},{13,9},{2,6},{6,2},{1... | collective-permute-start | bytes 2359304 | tf_op jit(solution)/shard_map/ppermute | solution.py:72
  268.7 36.2 %collective-permute-start.41 = (bf16[3,512,256]{2,1,0:T(8,128)(2,1)}, bf16[3,512,256]{2,1,0:T(8,128)(2,1)}, u32[]{:S(2)}, u32[]{:S(2)}) collective-permute-start(bf16[3,512,256]{2,1,0:T(8,128)(2,1)} %get-tuple-element.218), channel_id=1, source_target_pairs={{0,4},{4,0},{8,12},{12,8},{1,5},{5,1},{9,13},{13,9},{2,6},{6,2},{1... | collective-permute-start | bytes 2359304 | tf_op jit(solution)/shard_map/ppermute | solution.py:72
  269.2 35.7 %collective-permute-start.42 = (bf16[3,512,256]{2,1,0:T(8,128)(2,1)}, bf16[3,512,256]{2,1,0:T(8,128)(2,1)}, u32[]{:S(2)}, u32[]{:S(2)}) collective-permute-start(bf16[3,512,256]{2,1,0:T(8,128)(2,1)} %collective-permute-done.34.refs_3_), channel_id=1, source_target_pairs={{0,16},{16,0},{1,17},{17,1},{2,18},{18,2},{3,19},{19,3},{4,20},{20... | collective-permute-start | bytes 2359304 | tf_op jit(solution)/shard_map/ppermute | solution.py:80
  272.4 4.0 %copy-start.19 = (bf16[1,4096,64]{1,2,0:T(8,128)(2,1)S(1)}, bf16[1,4096,64]{1,2,0:T(8,128)(2,1)}, u32[]{:S(2)}) copy-start(bf16[1,4096,64]{1,2,0:T(8,128)(2,1)} %get-tuple-element.225) | copy-start | bytes 1572868
  285.5 5.6 %copy-start.18 = (bf16[3,512,256]{2,1,0:T(8,128)(2,1)S(1)}, bf16[3,512,256]{2,1,0:T(8,128)(2,1)}, u32[]{:S(2)}) copy-start(bf16[3,512,256]{2,1,0:T(8,128)(2,1)} %copy-done.17) | copy-start | bytes 2359300
  321.6 7.2 %copy-start.21 = (bf16[1,2,8,12288]{3,2,1,0:T(8,128)(2,1)S(1)}, bf16[1,2,8,12288]{3,2,1,0:T(8,128)(2,1)}, u32[]{:S(2)}) copy-start(bf16[1,2,8,12288]{3,2,1,0:T(8,128)(2,1)} %get-tuple-element.233) | copy-start | bytes 1179652
  322.9 1.4 collective-permute-start.44
  324.4 6.0 %collective-permute-start.47 = (bf16[2,12288]{1,0:T(2,128)(2,1)S(1)}, bf16[2,12288]{1,0:T(2,128)(2,1)S(1)}, u32[]{:S(2)}, u32[]{:S(2)}) collective-permute-start(bf16[2,12288]{1,0:T(2,128)(2,1)S(1)} %fusion.3), channel_id=1, source_target_pairs={{0,3},{1,2},{2,1},{3,0},{4,7},{5,6},{6,5},{7,4},{8,11},{9,10},{10,... | collective-permute-start | bytes 147464 | tf_op jit(solution)/shard_map/ppermute | solution.py:76
  328.1 5.0 %collective-permute-start.46 = (bf16[2,12288]{1,0:T(2,128)(2,1)S(1)}, bf16[2,12288]{1,0:T(2,128)(2,1)S(1)}, u32[]{:S(2)}, u32[]{:S(2)}) collective-permute-start(bf16[2,12288]{1,0:T(2,128)(2,1)S(1)} %fusion.3), channel_id=1, source_target_pairs={{0,2},{1,3},{2,0},{3,1},{4,6},{5,7},{6,4},{7,5},{8,10},{9,11},{10,... | collective-permute-start | bytes 147464 | tf_op jit(solution)/shard_map/ppermute | solution.py:76
  328.1 5.0 %collective-permute-start.45 = (bf16[2,12288]{1,0:T(2,128)(2,1)S(1)}, bf16[2,12288]{1,0:T(2,128)(2,1)S(1)}, u32[]{:S(2)}, u32[]{:S(2)}) collective-permute-start(bf16[2,12288]{1,0:T(2,128)(2,1)S(1)} %fusion.3), channel_id=1, source_target_pairs={{0,1},{1,0},{2,3},{3,2},{4,5},{5,4},{6,7},{7,6},{8,9},{9,8},{10,11... | collective-permute-start | bytes 147464 | tf_op jit(solution)/shard_map/ppermute | solution.py:76
  (9 other events, 9.7 us)
Sparse Core Ops, SparseCore 0:
  9.0 84.7 all-gather.4
  95.4 81.0 all-gather.6

commit v3 on v2

--- a/solution.py
+++ b/solution.py
@@ -10,6 +10,10 @@
 
 def dot(left, right):
     return jnp.dot(left, right, preferred_element_type=jnp.float32)
+
+
+def dot_rows(left, right):
+    return lax.dot_general(left, right, (((1,), (1,)), ((), ())), preferred_element_type=jnp.float32)
 
 
 def activations(gate_pre, up_pre, back_grad):
@@ -101,13 +105,17 @@
         if value is None:
             sums_ref[:, at] = sums_in[:, at]
         else:
-            product = lax.dot_general(value, ff_ref[m], (((1,), (1,)), ((), ())), preferred_element_type=jnp.float32)
-            sums_ref[:, at] = sums_in[:, at] + product
+            sums_ref[:, at] = sums_in[:, at] + dot_rows(value, ff_ref[m])
 
 
 def direct_kernel(tokens_ref, d_ref, out):
+    count, rank, model = d_ref.shape
     depth = tokens_ref.shape[2]
-    out[...] = sum(dot(tokens_ref[q], d_ref[q * depth : (q + 1) * depth]) for q in range(tokens_ref.shape[0]))
+    for m in range(count):
+        total = 0.0
+        for q in range(model // depth):
+            total += dot_rows(tokens_ref[q], d_ref[m, :, q * depth : (q + 1) * depth])
+        out[:, m * rank : (m + 1) * rank] = total
 
 
 def token_tiles(tokens, near_count, tile):
@@ -116,18 +124,19 @@
     return pl.BlockSpec(shape, lambda i, *_: (i // per_near, i % per_near, 0)), near_count * per_near
 
 
-def direct(tokens, d):
+def direct(tokens, d_columns, at, count):
     tile = 256
     spec, tiles = token_tiles(tokens, 2, tile)
+    _, rank, model = d_columns.shape
     return pl.pallas_call(
         direct_kernel,
-        out_shape=jax.ShapeDtypeStruct((tiles * tile, d.shape[1]), jnp.float32),
+        out_shape=jax.ShapeDtypeStruct((tiles * tile, count * rank), jnp.float32),
         grid=(tiles,),
-        in_specs=[spec, pl.BlockSpec(d.shape, lambda i: (0, 0))],
-        out_specs=pl.BlockSpec((tile, d.shape[1]), lambda i: (i, 0)),
+        in_specs=[spec, pl.BlockSpec((count, rank, model), lambda i: (at // count, 0, 0))],
+        out_specs=pl.BlockSpec((tile, count * rank), lambda i: (i, 0)),
         compiler_params=pltpu.CompilerParams(vmem_limit_bytes=48 * 2**20),
         cost_estimate=pl.CostEstimate(flops=1000, bytes_accessed=1000, transcendentals=0),
-    )(tokens, d)
+    )(tokens, d_columns)
 
 
 def planes(pieces, m):
@@ -275,7 +284,7 @@
     gathered_acts = lax.all_gather(acts, ("near", "tensor"))
     gathered_grad = lax.all_gather(mask_tokens(out_grad, lengths), ("near", "tensor"))
     sums = jnp.zeros((2 * tokens, 3 * rank), jnp.float32)
-    ff_columns = jnp.swapaxes(ff_proj, 1, 2)
+    ff_columns, d_columns = jnp.swapaxes(ff_proj, 1, 2), jnp.swapaxes(d_proj, 1, 2)
     far, relayed, near_rows, cuts = [], [], [], []
     factors = [None] * chunks
 
@@ -294,37 +303,44 @@
             (sums,) = run([full_acts, full_grad], weights, [(v, 3, 0) for v in sources], [])
         return sums
 
+    def make(j):
+        sources = [at(j - 2, w) for w in weights]
+        cuts.append(cut(sources, part, near * chunks + j, (1 - near) * chunks + j, rows, chunk))
+        if j > 0:
+            join(j - 1, *cuts[j])
+
     def send(g):
-        j = g // 2
-        if g % 2 == 0:
-            sources = [at(g - 3, w) for w in weights]
-            cuts.append(cut(sources, part, near * chunks + j, (1 - near) * chunks + j, rows, chunk))
-        far.append(permute_dp(at(g - 2, cuts[j][g % 2]), 2 + g % 2))
+        far.append(permute_dp(at(g - 2, cuts[g // 2][g % 2]), 2 + g % 2))
         join(g, far[g])
 
     work = {
-        6: [(forward_kernel, 0)],
-        7: [(forward_kernel, 1)],
+        5: [(forward_kernel, 0)],
+        6: [(forward_kernel, 1)],
         8: [(forward_kernel, 2)],
         9: [(backward_kernel, 0)],
-        10: [(forward_kernel, 3)],
+        10: [(both_kernel, 3)],
         11: [(backward_kernel, 1), (backward_kernel, 2)],
-        12: [(forward_kernel, 4)],
-        13: [(backward_kernel, 3), (backward_kernel, 4)],
+        12: [(both_kernel, 4)],
+        13: [(both_kernel, 5)],
     }
-    rest = [(both_kernel, 5), (both_kernel, 6)]
+    make(0)
     send(0)
     send(1)
     for g in range(blocks):
+        if g + 1 < chunks:
+            make(g + 1)
         if g in work:
             sums = after(sums, token(ticks[g - 1]))
             for kernel, j in work[g]:
                 sums = add(kernel, j, sums)
             end(g, sums)
+        elif g == 7:
+            left_both = direct(after(full_acts, token(ticks[g - 1])), d_columns, 0, 2)
+            end(g, left_both)
         else:
             end(g, ticks[-1] if ticks else jnp.zeros((8, 128), jnp.float32))
-        relayed.append(permute_parts(at(g, far[g])))
-        join(g + 2, relayed[g])
+        relayed.append(permute_parts(at(min(g, last - 1), far[g])))
+        join(g + 2 if g < 10 else g + 1, relayed[g])
         if g + 2 < blocks:
             send(g + 2)
         if g % 2 == 1:
@@ -333,15 +349,13 @@
         if g == 1:
             near_pair = permute_dp(at(1, pair), 1)
             join(3, near_pair)
-        if g == 5:
-            full_acts = at(5, gathered_acts)
+        if g == 4:
+            full_acts = at(4, gathered_acts)
         if g == 8:
             full_grad = at(8, gathered_grad)
     sums = at(last, sums)
-    left_both = direct(at(last, full_acts), jnp.concatenate([d_proj[0], d_proj[1]], axis=1))
-    right_down = direct(at(last, full_grad), d_proj[2])
-    for kernel, j in rest:
-        sums = add(kernel, j, sums)
+    right_down = direct(after(full_grad, sums), d_columns, 2, 1)
+    sums = add(both_kernel, 6, after(sums, right_down))
     right_gate, right_up, left_down = jnp.split(sums, 3, axis=1)
     left_gate, left_up = jnp.split(left_both, 2, axis=1)
     proj = jnp.stack(
@@ -354,9 +368,8 @@
     ).reshape(2, seq_dev, 3 * rank * rank)
     near_proj = permute_dp(lax.dynamic_index_in_dim(proj, 1 - near, 0, False), 1)
     proj = lax.dynamic_index_in_dim(proj, near, 0, False) + near_proj
-    sent = proj.astype(jnp.bfloat16)
-    for flip in range(1, lax.axis_size("tensor")):
-        proj += permute_tensor(sent, flip).astype(jnp.float32)
+    for flip in (1, 2):
+        proj += permute_tensor(proj, flip)
     flat_scores = lax.dot_general(
         proj.astype(jnp.bfloat16),
         jnp.stack([pair, near_pair]).reshape(4 * queries.shape[0], -1),

time: 344 us -> 330 us (0.959)
  Pallas kernels: 154 us -> 147 us
  local copies, waits for them, and re-layouts: 20.8 us -> 14.9 us
    ppermute x31, waiting for transfers between devices: 88.1 us -> 67.6 us  [permute_dp(): return lax.ppermute(value, DP, [(i, i ^ flip) for i in range(4)])]
    ppermute x14, waiting for transfers between devices: 3.24 us -> 22.9 us  [permute_parts(): return lax.ppermute(value, 'parts', [(0, 1), (1, 0)])]
    pallas_call x12 -> x10, Pallas kernels: 117 us -> 108 us  [add_hidden_units(): pl.pallas_call(kernel, out_shape=out_shape, grid_spec=pltpu.PrefetchScala...]
    unnamed x50 -> x51, local copies, waits for them, and re-layouts: 18.3 us -> 13.6 us
  transfers between devices with their start and end apart: 50 -> 49, of which waited for: 14 -> 19; matrix products, arithmetic and copies ran while one was open for 5% -> 2% of each run, Pallas kernels for 41% -> 41%
where the time goes in v3:
time: 330 us; the launch traced here: 329 us
  Pallas kernels  147 us (45%)
  waiting for transfers between devices  97.8 us (30%)
  starting transfers between devices  42.6 us (13%)
  local copies, waits for them, and re-layouts  14.9 us (5%)
  between operations  13.8 us (4%)
  other arithmetic  6.62 us (2%)
  matrix products  5.65 us (2%)
    pallas_call x10, Pallas kernels, add_hidden_units(): pl.pallas_call(kernel, out_shape=out_shape, grid_spec=pltpu.PrefetchScala...  108 us
    ppermute x31, waiting for transfers between devices, permute_dp(): return lax.ppermute(value, DP, [(i, i ^ flip) for i in range(4)])  67.6 us
    pallas_call x7, Pallas kernels, cut(): pl.pallas_call(cut_kernel, out_shape=[jax.ShapeDtypeStruct((3, rows, chun...  26.2 us
    ppermute x14, waiting for transfers between devices, permute_parts(): return lax.ppermute(value, 'parts', [(0, 1), (1, 0)])  22.9 us
    ppermute x31, starting transfers between devices, permute_dp(): return lax.ppermute(value, DP, [(i, i ^ flip) for i in range(4)])  21.7 us
    ppermute x14, starting transfers between devices, permute_parts(): return lax.ppermute(value, 'parts', [(0, 1), (1, 0)])  16.6 us
    unnamed x51, local copies, waits for them, and re-layouts  13.6 us
    pallas_call x2, Pallas kernels, direct(): pl.pallas_call(direct_kernel, out_shape=jax.ShapeDtypeStruct((tiles * til...  12.8 us
  transfers between devices with their start and end apart: 49, of which 19 were waited for; matrix products, arithmetic and copies ran while one was open for 2% of the time, Pallas kernels for 41%

profile of v3, /device:TPU:0, one launch (start us, length us, event | category | flops | bytes accessed | tf_op | source)
XLA Modules:
  0.0 328.5 jit_solution(13895720116567851990)
XLA Ops:
  8.0 2.3 broadcast_multiply_fusion
  10.4 3.0 collective-permute-start
  14.7 3.6 %shard_map.91 = (bf16[3,512,256]{2,1,0:T(8,128)(2,1)}, bf16[3,512,256]{2,1,0:T(8,128)(2,1)}, bf16[3,512,256]{2,1,0:T(8,128)(2,1)}) custom-call(s32[4]{0:T(128)} %get-tuple-element.229.at, bf16[1024,3584]{1,0:T(8,128)(2,1)} %w_gate.13, bf16[1024,3584]{1,0:T(8,128)(2,1)} %w_up.13, bf16[1024,3584]{1,0:T(8,128)(2,1)} %w_down.13, bf16[1024,3584]{1,0:T(8,128)(2,1)} %w_gate.13, ...), custom_call_target="tpu_custom_call" | custom-call | flops 1000 | bytes 1000 | tf_op jit(solution)/shard_map/pallas_call | solution.py:222
  19.3 4.4 %shard_map.92 = (bf16[3,512,256]{2,1,0:T(8,128)(2,1)}, bf16[3,512,256]{2,1,0:T(8,128)(2,1)}, bf16[3,512,256]{2,1,0:T(8,128)(2,1)}) custom-call(s32[4]{0:T(128)} %get-tuple-element.228.at, bf16[1024,3584]{1,0:T(8,128)(2,1)} %w_gate.13, bf16[1024,3584]{1,0:T(8,128)(2,1)} %w_up.13, bf16[1024,3584]{1,0:T(8,128)(2,1)} %w_down.13, bf16[1024,3584]{1,0:T(8,128)(2,1)} %w_gate.13, ...), custom_call_target="tpu_custom_call" | custom-call | flops 1000 | bytes 1000 | tf_op jit(solution)/shard_map/pallas_call | solution.py:222
  24.6 14.4 %collective-permute-done.1.refs_2_ = bf16[3,512,256]{2,1,0:T(8,128)(2,1)S(1)} collective-permute-done((bf16[3,512,256]{2,1,0:T(8,128)(2,1)}, bf16[3,512,256]{2,1,0:T(8,128)(2,1)S(1)}, u32[]{:S(2)}, u32[]{:S(2)}) %collective-permute-start.1) | collective-permute-done | bytes 786464 | tf_op jit(solution)/shard_map/ppermute | solution.py:76
  39.0 1.5 collective-permute-start.3
  41.1 3.6 %shard_map.93 = (bf16[3,512,256]{2,1,0:T(8,128)(2,1)}, bf16[3,512,256]{2,1,0:T(8,128)(2,1)}, bf16[3,512,256]{2,1,0:T(8,128)(2,1)}) custom-call(s32[4]{0:T(128)} %get-tuple-element.227.at, bf16[1024,3584]{1,0:T(8,128)(2,1)} %w_gate.13, bf16[1024,3584]{1,0:T(8,128)(2,1)} %w_up.13, bf16[1024,3584]{1,0:T(8,128)(2,1)} %w_down.13, bf16[1024,3584]{1,0:T(8,128)(2,1)} %w_gate.13, ...), custom_call_target="tpu_custom_call" | custom-call | flops 1000 | bytes 1000 | tf_op jit(solution)/shard_map/pallas_call | solution.py:222
  44.7 8.8 %collective-permute-done.2.refs_3_ = bf16[3,512,256]{2,1,0:T(8,128)(2,1)S(1)} collective-permute-done((bf16[3,512,256]{2,1,0:T(8,128)(2,1)}, bf16[3,512,256]{2,1,0:T(8,128)(2,1)S(1)}, u32[]{:S(2)}, u32[]{:S(2)}) %collective-permute-start.2) | collective-permute-done | bytes 786464 | tf_op jit(solution)/shard_map/ppermute | solution.py:76
  53.6 2.0 collective-permute-start.5
  55.6 1.8 collective-permute-start.9
  58.0 14.7 %collective-permute-done.4.refs_2_ = bf16[3,512,256]{2,1,0:T(8,128)(2,1)S(1)} collective-permute-done((bf16[3,512,256]{2,1,0:T(8,128)(2,1)}, bf16[3,512,256]{2,1,0:T(8,128)(2,1)S(1)}, u32[]{:S(2)}, u32[]{:S(2)}) %collective-permute-start.4) | collective-permute-done | bytes 786464 | tf_op jit(solution)/shard_map/ppermute | solution.py:76
  72.8 3.6 %shard_map.94 = (bf16[3,512,256]{2,1,0:T(8,128)(2,1)}, bf16[3,512,256]{2,1,0:T(8,128)(2,1)}, bf16[3,512,256]{2,1,0:T(8,128)(2,1)}) custom-call(s32[4]{0:T(128)} %get-tuple-element.226.at, bf16[1024,3584]{1,0:T(8,128)(2,1)} %w_gate.13, bf16[1024,3584]{1,0:T(8,128)(2,1)} %w_up.13, bf16[1024,3584]{1,0:T(8,128)(2,1)} %w_down.13, bf16[1024,3584]{1,0:T(8,128)(2,1)} %w_gate.13, ...), custom_call_target="tpu_custom_call" | custom-call | flops 1000 | bytes 1000 | tf_op jit(solution)/shard_map/pallas_call | solution.py:222
  76.4 1.6 collective-permute-start.10
  78.5 3.6 %shard_map.95 = (bf16[3,512,256]{2,1,0:T(8,128)(2,1)}, bf16[3,512,256]{2,1,0:T(8,128)(2,1)}, bf16[3,512,256]{2,1,0:T(8,128)(2,1)}) custom-call(s32[4]{0:T(128)} %get-tuple-element.225.at, bf16[1024,3584]{1,0:T(8,128)(2,1)} %w_gate.13, bf16[1024,3584]{1,0:T(8,128)(2,1)} %w_up.13, bf16[1024,3584]{1,0:T(8,128)(2,1)} %w_down.13, bf16[1024,3584]{1,0:T(8,128)(2,1)} %w_gate.13, ...), custom_call_target="tpu_custom_call" | custom-call | flops 1000 | bytes 1000 | tf_op jit(solution)/shard_map/pallas_call | solution.py:222
  82.1 5.2 %collective-permute-done.6.refs_3_ = bf16[3,512,256]{2,1,0:T(8,128)(2,1)S(1)} collective-permute-done((bf16[3,512,256]{2,1,0:T(8,128)(2,1)}, bf16[3,512,256]{2,1,0:T(8,128)(2,1)S(1)}, u32[]{:S(2)}, u32[]{:S(2)}) %collective-permute-start.6) | collective-permute-done | bytes 786464 | tf_op jit(solution)/shard_map/ppermute | solution.py:76
  87.3 2.6 collective-permute-start.14
  90.0 1.5 collective-permute-start.12
  91.5 5.4 %collective-permute-done.10.refs_4_ = bf16[3,512,256]{2,1,0:T(8,128)(2,1)} collective-permute-done((bf16[3,512,256]{2,1,0:T(8,128)(2,1)S(1)}, bf16[3,512,256]{2,1,0:T(8,128)(2,1)}, u32[]{:S(2)}, u32[]{:S(2)}) %collective-permute-start.10) | collective-permute-done | bytes 786464 | tf_op jit(solution)/shard_map/ppermute | solution.py:84
  96.9 3.6 %shard_map.96 = (bf16[3,512,256]{2,1,0:T(8,128)(2,1)}, bf16[3,512,256]{2,1,0:T(8,128)(2,1)}, bf16[3,512,256]{2,1,0:T(8,128)(2,1)}) custom-call(s32[4]{0:T(128)} %get-tuple-element.224.at, bf16[1024,3584]{1,0:T(8,128)(2,1)} %w_gate.13, bf16[1024,3584]{1,0:T(8,128)(2,1)} %w_up.13, bf16[1024,3584]{1,0:T(8,128)(2,1)} %w_down.13, bf16[1024,3584]{1,0:T(8,128)(2,1)} %w_gate.13, ...), custom_call_target="tpu_custom_call" | custom-call | flops 1000 | bytes 1000 | tf_op jit(solution)/shard_map/pallas_call | solution.py:222
  100.5 6.1 %collective-permute-done.11.refs_2_ = bf16[3,512,256]{2,1,0:T(8,128)(2,1)} collective-permute-done((bf16[3,512,256]{2,1,0:T(8,128)(2,1)}, bf16[3,512,256]{2,1,0:T(8,128)(2,1)}, u32[]{:S(2)}, u32[]{:S(2)}) %collective-permute-start.11) | collective-permute-done | bytes 786464 | tf_op jit(solution)/shard_map/ppermute | solution.py:76
  106.6 1.5 collective-permute-start.18
  108.2 3.7 %shard_map.99 = (bf16[3,512,256]{2,1,0:T(8,128)(2,1)}, bf16[3,512,256]{2,1,0:T(8,128)(2,1)}, bf16[3,512,256]{2,1,0:T(8,128)(2,1)}) custom-call(s32[4]{0:T(128)} %get-tuple-element.215.at, bf16[1024,3584]{1,0:T(8,128)(2,1)} %w_gate.13, bf16[1024,3584]{1,0:T(8,128)(2,1)} %w_up.13, bf16[1024,3584]{1,0:T(8,128)(2,1)} %w_down.13, bf16[1024,3584]{1,0:T(8,128)(2,1)} %w_gate.13, ...), custom_call_target="tpu_custom_call" | custom-call | flops 1000 | bytes 1000 | tf_op jit(solution)/shard_map/pallas_call | solution.py:222
  112.0 1.1 copy-done.9
  113.1 10.0 %shard_map.98 = (f32[1024,192]{1,0:T(8,128)S(1)}, f32[1024,256]{1,0:T(8,128)}, f32[1024,256]{1,0:T(8,128)}) custom-call(s32[8]{0:T(128)S(1)} %stack.137.places, bf16[8,512,1024]{2,1,0:T(8,128)(2,1)} %bitcast.84, bf16[1024,3584]{1,0:T(8,128)(2,1)} %w_gate.13, bf16[1024,3584]{1,0:T(8,128)(2,1)} %w_up.13, ...), custom_call_target="tpu_custom_call", output_to_operand_aliasing={{0}: (11, {})} | custom-call | flops 1000 | bytes 1000 | tf_op jit(solution)/shard_map/pallas_call | solution.py:190
  124.2 6.4 %collective-permute-done.18.refs_4_ = bf16[3,512,256]{2,1,0:T(8,128)(2,1)} collective-permute-done((bf16[3,512,256]{2,1,0:T(8,128)(2,1)}, bf16[3,512,256]{2,1,0:T(8,128)(2,1)}, u32[]{:S(2)}, u32[]{:S(2)}) %collective-permute-start.18) | collective-permute-done | bytes 786464 | tf_op jit(solution)/shard_map/ppermute | solution.py:84
  130.7 1.1 copy-done.4
  131.8 9.9 %shard_map.100 = (f32[1024,192]{1,0:T(8,128)S(1)}, f32[1024,256]{1,0:T(8,128)}, f32[1024,256]{1,0:T(8,128)}) custom-call(s32[8]{0:T(128)S(1)} %stack.280.places, bf16[8,512,1024]{2,1,0:T(8,128)(2,1)} %bitcast.85, bf16[1024,3584]{1,0:T(8,128)(2,1)} %w_gate.13, bf16[1024,3584]{1,0:T(8,128)(2,1)} %w_up.13, ...), custom_call_target="tpu_custom_call", output_to_operand_aliasing={{0}: (11, {})} | custom-call | flops 1000 | bytes 1000 | tf_op jit(solution)/shard_map/pallas_call | solution.py:190
  141.7 2.3 collective-permute-done.20.refs_2_
  144.4 7.3 %shard_map.97 = f32[1024,128]{1,0:T(8,128)S(1)} custom-call(bf16[8,512,1024]{2,1,0:T(8,128)(2,1)} %bitcast.86, bf16[3,64,4096]{2,1,0:T(8,128)(2,1)S(1)} %bitcast.73), custom_call_target="tpu_custom_call" | custom-call | flops 1000 | bytes 1000 | tf_op jit(solution)/shard_map/pallas_call | solution.py:131
  151.8 4.5 %collective-permute-done.23.refs_3_ = bf16[3,512,256]{2,1,0:T(8,128)(2,1)} collective-permute-done((bf16[3,512,256]{2,1,0:T(8,128)(2,1)}, bf16[3,512,256]{2,1,0:T(8,128)(2,1)}, u32[]{:S(2)}, u32[]{:S(2)}) %collective-permute-start.23) | collective-permute-done | bytes 786464 | tf_op jit(solution)/shard_map/ppermute | solution.py:76
  156.3 3.0 collective-permute-start.24
  160.1 4.5 %collective-permute-done.21.refs_4_ = bf16[3,512,256]{2,1,0:T(8,128)(2,1)S(1)} collective-permute-done((bf16[3,512,256]{2,1,0:T(8,128)(2,1)}, bf16[3,512,256]{2,1,0:T(8,128)(2,1)S(1)}, u32[]{:S(2)}, u32[]{:S(2)}) %collective-permute-start.21) | collective-permute-done | bytes 786464 | tf_op jit(solution)/shard_map/ppermute | solution.py:84
  165.7 10.2 %shard_map.101 = (f32[1024,192]{1,0:T(8,128)S(1)}, f32[1024,256]{1,0:T(8,128)}, f32[1024,256]{1,0:T(8,128)}) custom-call(s32[8]{0:T(128)S(1)} %stack.136.places, bf16[8,512,1024]{2,1,0:T(8,128)(2,1)} %bitcast.87, bf16[1024,3584]{1,0:T(8,128)(2,1)} %w_gate.13, bf16[1024,3584]{1,0:T(8,128)(2,1)} %w_up.13, ...), custom_call_target="tpu_custom_call", output_to_operand_aliasing={{0}: (11, {})} | custom-call | flops 1000 | bytes 1000 | tf_op jit(solution)/shard_map/pallas_call | solution.py:190
  177.0 1.1 collective-permute-start.32
  178.2 1.1 copy-done.7
  179.3 1.1 copy-done.10
  180.5 7.9 %shard_map.102.refs_7_ = f32[1024,192]{1,0:T(8,128)S(1)} custom-call(s32[8]{0:T(128)S(1)} %stack.137.places, bf16[8,512,1024]{2,1,0:T(8,128)(2,1)} %bitcast.76, bf16[1024,3584]{1,0:T(8,128)(2,1)} %w_down.13, bf16[3,512,256]{2,1,0:T(8,128)(2,1)} %collective-permute-done.7.refs_0_, ...), custom_call_target="tpu_custom_call", output_to_operand_aliasing={{}: (12, {})} | custom-call | flops 1000 | bytes 1000 | tf_op jit(solution)/shard_map/pallas_call | solution.py:190
  188.4 1.6 collective-permute-done.27.refs_3_
  190.0 3.0 collective-permute-start.30
  193.8 13.5 %shard_map.103.refs_9_ = f32[1024,192]{1,0:T(8,128)S(1)} custom-call(s32[8]{0:T(128)S(1)} %stack.282.places, bf16[8,512,1024]{2,1,0:T(8,128)(2,1)} %bitcast.88, bf16[8,512,1024]{2,1,0:T(8,128)(2,1)} %bitcast.77, bf16[1024,3584]{1,0:T(8,128)(2,1)} %w_gate.13, bf16[1024,3584]{1,0:T(8,128)(2,1)} %w_up.13, ...), custom_call_target="tpu_custom_call", output_to_operand_aliasing={{}: (13, {})} | custom-call | flops 1000 | bytes 1000 | tf_op jit(solution)/shard_map/pallas_call | solution.py:190
  207.5 1.4 collective-permute-start.34
  208.9 8.1 %shard_map.104.refs_9_ = f32[1024,192]{1,0:T(8,128)S(1)} custom-call(s32[8]{0:T(128)S(1)} %stack.280.places, bf16[8,512,1024]{2,1,0:T(8,128)(2,1)} %bitcast.78, bf16[1024,3584]{1,0:T(8,128)(2,1)} %w_down.13, bf16[3,512,256]{2,1,0:T(8,128)(2,1)} %collective-permute-done.14.refs_0_, ...), custom_call_target="tpu_custom_call", output_to_operand_aliasing={{}: (12, {})} | custom-call | flops 1000 | bytes 1000 | tf_op jit(solution)/shard_map/pallas_call | solution.py:190
  217.0 8.1 %shard_map.105.refs_7_ = f32[1024,192]{1,0:T(8,128)S(1)} custom-call(s32[8]{0:T(128)S(1)} %stack.136.places, bf16[8,512,1024]{2,1,0:T(8,128)(2,1)} %bitcast.79, bf16[1024,3584]{1,0:T(8,128)(2,1)} %w_down.13, bf16[3,512,256]{2,1,0:T(8,128)(2,1)} %collective-permute-done.16.refs_0_, ...), custom_call_target="tpu_custom_call", output_to_operand_aliasing={{}: (12, {})} | custom-call | flops 1000 | bytes 1000 | tf_op jit(solution)/shard_map/pallas_call | solution.py:190
  226.0 1.7 collective-permute-start.39
  229.5 1.7 collective-permute-done.34.refs_4_
  232.1 1.5 collective-permute-start.37
  234.5 1.1 copy-done.16
  235.6 1.1 copy-done.18
  236.7 1.1 copy-done.20
  237.9 13.0 %shard_map.106.refs_7_ = f32[1024,192]{1,0:T(8,128)S(1)} custom-call(s32[8]{0:T(128)S(1)} %stack.283.places, bf16[8,512,1024]{2,1,0:T(8,128)(2,1)} %bitcast.89, bf16[8,512,1024]{2,1,0:T(8,128)(2,1)} %bitcast.80, bf16[1024,3584]{1,0:T(8,128)(2,1)} %w_gate.13, bf16[1024,3584]{1,0:T(8,128)(2,1)} %w_up.13, ...), custom_call_target="tpu_custom_call", output_to_operand_aliasing={{}: (13, {})} | custom-call | flops 1000 | bytes 1000 | tf_op jit(solution)/shard_map/pallas_call | solution.py:190
  251.5 1.7 collective-permute-start.40
  253.3 8.5 %collective-permute-done.38.refs_3_ = bf16[3,512,256]{2,1,0:T(8,128)(2,1)} collective-permute-done((bf16[3,512,256]{2,1,0:T(8,128)(2,1)}, bf16[3,512,256]{2,1,0:T(8,128)(2,1)}, u32[]{:S(2)}, u32[]{:S(2)}) %collective-permute-start.38) | collective-permute-done | bytes 786464 | tf_op jit(solution)/shard_map/ppermute | solution.py:76
  262.6 1.1 copy-done.14
  263.7 13.5 %shard_map.107.refs_7_ = f32[1024,192]{1,0:T(8,128)S(1)} custom-call(s32[8]{0:T(128)S(1)} %stack.281.places, bf16[8,512,1024]{2,1,0:T(8,128)(2,1)} %bitcast.90, bf16[8,512,1024]{2,1,0:T(8,128)(2,1)} %bitcast.81, bf16[1024,3584]{1,0:T(8,128)(2,1)} %w_gate.13, bf16[1024,3584]{1,0:T(8,128)(2,1)} %w_up.13, ...), custom_call_target="tpu_custom_call", output_to_operand_aliasing={{}: (13, {})} | custom-call | flops 1000 | bytes 1000 | tf_op jit(solution)/shard_map/pallas_call | solution.py:190
  278.3 5.5 %shard_map.108 = f32[1024,64]{1,0:T(8,128)S(1)} custom-call(bf16[8,512,1024]{2,1,0:T(8,128)(2,1)} %bitcast.82, bf16[3,64,4096]{2,1,0:T(8,128)(2,1)S(1)} %bitcast.74), custom_call_target="tpu_custom_call" | custom-call | flops 1000 | bytes 1000 | tf_op jit(solution)/shard_map/pallas_call | solution.py:131
  283.8 4.2 %collective-permute-done.43.refs_5_ = bf16[3,512,256]{2,1,0:T(8,128)(2,1)} collective-permute-done((bf16[3,512,256]{2,1,0:T(8,128)(2,1)}, bf16[3,512,256]{2,1,0:T(8,128)(2,1)}, u32[]{:S(2)}, u32[]{:S(2)}) %collective-permute-start.43) | collective-permute-done | bytes 786464 | tf_op jit(solution)/shard_map/ppermute | solution.py:84
  288.0 14.0 %shard_map.109 = f32[1024,192]{1,0:T(8,128)S(1)} custom-call(s32[8]{0:T(128)S(1)} %stack.135.places, bf16[8,512,1024]{2,1,0:T(8,128)(2,1)} %bitcast.91, bf16[8,512,1024]{2,1,0:T(8,128)(2,1)} %bitcast.83, bf16[1024,3584]{1,0:T(8,128)(2,1)} %w_gate.13, bf16[1024,3584]{1,0:T(8,128)(2,1)} %w_up.13, ...), custom_call_target="tpu_custom_call", output_to_operand_aliasing={{}: (13, {})} | custom-call | flops 1000 | bytes 1000 | tf_op jit(solution)/shard_map/pallas_call | solution.py:190
  305.7 1.3 collective-permute-done.44
  307.1 1.6 collective-permute-start.45
  308.8 3.2 collective-permute-done.45
  312.0 2.7 collective-permute-start.46
  314.7 1.1 pad_maximum_fusion
  315.8 3.3 %collective-permute-done.46 = f32[2,12288]{1,0:T(2,128)S(1)} collective-permute-done((f32[2,12288]{1,0:T(2,128)S(1)}, f32[2,12288]{1,0:T(2,128)S(1)}, u32[]{:S(2)}, u32[]{:S(2)}) %collective-permute-start.46) | collective-permute-done | bytes 98336 | tf_op jit(solution)/shard_map/ppermute | solution.py:80
  319.1 1.8 fusion.1
  (134 shorter events, 23.8 us)
Async XLA Ops:
  6.5 105.4 %all-gather.5.cloned.1.call-start = ((), (), s32[]{:S(2)}) async-start(), calls=%async_computation | async-start | bytes 9437184 | tf_op jit(solution)/shard_map/all_gather | solution.py:284
  7.3 170.9 %all-gather.7.cloned.1.call-start = ((), (), s32[]{:S(2)}) async-start(), calls=%async_computation.1 | async-start | bytes 9437184 | tf_op jit(solution)/shard_map/all_gather | solution.py:285
  10.4 13.3 %collective-permute-start = (bf16[8,12288]{1,0:T(8,128)(2,1)}, bf16[8,12288]{1,0:T(8,128)(2,1)S(1)}, u32[]{:S(2)}, u32[]{:S(2)}) collective-permute-start(bf16[8,12288]{1,0:T(8,128)(2,1)} %param.17), channel_id=1, source_target_pairs={{0,8},{4,12},{8,0},{12,4},{1,9},{5,13},{9,1},{13,5},{2,10},{6,14},... | collective-permute-start | bytes 589832 | tf_op jit(solution)/shard_map/ppermute | solution.py:76
  18.4 20.7 %collective-permute-start.1 = (bf16[3,512,256]{2,1,0:T(8,128)(2,1)}, bf16[3,512,256]{2,1,0:T(8,128)(2,1)S(1)}, u32[]{:S(2)}, u32[]{:S(2)}) collective-permute-start(bf16[3,512,256]{2,1,0:T(8,128)(2,1)} %get-tuple-element.110), channel_id=1, source_target_pairs={{0,8},{4,12},{8,0},{12,4},{1,9},{5,13},{9,1},{13,5},{2,10},{6,14},... | collective-permute-start | bytes 2359304 | tf_op jit(solution)/shard_map/ppermute | solution.py:76
  18.4 35.1 %collective-permute-start.2 = (bf16[3,512,256]{2,1,0:T(8,128)(2,1)}, bf16[3,512,256]{2,1,0:T(8,128)(2,1)S(1)}, u32[]{:S(2)}, u32[]{:S(2)}) collective-permute-start(bf16[3,512,256]{2,1,0:T(8,128)(2,1)} %get-tuple-element.134), channel_id=1, source_target_pairs={{0,12},{4,8},{8,4},{12,0},{1,13},{5,9},{9,5},{13,1},{2,14},{6,10},... | collective-permute-start | bytes 2359304 | tf_op jit(solution)/shard_map/ppermute | solution.py:76
  19.3 4.4 %copy-start.22 = (bf16[8,12288]{1,0:T(8,128)(2,1)S(1)}, bf16[8,12288]{1,0:T(8,128)(2,1)}, u32[]{:S(2)}) copy-start(bf16[8,12288]{1,0:T(8,128)(2,1)} %param.17) | copy-start | bytes 589828
  39.0 72.9 %copy-start.6 = (bf16[3,512,256]{2,1,0:T(8,128)(2,1)}, bf16[3,512,256]{2,1,0:T(8,128)(2,1)S(1)}, u32[]{:S(2)}) copy-start(bf16[3,512,256]{2,1,0:T(8,128)(2,1)S(1)} %collective-permute-done.1.refs_2_) | copy-start | bytes 2359300
  39.0 18.5 %collective-permute-start.3 = (bf16[3,512,256]{2,1,0:T(8,128)(2,1)S(1)}, bf16[3,512,256]{2,1,0:T(8,128)(2,1)}, u32[]{:S(2)}, u32[]{:S(2)}) collective-permute-start(bf16[3,512,256]{2,1,0:T(8,128)(2,1)S(1)} %collective-permute-done.1.refs_2_), channel_id=1, source_target_pairs={{0,16},{16,0},{1,17},{17,1},{2,18},{18,2},{3,19},{19,3},{4,20},{20... | collective-permute-start | bytes 2359304 | tf_op jit(solution)/shard_map/ppermute | solution.py:84
  40.6 32.2 %collective-permute-start.4 = (bf16[3,512,256]{2,1,0:T(8,128)(2,1)}, bf16[3,512,256]{2,1,0:T(8,128)(2,1)S(1)}, u32[]{:S(2)}, u32[]{:S(2)}) collective-permute-start(bf16[3,512,256]{2,1,0:T(8,128)(2,1)} %get-tuple-element.124), channel_id=1, source_target_pairs={{0,8},{4,12},{8,0},{12,4},{1,9},{5,13},{9,1},{13,5},{2,10},{6,14},... | collective-permute-start | bytes 2359304 | tf_op jit(solution)/shard_map/ppermute | solution.py:76
  53.5 22.8 %copy-start.8 = (bf16[3,512,256]{2,1,0:T(8,128)(2,1)}, bf16[3,512,256]{2,1,0:T(8,128)(2,1)S(1)}, u32[]{:S(2)}) copy-start(bf16[3,512,256]{2,1,0:T(8,128)(2,1)S(1)} %collective-permute-done.2.refs_3_) | copy-start | bytes 2359300
  53.6 24.4 %collective-permute-start.5 = (bf16[3,512,256]{2,1,0:T(8,128)(2,1)S(1)}, bf16[3,512,256]{2,1,0:T(8,128)(2,1)}, u32[]{:S(2)}, u32[]{:S(2)}) collective-permute-start(bf16[3,512,256]{2,1,0:T(8,128)(2,1)S(1)} %collective-permute-done.2.refs_3_), channel_id=1, source_target_pairs={{0,16},{16,0},{1,17},{17,1},{2,18},{18,2},{3,19},{19,3},{4,20},{20... | collective-permute-start | bytes 2359304 | tf_op jit(solution)/shard_map/ppermute | solution.py:84
  55.6 20.8 %collective-permute-start.9 = (bf16[2,8,12288]{2,1,0:T(8,128)(2,1)}, bf16[2,8,12288]{2,1,0:T(8,128)(2,1)}, u32[]{:S(2)}, u32[]{:S(2)}) collective-permute-start(bf16[2,8,12288]{2,1,0:T(8,128)(2,1)} %get-tuple-element.137), channel_id=1, source_target_pairs={{0,4},{4,0},{8,12},{12,8},{1,5},{5,1},{9,13},{13,9},{2,6},{6,2},{1... | collective-permute-start | bytes 1179656 | tf_op jit(solution)/shard_map/ppermute | solution.py:76
  57.4 29.9 %collective-permute-start.6 = (bf16[3,512,256]{2,1,0:T(8,128)(2,1)}, bf16[3,512,256]{2,1,0:T(8,128)(2,1)S(1)}, u32[]{:S(2)}, u32[]{:S(2)}) collective-permute-start(bf16[3,512,256]{2,1,0:T(8,128)(2,1)} %get-tuple-element.158), channel_id=1, source_target_pairs={{0,12},{4,8},{8,4},{12,0},{1,13},{5,9},{9,5},{13,1},{2,14},{6,10},... | collective-permute-start | bytes 2359304 | tf_op jit(solution)/shard_map/ppermute | solution.py:76
  57.5 29.7 %collective-permute-start.7 = (bf16[3,512,256]{2,1,0:T(8,128)(2,1)}, bf16[3,512,256]{2,1,0:T(8,128)(2,1)}, u32[]{:S(2)}, u32[]{:S(2)}) collective-permute-start(bf16[3,512,256]{2,1,0:T(8,128)(2,1)} %get-tuple-element.134), channel_id=1, source_target_pairs={{0,4},{4,0},{8,12},{12,8},{1,5},{5,1},{9,13},{13,9},{2,6},{6,2},{1... | collective-permute-start | bytes 2359304 | tf_op jit(solution)/shard_map/ppermute | solution.py:76
  72.8 57.9 %copy-start.1 = (bf16[3,512,256]{2,1,0:T(8,128)(2,1)}, bf16[3,512,256]{2,1,0:T(8,128)(2,1)S(1)}, u32[]{:S(2)}) copy-start(bf16[3,512,256]{2,1,0:T(8,128)(2,1)S(1)} %collective-permute-done.4.refs_2_) | copy-start | bytes 2359300
  72.8 14.5 %collective-permute-start.8 = (bf16[3,512,256]{2,1,0:T(8,128)(2,1)}, bf16[3,512,256]{2,1,0:T(8,128)(2,1)}, u32[]{:S(2)}, u32[]{:S(2)}) collective-permute-start(bf16[3,512,256]{2,1,0:T(8,128)(2,1)} %get-tuple-element.136), channel_id=1, source_target_pairs={{0,4},{4,0},{8,12},{12,8},{1,5},{5,1},{9,13},{13,9},{2,6},{6,2},{1... | collective-permute-start | bytes 2359304 | tf_op jit(solution)/shard_map/ppermute | solution.py:76
  76.4 20.5 %collective-permute-start.10 = (bf16[3,512,256]{2,1,0:T(8,128)(2,1)S(1)}, bf16[3,512,256]{2,1,0:T(8,128)(2,1)}, u32[]{:S(2)}, u32[]{:S(2)}) collective-permute-start(bf16[3,512,256]{2,1,0:T(8,128)(2,1)S(1)} %collective-permute-done.4.refs_2_), channel_id=1, source_target_pairs={{0,16},{16,0},{1,17},{17,1},{2,18},{18,2},{3,19},{19,3},{4,20},{20... | collective-permute-start | bytes 2359304 | tf_op jit(solution)/shard_map/ppermute | solution.py:84
  78.0 28.6 %collective-permute-start.11 = (bf16[3,512,256]{2,1,0:T(8,128)(2,1)}, bf16[3,512,256]{2,1,0:T(8,128)(2,1)}, u32[]{:S(2)}, u32[]{:S(2)}) collective-permute-start(bf16[3,512,256]{2,1,0:T(8,128)(2,1)} %get-tuple-element.146), channel_id=1, source_target_pairs={{0,8},{4,12},{8,0},{12,4},{1,9},{5,13},{9,1},{13,5},{2,10},{6,14},... | collective-permute-start | bytes 2359304 | tf_op jit(solution)/shard_map/ppermute | solution.py:76
  87.3 13.2 %copy-start.3 = (bf16[3,512,256]{2,1,0:T(8,128)(2,1)}, bf16[3,512,256]{2,1,0:T(8,128)(2,1)S(1)}, u32[]{:S(2)}) copy-start(bf16[3,512,256]{2,1,0:T(8,128)(2,1)S(1)} %collective-permute-done.6.refs_3_) | copy-start | bytes 2359300
  87.3 35.9 %collective-permute-start.14 = (bf16[3,512,256]{2,1,0:T(8,128)(2,1)}, bf16[3,512,256]{2,1,0:T(8,128)(2,1)}, u32[]{:S(2)}, u32[]{:S(2)}) collective-permute-start(bf16[3,512,256]{2,1,0:T(8,128)(2,1)} %get-tuple-element.158), channel_id=1, source_target_pairs={{0,4},{4,0},{8,12},{12,8},{1,5},{5,1},{9,13},{13,9},{2,6},{6,2},{1... | collective-permute-start | bytes 2359304 | tf_op jit(solution)/shard_map/ppermute | solution.py:76
  89.9 33.7 %collective-permute-start.15 = (bf16[3,512,256]{2,1,0:T(8,128)(2,1)}, bf16[3,512,256]{2,1,0:T(8,128)(2,1)}, u32[]{:S(2)}, u32[]{:S(2)}) collective-permute-start(bf16[3,512,256]{2,1,0:T(8,128)(2,1)} %get-tuple-element.159), channel_id=1, source_target_pairs={{0,4},{4,0},{8,12},{12,8},{1,5},{5,1},{9,13},{13,9},{2,6},{6,2},{1... | collective-permute-start | bytes 2359304 | tf_op jit(solution)/shard_map/ppermute | solution.py:76
  90.0 33.6 %collective-permute-start.12 = (bf16[3,512,256]{2,1,0:T(8,128)(2,1)S(1)}, bf16[3,512,256]{2,1,0:T(8,128)(2,1)}, u32[]{:S(2)}, u32[]{:S(2)}) collective-permute-start(bf16[3,512,256]{2,1,0:T(8,128)(2,1)S(1)} %collective-permute-done.6.refs_3_), channel_id=1, source_target_pairs={{0,16},{16,0},{1,17},{17,1},{2,18},{18,2},{3,19},{19,3},{4,20},{20... | collective-permute-start | bytes 2359304 | tf_op jit(solution)/shard_map/ppermute | solution.py:84
  96.9 26.7 %collective-permute-start.13 = (bf16[3,512,256]{2,1,0:T(8,128)(2,1)}, bf16[3,512,256]{2,1,0:T(8,128)(2,1)}, u32[]{:S(2)}, u32[]{:S(2)}) collective-permute-start(bf16[3,512,256]{2,1,0:T(8,128)(2,1)} %get-tuple-element.167), channel_id=1, source_target_pairs={{0,12},{4,8},{8,4},{12,0},{1,13},{5,9},{9,5},{13,1},{2,14},{6,10},... | collective-permute-start | bytes 2359304 | tf_op jit(solution)/shard_map/ppermute | solution.py:76
  106.6 24.0 %collective-permute-start.18 = (bf16[3,512,256]{2,1,0:T(8,128)(2,1)}, bf16[3,512,256]{2,1,0:T(8,128)(2,1)}, u32[]{:S(2)}, u32[]{:S(2)}) collective-permute-start(bf16[3,512,256]{2,1,0:T(8,128)(2,1)} %collective-permute-done.11.refs_2_), channel_id=1, source_target_pairs={{0,16},{16,0},{1,17},{17,1},{2,18},{18,2},{3,19},{19,3},{4,20},{20... | collective-permute-start | bytes 2359304 | tf_op jit(solution)/shard_map/ppermute | solution.py:84
  123.1 20.9 %collective-permute-start.20 = (bf16[3,512,256]{2,1,0:T(8,128)(2,1)}, bf16[3,512,256]{2,1,0:T(8,128)(2,1)}, u32[]{:S(2)}, u32[]{:S(2)}) collective-permute-start(bf16[3,512,256]{2,1,0:T(8,128)(2,1)} %get-tuple-element.173), channel_id=1, source_target_pairs={{0,8},{4,12},{8,0},{12,4},{1,9},{5,13},{9,1},{13,5},{2,10},{6,14},... | collective-permute-start | bytes 2359304 | tf_op jit(solution)/shard_map/ppermute | solution.py:76
  123.6 28.0 %collective-permute-start.16 = (bf16[3,512,256]{2,1,0:T(8,128)(2,1)}, bf16[3,512,256]{2,1,0:T(8,128)(2,1)}, u32[]{:S(2)}, u32[]{:S(2)}) collective-permute-start(bf16[3,512,256]{2,1,0:T(8,128)(2,1)} %get-tuple-element.167), channel_id=1, source_target_pairs={{0,4},{4,0},{8,12},{12,8},{1,5},{5,1},{9,13},{13,9},{2,6},{6,2},{1... | collective-permute-start | bytes 2359304 | tf_op jit(solution)/shard_map/ppermute | solution.py:76
  123.7 28.1 %collective-permute-start.17 = (bf16[3,512,256]{2,1,0:T(8,128)(2,1)}, bf16[3,512,256]{2,1,0:T(8,128)(2,1)}, u32[]{:S(2)}, u32[]{:S(2)}) collective-permute-start(bf16[3,512,256]{2,1,0:T(8,128)(2,1)} %get-tuple-element.168), channel_id=1, source_target_pairs={{0,4},{4,0},{8,12},{12,8},{1,5},{5,1},{9,13},{13,9},{2,6},{6,2},{1... | collective-permute-start | bytes 2359304 | tf_op jit(solution)/shard_map/ppermute | solution.py:76
  124.2 27.6 %collective-permute-start.19 = (bf16[3,512,256]{2,1,0:T(8,128)(2,1)}, bf16[3,512,256]{2,1,0:T(8,128)(2,1)}, u32[]{:S(2)}, u32[]{:S(2)}) collective-permute-start(bf16[3,512,256]{2,1,0:T(8,128)(2,1)} %collective-permute-done.13.refs_3_), channel_id=1, source_target_pairs={{0,16},{16,0},{1,17},{17,1},{2,18},{18,2},{3,19},{19,3},{4,20},{20... | collective-permute-start | bytes 2359304 | tf_op jit(solution)/shard_map/ppermute | solution.py:84
  130.6 25.7 %collective-permute-start.23 = (bf16[3,512,256]{2,1,0:T(8,128)(2,1)}, bf16[3,512,256]{2,1,0:T(8,128)(2,1)}, u32[]{:S(2)}, u32[]{:S(2)}) collective-permute-start(bf16[3,512,256]{2,1,0:T(8,128)(2,1)} %get-tuple-element.185), channel_id=1, source_target_pairs={{0,12},{4,8},{8,4},{12,0},{1,13},{5,9},{9,5},{13,1},{2,14},{6,10},... | collective-permute-start | bytes 2359304 | tf_op jit(solution)/shard_map/ppermute | solution.py:76
  130.7 1.1 copy-start.4
  131.8 12.5 %copy-start = (bf16[3,4096,64]{1,2,0:T(8,128)(2,1)S(1)}, bf16[3,4096,64]{1,2,0:T(8,128)(2,1)}, u32[]{:S(2)}) copy-start(bf16[3,4096,64]{1,2,0:T(8,128)(2,1)} %param.15) | copy-start | bytes 4718596
  144.0 20.7 %collective-permute-start.21 = (bf16[3,512,256]{2,1,0:T(8,128)(2,1)}, bf16[3,512,256]{2,1,0:T(8,128)(2,1)S(1)}, u32[]{:S(2)}, u32[]{:S(2)}) collective-permute-start(bf16[3,512,256]{2,1,0:T(8,128)(2,1)} %collective-permute-done.20.refs_2_), channel_id=1, source_target_pairs={{0,16},{16,0},{1,17},{17,1},{2,18},{18,2},{3,19},{19,3},{4,20},{20... | collective-permute-start | bytes 2359304 | tf_op jit(solution)/shard_map/ppermute | solution.py:84
  151.7 24.4 %collective-permute-start.22 = (bf16[3,512,256]{2,1,0:T(8,128)(2,1)}, bf16[3,512,256]{2,1,0:T(8,128)(2,1)}, u32[]{:S(2)}, u32[]{:S(2)}) collective-permute-start(bf16[3,512,256]{2,1,0:T(8,128)(2,1)} %get-tuple-element.176), channel_id=1, source_target_pairs={{0,8},{4,12},{8,0},{12,4},{1,9},{5,13},{9,1},{13,5},{2,10},{6,14},... | collective-permute-start | bytes 2359304 | tf_op jit(solution)/shard_map/ppermute | solution.py:76
  156.3 20.7 %collective-permute-start.24 = (bf16[3,512,256]{2,1,0:T(8,128)(2,1)}, bf16[3,512,256]{2,1,0:T(8,128)(2,1)}, u32[]{:S(2)}, u32[]{:S(2)}) collective-permute-start(bf16[3,512,256]{2,1,0:T(8,128)(2,1)} %get-tuple-element.185), channel_id=1, source_target_pairs={{0,4},{4,0},{8,12},{12,8},{1,5},{5,1},{9,13},{13,9},{2,6},{6,2},{1... | collective-permute-start | bytes 2359304 | tf_op jit(solution)/shard_map/ppermute | solution.py:76
  159.3 29.1 %collective-permute-start.25 = (bf16[3,512,256]{2,1,0:T(8,128)(2,1)}, bf16[3,512,256]{2,1,0:T(8,128)(2,1)}, u32[]{:S(2)}, u32[]{:S(2)}) collective-permute-start(bf16[3,512,256]{2,1,0:T(8,128)(2,1)} %get-tuple-element.186), channel_id=1, source_target_pairs={{0,4},{4,0},{8,12},{12,8},{1,5},{5,1},{9,13},{13,9},{2,6},{6,2},{1... | collective-permute-start | bytes 2359304 | tf_op jit(solution)/shard_map/ppermute | solution.py:76
  159.3 29.1 %collective-permute-start.26 = (bf16[3,512,256]{2,1,0:T(8,128)(2,1)}, bf16[3,512,256]{2,1,0:T(8,128)(2,1)}, u32[]{:S(2)}, u32[]{:S(2)}) collective-permute-start(bf16[3,512,256]{2,1,0:T(8,128)(2,1)} %collective-permute-done.23.refs_3_), channel_id=1, source_target_pairs={{0,16},{16,0},{1,17},{17,1},{2,18},{18,2},{3,19},{19,3},{4,20},{20... | collective-permute-start | bytes 2359304 | tf_op jit(solution)/shard_map/ppermute | solution.py:84
  165.6 24.4 %collective-permute-start.27 = (bf16[3,512,256]{2,1,0:T(8,128)(2,1)}, bf16[3,512,256]{2,1,0:T(8,128)(2,1)}, u32[]{:S(2)}, u32[]{:S(2)}) collective-permute-start(bf16[3,512,256]{2,1,0:T(8,128)(2,1)} %get-tuple-element.194), channel_id=1, source_target_pairs={{0,12},{4,8},{8,4},{12,0},{1,13},{5,9},{9,5},{13,1},{2,14},{6,10},... | collective-permute-start | bytes 2359304 | tf_op jit(solution)/shard_map/ppermute | solution.py:76
  176.0 31.3 %collective-permute-start.33 = (bf16[3,512,256]{2,1,0:T(8,128)(2,1)}, bf16[3,512,256]{2,1,0:T(8,128)(2,1)}, u32[]{:S(2)}, u32[]{:S(2)}) collective-permute-start(bf16[3,512,256]{2,1,0:T(8,128)(2,1)} %collective-permute-done.22.refs_2_), channel_id=1, source_target_pairs={{0,16},{16,0},{1,17},{17,1},{2,18},{18,2},{3,19},{19,3},{4,20},{20... | collective-permute-start | bytes 2359304 | tf_op jit(solution)/shard_map/ppermute | solution.py:84
  177.0 30.5 %collective-permute-start.32 = (bf16[3,512,256]{2,1,0:T(8,128)(2,1)}, bf16[3,512,256]{2,1,0:T(8,128)(2,1)}, u32[]{:S(2)}, u32[]{:S(2)}) collective-permute-start(bf16[3,512,256]{2,1,0:T(8,128)(2,1)} %get-tuple-element.196), channel_id=1, source_target_pairs={{0,8},{4,12},{8,0},{12,4},{1,9},{5,13},{9,1},{13,5},{2,10},{6,14},... | collective-permute-start | bytes 2359304 | tf_op jit(solution)/shard_map/ppermute | solution.py:76
  178.2 1.1 copy-start.7
  180.5 12.6 %copy-start.24 = (bf16[3,512,256]{2,1,0:T(8,128)(2,1)S(1)}, bf16[3,512,256]{2,1,0:T(8,128)(2,1)}, u32[]{:S(2)}) copy-start(bf16[3,512,256]{2,1,0:T(8,128)(2,1)} %get-tuple-element.195) | copy-start | bytes 2359300
  180.5 13.4 %copy-start.12 = (bf16[3,512,256]{2,1,0:T(8,128)(2,1)S(1)}, bf16[3,512,256]{2,1,0:T(8,128)(2,1)}, u32[]{:S(2)}) copy-start(bf16[3,512,256]{2,1,0:T(8,128)(2,1)} %copy-done.11) | copy-start | bytes 2359300
  188.4 19.0 %copy-start.23 = (bf16[3,512,256]{2,1,0:T(8,128)(2,1)S(1)}, bf16[3,512,256]{2,1,0:T(8,128)(2,1)}, u32[]{:S(2)}) copy-start(bf16[3,512,256]{2,1,0:T(8,128)(2,1)} %get-tuple-element.201) | copy-start | bytes 2359300
  188.4 20.5 %copy-start.2 = (bf16[3,512,256]{2,1,0:T(8,128)(2,1)S(1)}, bf16[3,512,256]{2,1,0:T(8,128)(2,1)}, u32[]{:S(2)}) copy-start(bf16[3,512,256]{2,1,0:T(8,128)(2,1)} %copy-done.1) | copy-start | bytes 2359300
  188.4 20.5 %copy-start.5 = (bf16[3,512,256]{2,1,0:T(8,128)(2,1)S(1)}, bf16[3,512,256]{2,1,0:T(8,128)(2,1)}, u32[]{:S(2)}) copy-start(bf16[3,512,256]{2,1,0:T(8,128)(2,1)} %copy-done.3) | copy-start | bytes 2359300
  190.0 35.1 %collective-permute-start.30 = (bf16[3,512,256]{2,1,0:T(8,128)(2,1)}, bf16[3,512,256]{2,1,0:T(8,128)(2,1)S(1)}, u32[]{:S(2)}, u32[]{:S(2)}) collective-permute-start(bf16[3,512,256]{2,1,0:T(8,128)(2,1)} %get-tuple-element.194), channel_id=1, source_target_pairs={{0,4},{4,0},{8,12},{12,8},{1,5},{5,1},{9,13},{13,9},{2,6},{6,2},{1... | collective-permute-start | bytes 2359304 | tf_op jit(solution)/shard_map/ppermute | solution.py:76
  193.0 34.7 %collective-permute-start.31 = (bf16[3,512,256]{2,1,0:T(8,128)(2,1)S(1)}, bf16[3,512,256]{2,1,0:T(8,128)(2,1)S(1)}, u32[]{:S(2)}, u32[]{:S(2)}) collective-permute-start(bf16[3,512,256]{2,1,0:T(8,128)(2,1)S(1)} %copy-done.24), channel_id=1, source_target_pairs={{0,4},{4,0},{8,12},{12,8},{1,5},{5,1},{9,13},{13,9},{2,6},{6,2},{1... | collective-permute-start | bytes 2359304 | tf_op jit(solution)/shard_map/ppermute | solution.py:76
  193.0 35.6 %collective-permute-start.28 = (bf16[3,512,256]{2,1,0:T(8,128)(2,1)}, bf16[3,512,256]{2,1,0:T(8,128)(2,1)S(1)}, u32[]{:S(2)}, u32[]{:S(2)}) collective-permute-start(bf16[3,512,256]{2,1,0:T(8,128)(2,1)} %collective-permute-done.27.refs_3_), channel_id=1, source_target_pairs={{0,16},{16,0},{1,17},{17,1},{2,18},{18,2},{3,19},{19,3},{4,20},{20... | collective-permute-start | bytes 2359304 | tf_op jit(solution)/shard_map/ppermute | solution.py:84
  207.4 22.1 %collective-permute-start.29 = (bf16[3,512,256]{2,1,0:T(8,128)(2,1)S(1)}, bf16[3,512,256]{2,1,0:T(8,128)(2,1)}, u32[]{:S(2)}, u32[]{:S(2)}) collective-permute-start(bf16[3,512,256]{2,1,0:T(8,128)(2,1)S(1)} %copy-done.23), channel_id=1, source_target_pairs={{0,12},{4,8},{8,4},{12,0},{1,13},{5,9},{9,5},{13,1},{2,14},{6,10},... | collective-permute-start | bytes 2359304 | tf_op jit(solution)/shard_map/ppermute | solution.py:76
  207.5 23.8 %collective-permute-start.34 = (bf16[3,512,256]{2,1,0:T(8,128)(2,1)}, bf16[3,512,256]{2,1,0:T(8,128)(2,1)S(1)}, u32[]{:S(2)}, u32[]{:S(2)}) collective-permute-start(bf16[3,512,256]{2,1,0:T(8,128)(2,1)} %collective-permute-done.32.refs_2_), channel_id=1, source_target_pairs={{0,16},{16,0},{1,17},{17,1},{2,18},{18,2},{3,19},{19,3},{4,20},{20... | collective-permute-start | bytes 2359304 | tf_op jit(solution)/shard_map/ppermute | solution.py:84
  226.0 24.9 %collective-permute-start.39 = (bf16[3,512,256]{2,1,0:T(8,128)(2,1)}, bf16[3,512,256]{2,1,0:T(8,128)(2,1)}, u32[]{:S(2)}, u32[]{:S(2)}) collective-permute-start(bf16[3,512,256]{2,1,0:T(8,128)(2,1)} %get-tuple-element.205), channel_id=1, source_target_pairs={{0,8},{4,12},{8,0},{12,4},{1,9},{5,13},{9,1},{13,5},{2,10},{6,14},... | collective-permute-start | bytes 2359304 | tf_op jit(solution)/shard_map/ppermute | solution.py:76
  232.1 19.4 %collective-permute-start.37 = (bf16[3,512,256]{2,1,0:T(8,128)(2,1)}, bf16[3,512,256]{2,1,0:T(8,128)(2,1)}, u32[]{:S(2)}, u32[]{:S(2)}) collective-permute-start(bf16[3,512,256]{2,1,0:T(8,128)(2,1)} %collective-permute-done.29.refs_3_), channel_id=1, source_target_pairs={{0,16},{16,0},{1,17},{17,1},{2,18},{18,2},{3,19},{19,3},{4,20},{20... | collective-permute-start | bytes 2359304 | tf_op jit(solution)/shard_map/ppermute | solution.py:84
  233.7 28.8 %collective-permute-start.35 = (bf16[3,512,256]{2,1,0:T(8,128)(2,1)}, bf16[3,512,256]{2,1,0:T(8,128)(2,1)}, u32[]{:S(2)}, u32[]{:S(2)}) collective-permute-start(bf16[3,512,256]{2,1,0:T(8,128)(2,1)} %get-tuple-element.201), channel_id=1, source_target_pairs={{0,4},{4,0},{8,12},{12,8},{1,5},{5,1},{9,13},{13,9},{2,6},{6,2},{1... | collective-permute-start | bytes 2359304 | tf_op jit(solution)/shard_map/ppermute | solution.py:76
  233.8 28.8 %collective-permute-start.36 = (bf16[3,512,256]{2,1,0:T(8,128)(2,1)}, bf16[3,512,256]{2,1,0:T(8,128)(2,1)}, u32[]{:S(2)}, u32[]{:S(2)}) collective-permute-start(bf16[3,512,256]{2,1,0:T(8,128)(2,1)} %get-tuple-element.202), channel_id=1, source_target_pairs={{0,4},{4,0},{8,12},{12,8},{1,5},{5,1},{9,13},{13,9},{2,6},{6,2},{1... | collective-permute-start | bytes 2359304 | tf_op jit(solution)/shard_map/ppermute | solution.py:76
  234.3 27.6 %collective-permute-start.38 = (bf16[3,512,256]{2,1,0:T(8,128)(2,1)}, bf16[3,512,256]{2,1,0:T(8,128)(2,1)}, u32[]{:S(2)}, u32[]{:S(2)}) collective-permute-start(bf16[3,512,256]{2,1,0:T(8,128)(2,1)} %get-tuple-element.209), channel_id=1, source_target_pairs={{0,12},{4,8},{8,4},{12,0},{1,13},{5,9},{9,5},{13,1},{2,14},{6,10},... | collective-permute-start | bytes 2359304 | tf_op jit(solution)/shard_map/ppermute | solution.py:76
  251.5 25.8 %collective-permute-start.40 = (bf16[3,512,256]{2,1,0:T(8,128)(2,1)}, bf16[3,512,256]{2,1,0:T(8,128)(2,1)}, u32[]{:S(2)}, u32[]{:S(2)}) collective-permute-start(bf16[3,512,256]{2,1,0:T(8,128)(2,1)} %collective-permute-done.39.refs_2_), channel_id=1, source_target_pairs={{0,16},{16,0},{1,17},{17,1},{2,18},{18,2},{3,19},{19,3},{4,20},{20... | collective-permute-start | bytes 2359304 | tf_op jit(solution)/shard_map/ppermute | solution.py:84
  261.9 26.1 %collective-permute-start.43 = (bf16[3,512,256]{2,1,0:T(8,128)(2,1)}, bf16[3,512,256]{2,1,0:T(8,128)(2,1)}, u32[]{:S(2)}, u32[]{:S(2)}) collective-permute-start(bf16[3,512,256]{2,1,0:T(8,128)(2,1)} %collective-permute-done.38.refs_3_), channel_id=1, source_target_pairs={{0,16},{16,0},{1,17},{17,1},{2,18},{18,2},{3,19},{19,3},{4,20},{20... | collective-permute-start | bytes 2359304 | tf_op jit(solution)/shard_map/ppermute | solution.py:84
  262.6 1.1 copy-start.14
  277.3 10.8 %collective-permute-start.41 = (bf16[3,512,256]{2,1,0:T(8,128)(2,1)}, bf16[3,512,256]{2,1,0:T(8,128)(2,1)}, u32[]{:S(2)}, u32[]{:S(2)}) collective-permute-start(bf16[3,512,256]{2,1,0:T(8,128)(2,1)} %get-tuple-element.209), channel_id=1, source_target_pairs={{0,4},{4,0},{8,12},{12,8},{1,5},{5,1},{9,13},{13,9},{2,6},{6,2},{1... | collective-permute-start | bytes 2359304 | tf_op jit(solution)/shard_map/ppermute | solution.py:76
  277.9 10.1 %collective-permute-start.42 = (bf16[3,512,256]{2,1,0:T(8,128)(2,1)}, bf16[3,512,256]{2,1,0:T(8,128)(2,1)}, u32[]{:S(2)}, u32[]{:S(2)}) collective-permute-start(bf16[3,512,256]{2,1,0:T(8,128)(2,1)} %get-tuple-element.210), channel_id=1, source_target_pairs={{0,4},{4,0},{8,12},{12,8},{1,5},{5,1},{9,13},{13,9},{2,6},{6,2},{1... | collective-permute-start | bytes 2359304 | tf_op jit(solution)/shard_map/ppermute | solution.py:76
  302.0 12.7 %copy-start.21 = (bf16[1,2,8,12288]{3,2,1,0:T(8,128)(2,1)S(1)}, bf16[1,2,8,12288]{3,2,1,0:T(8,128)(2,1)}, u32[]{:S(2)}) copy-start(bf16[1,2,8,12288]{3,2,1,0:T(8,128)(2,1)} %get-tuple-element.222) | copy-start | bytes 1179652
  305.6 1.4 collective-permute-start.44
  307.1 4.9 %collective-permute-start.45 = (f32[2,12288]{1,0:T(2,128)S(1)}, f32[2,12288]{1,0:T(2,128)S(1)}, u32[]{:S(2)}, u32[]{:S(2)}) collective-permute-start(f32[2,12288]{1,0:T(2,128)S(1)} %bitcast_add_fusion), channel_id=1, source_target_pairs={{0,1},{1,0},{2,3},{3,2},{4,5},{5,4},{6,7},{7,6},{8,9},{9,8},{10,11... | collective-permute-start | bytes 294920 | tf_op jit(solution)/shard_map/ppermute | solution.py:80
  312.0 7.1 %collective-permute-start.46 = (f32[2,12288]{1,0:T(2,128)S(1)}, f32[2,12288]{1,0:T(2,128)S(1)}, u32[]{:S(2)}, u32[]{:S(2)}) collective-permute-start(f32[2,12288]{1,0:T(2,128)S(1)} %add.75), channel_id=1, source_target_pairs={{0,2},{1,3},{2,0},{3,1},{4,6},{5,7},{6,4},{7,5},{8,10},{9,11},{10,... | collective-permute-start | bytes 294920 | tf_op jit(solution)/shard_map/ppermute | solution.py:80
  (10 other events, 10.2 us)
Sparse Core Ops, SparseCore 0:
  9.0 84.7 all-gather.4
  95.3 81.0 all-gather.6

commit v4 on v3

--- a/solution.py
+++ b/solution.py
@@ -134,7 +134,7 @@
         grid=(tiles,),
         in_specs=[spec, pl.BlockSpec((count, rank, model), lambda i: (at // count, 0, 0))],
         out_specs=pl.BlockSpec((tile, count * rank), lambda i: (i, 0)),
-        compiler_params=pltpu.CompilerParams(vmem_limit_bytes=48 * 2**20),
+        compiler_params=pltpu.CompilerParams(vmem_limit_bytes=60 * 2**20),
         cost_estimate=pl.CostEstimate(flops=1000, bytes_accessed=1000, transcendentals=0),
     )(tokens, d_columns)
 
@@ -169,6 +169,88 @@
     grad_gate = (back_grad * gate_factor[...]).astype(jnp.bfloat16)
     grad_up = (back_grad * up_factor[...]).astype(jnp.bfloat16)
     add_projected(sums_in, sums_ref, (grad_gate, grad_up, None), ff_ref)
+
+
+def partial_kernel(places, acts_ref, grad_ref, w_gate, w_up, w_down, *refs):
+    *pieces, gate_out, up_out, back_out = refs
+    gate_out[...] = pre_activation(places, acts_ref, w_gate, planes(pieces, 0))
+    up_out[...] = pre_activation(places, acts_ref, w_up, planes(pieces, 1))
+    back_out[...] = pre_activation(places, grad_ref, w_down, planes(pieces, 2))
+
+
+def last_kernel(places, acts_ref, grad_ref, gate_in, up_in, back_in, piece, ff_ref, sums_in, sums_ref):
+    hidden, grad_gate, grad_up = activations(
+        gate_in[...] + dot(acts_ref[0], piece[0]),
+        up_in[...] + dot(acts_ref[0], piece[1]),
+        back_in[...] + dot(grad_ref[0], piece[2]),
+    )
+    add_projected(sums_in, sums_ref, (grad_gate, grad_up, hidden), ff_ref)
+
+
+def direct_backward_kernel(places, grad_ref, w_down, *refs):
+    *refs, d_ref, ff_ref, sums_in, sums_ref, out = refs
+    backward_kernel(places, grad_ref, w_down, *refs, ff_ref, sums_in, sums_ref)
+    direct_kernel(grad_ref, d_ref, out)
+
+
+def small_call(kernel, out_shape, grid, in_specs, out_specs, aliases, operands):
+    return pl.pallas_call(
+        kernel,
+        out_shape=out_shape,
+        grid_spec=pltpu.PrefetchScalarGridSpec(
+            num_scalar_prefetch=1, grid=grid, in_specs=in_specs, out_specs=out_specs
+        ),
+        input_output_aliases=aliases,
+        compiler_params=pltpu.CompilerParams(vmem_limit_bytes=60 * 2**20),
+        cost_estimate=pl.CostEstimate(flops=1000, bytes_accessed=1000, transcendentals=0),
+    )(*operands)
+
+
+def partial_hidden_units(places, tokens, weights, pieces):
+    tile = 256
+    token_spec, tiles = token_tiles(tokens[0], 2, tile)
+    depth, chunk = weights[0].shape[0], pieces[0].shape[2]
+    own = pl.BlockSpec((depth, chunk), lambda i, places: (0, places[0]))
+    whole = pl.BlockSpec(pieces[0].shape, lambda i, places: (0, 0, 0))
+    out = pl.BlockSpec((tile, chunk), lambda i, places: (i, 0))
+    return small_call(
+        partial_kernel,
+        [jax.ShapeDtypeStruct((tiles * tile, chunk), jnp.float32)] * 3,
+        (tiles,),
+        [token_spec] * 2 + [own] * 3 + [whole] * len(pieces),
+        [out] * 3,
+        {},
+        [places, *tokens, *weights, *pieces],
+    )
+
+
+def last_hidden_units(places, tokens, partial, piece, ff_columns, sums):
+    tile = 256
+    _, tiles = token_tiles(tokens[0], 2, tile)
+    per_near = tiles // 2
+    quarters, depth = tokens[0].shape[0] // 2, tokens[0].shape[2]
+    rows, chunk = piece.shape[1:]
+
+    def columns(i, places):
+        return (i // per_near) * quarters + places[1] // depth, i % per_near, lax.rem(places[1], depth) // rows
+
+    by_tile = lambda i, places: (i, 0)
+    total = pl.BlockSpec((tile, sums.shape[1]), by_tile)
+    return small_call(
+        last_kernel,
+        jax.ShapeDtypeStruct(sums.shape, sums.dtype),
+        (tiles,),
+        [pl.BlockSpec((1, tile, rows), columns)] * 2
+        + [pl.BlockSpec((tile, chunk), by_tile)] * 3
+        + [
+            pl.BlockSpec(piece.shape, lambda i, places: (0, 0, 0)),
+            pl.BlockSpec((3, ff_columns.shape[1], chunk), lambda i, places: (0, 0, places[0])),
+            total,
+        ],
+        total,
+        {8: 0},
+        [places, *tokens, *partial, piece, ff_columns, sums],
+    )
 
 
 def add_hidden_units(kernel, places, tokens, weights, pieces, factors, ff_proj, sums):
@@ -183,6 +265,9 @@
     factor = pl.BlockSpec((tile, chunk), by_tile)
     total = pl.BlockSpec((tile, sums.shape[1]), by_tile)
     out_shape, out_specs = [jax.ShapeDtypeStruct(sums.shape, sums.dtype)], [total]
+    if kernel is direct_backward_kernel:
+        out_shape += [jax.ShapeDtypeStruct((rows, ff_proj.shape[1]), jnp.float32)]
+        out_specs += [pl.BlockSpec((tile, ff_proj.shape[1]), by_tile)]
     if kernel is forward_kernel:
         out_shape += [jax.ShapeDtypeStruct((rows, chunk), jnp.float32)] * 2
         out_specs += [factor] * 2
@@ -196,12 +281,13 @@
             in_specs=[token_spec] * len(tokens)
             + [own] * len(weights)
             + [piece(*p) for p in pieces]
-            + [factor] * len(factors)
+            + [factor] * 2 * (len(factors) > 1)
+            + [pl.BlockSpec((1, *v.shape[1:]), lambda i, places: (2, 0, 0)) for v in factors[2:]]
             + [pl.BlockSpec((3, ff_proj.shape[1], chunk), lambda i, places: (0, 0, places[0])), total],
             out_specs=out_specs,
         ),
         input_output_aliases={len(operands): 0},
-        compiler_params=pltpu.CompilerParams(vmem_limit_bytes=48 * 2**20),
+        compiler_params=pltpu.CompilerParams(vmem_limit_bytes=60 * 2**20),
         cost_estimate=pl.CostEstimate(flops=1000, bytes_accessed=1000, transcendentals=0),
     )(places, *operands)
 
@@ -286,17 +372,23 @@
     sums = jnp.zeros((2 * tokens, 3 * rank), jnp.float32)
     ff_columns, d_columns = jnp.swapaxes(ff_proj, 1, 2), jnp.swapaxes(d_proj, 1, 2)
     far, relayed, near_rows, cuts = [], [], [], []
-    factors = [None] * chunks
-
-    def add(kernel, j, sums):
+    factors, rights = [None] * chunks, []
+
+    def places_of(j):
         starts = [near * chunks + j, me * depth]
         starts += [(me ^ 1) * depth + side * rows for side in (part, 1 - part)]
         starts += [(me ^ flip) * depth + side * rows for side in (part, 1 - part) for flip in (2, 3)]
-        places = jnp.stack([jnp.asarray(s, jnp.int32) for s in starts])
+        return jnp.stack([jnp.asarray(s, jnp.int32) for s in starts])
+
+    def add(kernel, j, sums):
+        places = places_of(j)
         sources = near_rows[j] + far[2 * j : 2 * j + 2] + relayed[2 * j : 2 * j + 2]
         run = lambda *args: add_hidden_units(kernel, places, *args, ff_columns, sums)
         if kernel is forward_kernel:
             sums, *factors[j] = run([full_acts], weights[:2], [(v, 2, 0) for v in sources], [])
+        elif kernel is direct_backward_kernel:
+            sums, right_down = run([full_grad], weights[2:], [(v, 1, 2) for v in sources], [*factors[j], d_columns])
+            rights.append(right_down)
         elif kernel is backward_kernel:
             (sums,) = run([full_grad], weights[2:], [(v, 1, 2) for v in sources], factors[j])
         else:
@@ -317,7 +409,7 @@
         5: [(forward_kernel, 0)],
         6: [(forward_kernel, 1)],
         8: [(forward_kernel, 2)],
-        9: [(backward_kernel, 0)],
+        9: [(direct_backward_kernel, 0)],
         10: [(both_kernel, 3)],
         11: [(backward_kernel, 1), (backward_kernel, 2)],
         12: [(both_kernel, 4)],
@@ -354,15 +446,18 @@
         if g == 8:
             full_grad = at(8, gathered_grad)
     sums = at(last, sums)
-    right_down = direct(after(full_grad, sums), d_columns, 2, 1)
-    sums = add(both_kernel, 6, after(sums, right_down))
+    places = places_of(chunks - 1)
+    both_tokens = [after(full_acts, sums), full_grad]
+    partial = partial_hidden_units(places, both_tokens, weights, near_rows[-1] + far[-2:] + relayed[-2:-1])
+    places = jnp.stack([places[0], places[-1]])
+    sums = last_hidden_units(places, [full_acts, full_grad], partial, relayed[-1], ff_columns, sums)
     right_gate, right_up, left_down = jnp.split(sums, 3, axis=1)
     left_gate, left_up = jnp.split(left_both, 2, axis=1)
     proj = jnp.stack(
         [
             outer_sum(left_gate, right_gate, length),
             outer_sum(left_up, right_up, length),
-            outer_sum(left_down, right_down, length),
+            outer_sum(left_down, rights[0], length),
         ],
         axis=1,
     ).reshape(2, seq_dev, 3 * rank * rank)

time: 330 us -> 326 us (0.988)
  Pallas kernels: 147 us -> 162 us
  waiting for transfers between devices: 97.8 us -> 89.6 us
  local copies, waits for them, and re-layouts: 14.9 us -> 8.61 us
  starting transfers between devices: 42.6 us -> 39.1 us
    pallas_call x0 -> x2, Pallas kernels: none -> 19.7 us  [small_call(): pl.pallas_call(kernel, out_shape=out_shape, grid_spec=pltpu.PrefetchScala...]
    unnamed x51 -> x45, local copies, waits for them, and re-layouts: 13.6 us -> 0.98 us
    ppermute x31, waiting for transfers between devices: 67.6 us -> 61.3 us  [permute_dp(): return lax.ppermute(value, DP, [(i, i ^ flip) for i in range(4)])]
    pallas_call x2 -> x1, Pallas kernels: 12.8 us -> 8.16 us  [direct(): pl.pallas_call(direct_kernel, out_shape=jax.ShapeDtypeStruct((tiles * til...]
    another operation x7, local copies, waits for them, and re-layouts: 0.59 us -> 4.41 us  [places_of(): return jnp.stack([jnp.asarray(s, jnp.int32) for s in starts])]
    pallas_call x10 -> x9, Pallas kernels: 108 us -> 108 us  [add_hidden_units(): pl.pallas_call(kernel, out_shape=out_shape, grid_spec=pltpu.PrefetchScala...]
  transfers between devices with their start and end apart: 49 -> 49, of which waited for: 19 -> 20; matrix products, arithmetic and copies ran while one was open for 2% -> 4% of each run, Pallas kernels for 41% -> 48%
where the time goes in v4:
time: 326 us; the launch traced here: 325 us
  Pallas kernels  162 us (50%)
  waiting for transfers between devices  89.6 us (27%)
  starting transfers between devices  39.1 us (12%)
  between operations  13.7 us (4%)
  local copies, waits for them, and re-layouts  8.61 us (3%)
  other arithmetic  6.07 us (2%)
  matrix products  5.65 us (2%)
    pallas_call x9, Pallas kernels, add_hidden_units(): pl.pallas_call(kernel, out_shape=out_shape, grid_spec=pltpu.PrefetchScala...  108 us
    ppermute x31, waiting for transfers between devices, permute_dp(): return lax.ppermute(value, DP, [(i, i ^ flip) for i in range(4)])  61.3 us
    pallas_call x7, Pallas kernels, cut(): pl.pallas_call(cut_kernel, out_shape=[jax.ShapeDtypeStruct((3, rows, chun...  25.8 us
    ppermute x14, waiting for transfers between devices, permute_parts(): return lax.ppermute(value, 'parts', [(0, 1), (1, 0)])  20 us
    ppermute x31, starting transfers between devices, permute_dp(): return lax.ppermute(value, DP, [(i, i ^ flip) for i in range(4)])  19.9 us
    pallas_call x2, Pallas kernels, small_call(): pl.pallas_call(kernel, out_shape=out_shape, grid_spec=pltpu.PrefetchScala...  19.7 us
    ppermute x14, starting transfers between devices, permute_parts(): return lax.ppermute(value, 'parts', [(0, 1), (1, 0)])  14.8 us
    pallas_call x1, Pallas kernels, direct(): pl.pallas_call(direct_kernel, out_shape=jax.ShapeDtypeStruct((tiles * til...  8.16 us
  transfers between devices with their start and end apart: 49, of which 20 were waited for; matrix products, arithmetic and copies ran while one was open for 4% of the time, Pallas kernels for 48%

profile of v4, /device:TPU:0, one launch (start us, length us, event | category | flops | bytes accessed | tf_op | source)
XLA Modules:
  0.0 325.0 jit_solution(4017893955255204306)
XLA Ops:
  8.0 2.3 broadcast_multiply_fusion
  10.4 3.0 collective-permute-start
  14.6 3.6 %shard_map.91 = (bf16[3,512,256]{2,1,0:T(8,128)(2,1)}, bf16[3,512,256]{2,1,0:T(8,128)(2,1)}, bf16[3,512,256]{2,1,0:T(8,128)(2,1)}) custom-call(s32[4]{0:T(128)} %get-tuple-element.237.at, bf16[1024,3584]{1,0:T(8,128)(2,1)} %w_gate.13, bf16[1024,3584]{1,0:T(8,128)(2,1)} %w_up.13, bf16[1024,3584]{1,0:T(8,128)(2,1)} %w_down.13, bf16[1024,3584]{1,0:T(8,128)(2,1)} %w_gate.13, ...), custom_call_target="tpu_custom_call" | custom-call | flops 1000 | bytes 1000 | tf_op jit(solution)/shard_map/pallas_call | solution.py:308
  18.2 0.8 collective-permute-start.2
  19.1 4.2 %shard_map.92 = (bf16[3,512,256]{2,1,0:T(8,128)(2,1)}, bf16[3,512,256]{2,1,0:T(8,128)(2,1)}, bf16[3,512,256]{2,1,0:T(8,128)(2,1)}) custom-call(s32[4]{0:T(128)} %get-tuple-element.236.at, bf16[1024,3584]{1,0:T(8,128)(2,1)} %w_gate.13, bf16[1024,3584]{1,0:T(8,128)(2,1)} %w_up.13, bf16[1024,3584]{1,0:T(8,128)(2,1)} %w_down.13, bf16[1024,3584]{1,0:T(8,128)(2,1)} %w_gate.13, ...), custom_call_target="tpu_custom_call" | custom-call | flops 1000 | bytes 1000 | tf_op jit(solution)/shard_map/pallas_call | solution.py:308
  23.3 0.9 fusion.8
  24.3 14.6 %collective-permute-done.1.refs_2_ = bf16[3,512,256]{2,1,0:T(8,128)(2,1)S(1)} collective-permute-done((bf16[3,512,256]{2,1,0:T(8,128)(2,1)}, bf16[3,512,256]{2,1,0:T(8,128)(2,1)S(1)}, u32[]{:S(2)}, u32[]{:S(2)}) %collective-permute-start.1) | collective-permute-done | bytes 786464 | tf_op jit(solution)/shard_map/ppermute | solution.py:76
  38.9 1.5 collective-permute-start.3
  40.9 3.7 %shard_map.93 = (bf16[3,512,256]{2,1,0:T(8,128)(2,1)}, bf16[3,512,256]{2,1,0:T(8,128)(2,1)}, bf16[3,512,256]{2,1,0:T(8,128)(2,1)}) custom-call(s32[4]{0:T(128)} %get-tuple-element.235.at, bf16[1024,3584]{1,0:T(8,128)(2,1)} %w_gate.13, bf16[1024,3584]{1,0:T(8,128)(2,1)} %w_up.13, bf16[1024,3584]{1,0:T(8,128)(2,1)} %w_down.13, bf16[1024,3584]{1,0:T(8,128)(2,1)} %w_gate.13, ...), custom_call_target="tpu_custom_call" | custom-call | flops 1000 | bytes 1000 | tf_op jit(solution)/shard_map/pallas_call | solution.py:308
  44.6 8.8 %collective-permute-done.2.refs_3_ = bf16[3,512,256]{2,1,0:T(8,128)(2,1)S(1)} collective-permute-done((bf16[3,512,256]{2,1,0:T(8,128)(2,1)}, bf16[3,512,256]{2,1,0:T(8,128)(2,1)S(1)}, u32[]{:S(2)}, u32[]{:S(2)}) %collective-permute-start.2) | collective-permute-done | bytes 786464 | tf_op jit(solution)/shard_map/ppermute | solution.py:76
  53.4 2.0 collective-permute-start.5
  55.4 1.8 collective-permute-start.9
  57.8 14.7 %collective-permute-done.4.refs_2_ = bf16[3,512,256]{2,1,0:T(8,128)(2,1)S(1)} collective-permute-done((bf16[3,512,256]{2,1,0:T(8,128)(2,1)}, bf16[3,512,256]{2,1,0:T(8,128)(2,1)S(1)}, u32[]{:S(2)}, u32[]{:S(2)}) %collective-permute-start.4) | collective-permute-done | bytes 786464 | tf_op jit(solution)/shard_map/ppermute | solution.py:76
  72.6 3.5 %shard_map.94 = (bf16[3,512,256]{2,1,0:T(8,128)(2,1)}, bf16[3,512,256]{2,1,0:T(8,128)(2,1)}, bf16[3,512,256]{2,1,0:T(8,128)(2,1)}) custom-call(s32[4]{0:T(128)} %get-tuple-element.234.at, bf16[1024,3584]{1,0:T(8,128)(2,1)} %w_gate.13, bf16[1024,3584]{1,0:T(8,128)(2,1)} %w_up.13, bf16[1024,3584]{1,0:T(8,128)(2,1)} %w_down.13, bf16[1024,3584]{1,0:T(8,128)(2,1)} %w_gate.13, ...), custom_call_target="tpu_custom_call" | custom-call | flops 1000 | bytes 1000 | tf_op jit(solution)/shard_map/pallas_call | solution.py:308
  76.1 1.6 collective-permute-start.10
  78.3 3.6 %shard_map.95 = (bf16[3,512,256]{2,1,0:T(8,128)(2,1)}, bf16[3,512,256]{2,1,0:T(8,128)(2,1)}, bf16[3,512,256]{2,1,0:T(8,128)(2,1)}) custom-call(s32[4]{0:T(128)} %get-tuple-element.233.at, bf16[1024,3584]{1,0:T(8,128)(2,1)} %w_gate.13, bf16[1024,3584]{1,0:T(8,128)(2,1)} %w_up.13, bf16[1024,3584]{1,0:T(8,128)(2,1)} %w_down.13, bf16[1024,3584]{1,0:T(8,128)(2,1)} %w_gate.13, ...), custom_call_target="tpu_custom_call" | custom-call | flops 1000 | bytes 1000 | tf_op jit(solution)/shard_map/pallas_call | solution.py:308
  81.9 5.2 %collective-permute-done.6.refs_3_ = bf16[3,512,256]{2,1,0:T(8,128)(2,1)S(1)} collective-permute-done((bf16[3,512,256]{2,1,0:T(8,128)(2,1)}, bf16[3,512,256]{2,1,0:T(8,128)(2,1)S(1)}, u32[]{:S(2)}, u32[]{:S(2)}) %collective-permute-start.6) | collective-permute-done | bytes 786464 | tf_op jit(solution)/shard_map/ppermute | solution.py:76
  87.1 2.6 collective-permute-start.14
  89.8 1.5 collective-permute-start.12
  91.3 5.3 %collective-permute-done.10.refs_4_ = bf16[3,512,256]{2,1,0:T(8,128)(2,1)} collective-permute-done((bf16[3,512,256]{2,1,0:T(8,128)(2,1)S(1)}, bf16[3,512,256]{2,1,0:T(8,128)(2,1)}, u32[]{:S(2)}, u32[]{:S(2)}) %collective-permute-start.10) | collective-permute-done | bytes 786464 | tf_op jit(solution)/shard_map/ppermute | solution.py:84
  96.7 3.6 %shard_map.96 = (bf16[3,512,256]{2,1,0:T(8,128)(2,1)}, bf16[3,512,256]{2,1,0:T(8,128)(2,1)}, bf16[3,512,256]{2,1,0:T(8,128)(2,1)}) custom-call(s32[4]{0:T(128)} %get-tuple-element.232.at, bf16[1024,3584]{1,0:T(8,128)(2,1)} %w_gate.13, bf16[1024,3584]{1,0:T(8,128)(2,1)} %w_up.13, bf16[1024,3584]{1,0:T(8,128)(2,1)} %w_down.13, bf16[1024,3584]{1,0:T(8,128)(2,1)} %w_gate.13, ...), custom_call_target="tpu_custom_call" | custom-call | flops 1000 | bytes 1000 | tf_op jit(solution)/shard_map/pallas_call | solution.py:308
  100.2 6.0 %collective-permute-done.11.refs_2_ = bf16[3,512,256]{2,1,0:T(8,128)(2,1)S(1)} collective-permute-done((bf16[3,512,256]{2,1,0:T(8,128)(2,1)}, bf16[3,512,256]{2,1,0:T(8,128)(2,1)S(1)}, u32[]{:S(2)}, u32[]{:S(2)}) %collective-permute-start.11) | collective-permute-done | bytes 786464 | tf_op jit(solution)/shard_map/ppermute | solution.py:76
  106.3 1.5 collective-permute-start.18
  108.5 3.6 %shard_map.99 = (bf16[3,512,256]{2,1,0:T(8,128)(2,1)}, bf16[3,512,256]{2,1,0:T(8,128)(2,1)}, bf16[3,512,256]{2,1,0:T(8,128)(2,1)}) custom-call(s32[4]{0:T(128)} %get-tuple-element.223.at, bf16[1024,3584]{1,0:T(8,128)(2,1)} %w_gate.13, bf16[1024,3584]{1,0:T(8,128)(2,1)} %w_up.13, bf16[1024,3584]{1,0:T(8,128)(2,1)} %w_down.13, bf16[1024,3584]{1,0:T(8,128)(2,1)} %w_gate.13, ...), custom_call_target="tpu_custom_call" | custom-call | flops 1000 | bytes 1000 | tf_op jit(solution)/shard_map/pallas_call | solution.py:308
  112.1 1.1 broadcast_in_dim.5.refs_7_
  113.2 10.8 %shard_map.98 = (f32[1024,192]{1,0:T(8,128)}, f32[1024,256]{1,0:T(8,128)}, f32[1024,256]{1,0:T(8,128)}) custom-call(s32[8]{0:T(128)} %stack.139.places, bf16[8,512,1024]{2,1,0:T(8,128)(2,1)} %bitcast.73, bf16[1024,3584]{1,0:T(8,128)(2,1)} %w_gate.13, bf16[1024,3584]{1,0:T(8,128)(2,1)} %w_up.13, ...), custom_call_target="tpu_custom_call", output_to_operand_aliasing={{0}: (11, {})} | custom-call | flops 1000 | bytes 1000 | tf_op jit(solution)/shard_map/pallas_call | solution.py:275
  125.2 5.2 %collective-permute-done.18.refs_4_ = bf16[3,512,256]{2,1,0:T(8,128)(2,1)} collective-permute-done((bf16[3,512,256]{2,1,0:T(8,128)(2,1)S(1)}, bf16[3,512,256]{2,1,0:T(8,128)(2,1)}, u32[]{:S(2)}, u32[]{:S(2)}) %collective-permute-start.18) | collective-permute-done | bytes 786464 | tf_op jit(solution)/shard_map/ppermute | solution.py:84
  131.0 10.9 %shard_map.100 = (f32[1024,192]{1,0:T(8,128)}, f32[1024,256]{1,0:T(8,128)}, f32[1024,256]{1,0:T(8,128)}) custom-call(s32[8]{0:T(128)} %stack.283.places, bf16[8,512,1024]{2,1,0:T(8,128)(2,1)} %bitcast.74, bf16[1024,3584]{1,0:T(8,128)(2,1)} %w_gate.13, bf16[1024,3584]{1,0:T(8,128)(2,1)} %w_up.13, ...), custom_call_target="tpu_custom_call", output_to_operand_aliasing={{0}: (11, {})} | custom-call | flops 1000 | bytes 1000 | tf_op jit(solution)/shard_map/pallas_call | solution.py:275
  141.9 3.0 collective-permute-done.20.refs_2_
  145.3 8.2 %shard_map.97 = f32[1024,128]{1,0:T(8,128)} custom-call(bf16[8,512,1024]{2,1,0:T(8,128)(2,1)} %bitcast.75, bf16[3,64,4096]{2,1,0:T(8,128)(2,1)} %bitcast.100), custom_call_target="tpu_custom_call" | custom-call | flops 1000 | bytes 1000 | tf_op jit(solution)/shard_map/pallas_call | solution.py:131
  153.6 3.6 %collective-permute-done.23.refs_3_ = bf16[3,512,256]{2,1,0:T(8,128)(2,1)} collective-permute-done((bf16[3,512,256]{2,1,0:T(8,128)(2,1)}, bf16[3,512,256]{2,1,0:T(8,128)(2,1)}, u32[]{:S(2)}, u32[]{:S(2)}) %collective-permute-start.23) | collective-permute-done | bytes 786464 | tf_op jit(solution)/shard_map/ppermute | solution.py:76
  157.2 2.9 collective-permute-start.24
  160.9 2.8 collective-permute-done.21.refs_4_
  164.4 10.6 %shard_map.101 = (f32[1024,192]{1,0:T(8,128)}, f32[1024,256]{1,0:T(8,128)}, f32[1024,256]{1,0:T(8,128)}) custom-call(s32[8]{0:T(128)} %stack.138.places, bf16[8,512,1024]{2,1,0:T(8,128)(2,1)} %bitcast.76, bf16[1024,3584]{1,0:T(8,128)(2,1)} %w_gate.13, bf16[1024,3584]{1,0:T(8,128)(2,1)} %w_up.13, ...), custom_call_target="tpu_custom_call", output_to_operand_aliasing={{0}: (11, {})} | custom-call | flops 1000 | bytes 1000 | tf_op jit(solution)/shard_map/pallas_call | solution.py:275
  175.0 1.8 collective-permute-done.22.refs_2_
  178.2 13.9 %shard_map.102 = (f32[1024,192]{1,0:T(8,128)}, f32[1024,64]{1,0:T(8,128)}) custom-call(s32[8]{0:T(128)} %stack.139.places, bf16[8,512,1024]{2,1,0:T(8,128)(2,1)} %bitcast.82, bf16[1024,3584]{1,0:T(8,128)(2,1)} %w_down.13, bf16[3,512,256]{2,1,0:T(8,128)(2,1)} %collective-permute-done.7.refs_0_, ...), custom_call_target="tpu_custom_call", output_to_operand_aliasing={{0}: (13, {})} | custom-call | flops 1000 | bytes 1000 | tf_op jit(solution)/shard_map/pallas_call | solution.py:275
  192.2 1.7 collective-permute-start.30
  194.6 14.8 %shard_map.103.refs_9_ = f32[1024,192]{1,0:T(8,128)} custom-call(s32[8]{0:T(128)} %stack.286.places, bf16[8,512,1024]{2,1,0:T(8,128)(2,1)} %bitcast.77, bf16[8,512,1024]{2,1,0:T(8,128)(2,1)} %bitcast.83, bf16[1024,3584]{1,0:T(8,128)(2,1)} %w_gate.13, bf16[1024,3584]{1,0:T(8,128)(2,1)} %w_up.13, ...), custom_call_target="tpu_custom_call", output_to_operand_aliasing={{}: (13, {})} | custom-call | flops 1000 | bytes 1000 | tf_op jit(solution)/shard_map/pallas_call | solution.py:275
  209.4 0.8 collective-permute-start.29
  211.0 9.1 %shard_map.104.refs_9_ = f32[1024,192]{1,0:T(8,128)} custom-call(s32[8]{0:T(128)} %stack.283.places, bf16[8,512,1024]{2,1,0:T(8,128)(2,1)} %bitcast.84, bf16[1024,3584]{1,0:T(8,128)(2,1)} %w_down.13, bf16[3,512,256]{2,1,0:T(8,128)(2,1)} %copy-done.6, bf16[3,512,256]{2,1,0:T(8,128)(2,1)} %collective-permute-done.15.refs_1_, ...), custom_call_target="tpu_custom_call", output_to_operand_aliasing={{}: (12, {})} | custom-call | flops 1000 | bytes 1000 | tf_op jit(solution)/shard_map/pallas_call | solution.py:275
  220.1 9.1 %shard_map.105.refs_7_ = f32[1024,192]{1,0:T(8,128)} custom-call(s32[8]{0:T(128)} %stack.138.places, bf16[8,512,1024]{2,1,0:T(8,128)(2,1)} %bitcast.85, bf16[1024,3584]{1,0:T(8,128)(2,1)} %w_down.13, bf16[3,512,256]{2,1,0:T(8,128)(2,1)} %copy-done.8, bf16[3,512,256]{2,1,0:T(8,128)(2,1)} %collective-permute-done.17.refs_1_, ...), custom_call_target="tpu_custom_call", output_to_operand_aliasing={{}: (12, {})} | custom-call | flops 1000 | bytes 1000 | tf_op jit(solution)/shard_map/pallas_call | solution.py:275
  229.2 1.7 collective-permute-start.39
  231.1 1.5 collective-permute-start.37
  233.9 14.6 %shard_map.106.refs_7_ = f32[1024,192]{1,0:T(8,128)} custom-call(s32[8]{0:T(128)} %stack.287.places, bf16[8,512,1024]{2,1,0:T(8,128)(2,1)} %bitcast.78, bf16[8,512,1024]{2,1,0:T(8,128)(2,1)} %bitcast.86, bf16[1024,3584]{1,0:T(8,128)(2,1)} %w_gate.13, bf16[1024,3584]{1,0:T(8,128)(2,1)} %w_up.13, ...), custom_call_target="tpu_custom_call", output_to_operand_aliasing={{}: (13, {})} | custom-call | flops 1000 | bytes 1000 | tf_op jit(solution)/shard_map/pallas_call | solution.py:275
  248.5 1.3 collective-permute-done.39.refs_2_
  249.8 0.9 collective-permute-done.37.refs_5_
  250.7 0.9 collective-permute-start.40
  252.3 14.8 %shard_map.107.sums_in = f32[1024,192]{1,0:T(8,128)} custom-call(s32[8]{0:T(128)} %stack.285.places, bf16[8,512,1024]{2,1,0:T(8,128)(2,1)} %bitcast.79, bf16[8,512,1024]{2,1,0:T(8,128)(2,1)} %bitcast.87, bf16[1024,3584]{1,0:T(8,128)(2,1)} %w_gate.13, bf16[1024,3584]{1,0:T(8,128)(2,1)} %w_up.13, ...), custom_call_target="tpu_custom_call", output_to_operand_aliasing={{}: (13, {})} | custom-call | flops 1000 | bytes 1000 | tf_op jit(solution)/shard_map/pallas_call | solution.py:275
  267.1 2.1 collective-permute-done.40.refs_4_
  271.8 1.1 collective-permute-done.42.refs_1_
  272.9 12.8 %shard_map.108 = (f32[1024,256]{1,0:T(8,128)}, f32[1024,256]{1,0:T(8,128)}, f32[1024,256]{1,0:T(8,128)}) custom-call(s32[8]{0:T(128)} %stack.284.places, bf16[8,512,1024]{2,1,0:T(8,128)(2,1)} %bitcast.80, bf16[8,512,1024]{2,1,0:T(8,128)(2,1)} %bitcast.88, bf16[1024,3584]{1,0:T(8,128)(2,1)} %w_gate.13, bf16[1024,3584]{1,0:T(8,128)(2,1)} %w_up.13, ...), custom_call_target="tpu_custom_call" | custom-call | flops 1000 | bytes 1000 | tf_op jit(solution)/shard_map/pallas_call | solution.py:197
  285.7 3.4 %collective-permute-done.43.piece = bf16[3,512,256]{2,1,0:T(8,128)(2,1)S(1)} collective-permute-done((bf16[3,512,256]{2,1,0:T(8,128)(2,1)S(1)}, bf16[3,512,256]{2,1,0:T(8,128)(2,1)S(1)}, u32[]{:S(2)}, u32[]{:S(2)}) %collective-permute-start.43) | collective-permute-done | bytes 786464 | tf_op jit(solution)/shard_map/ppermute | solution.py:84
  289.1 0.9 copy-done.17
  290.0 6.9 %shard_map.109 = f32[1024,192]{1,0:T(8,128)} custom-call(s32[2]{0:T(128)} %pad_add_fusion.7.places, bf16[8,512,1024]{2,1,0:T(8,128)(2,1)} %bitcast.81, bf16[8,512,1024]{2,1,0:T(8,128)(2,1)} %bitcast.89, f32[1024,256]{1,0:T(8,128)} %get-tuple-element.218.gate_in, f32[1024,256]{1,0:T(8,128)} %get-tuple-element.219.up_in, ...), custom_call_target="tpu_custom_call", output_to_operand_aliasing={{}: (8, {})} | custom-call | flops 1000 | bytes 1000 | tf_op jit(solution)/shard_map/pallas_call | solution.py:197
  296.9 1.6 fusion.9
  298.6 1.0 convolution_bitcast_fusion
  299.6 1.0 convolution_bitcast_fusion.1
  300.6 1.0 convolution_bitcast_fusion.2
  302.1 1.3 collective-permute-done.44
  303.4 1.6 collective-permute-start.45
  305.1 3.2 collective-permute-done.45
  308.4 2.8 collective-permute-start.46
  311.3 4.3 %collective-permute-done.46 = f32[2,12288]{1,0:T(2,128)S(1)} collective-permute-done((f32[2,12288]{1,0:T(2,128)S(1)}, f32[2,12288]{1,0:T(2,128)S(1)}, u32[]{:S(2)}, u32[]{:S(2)}) %collective-permute-start.46) | collective-permute-done | bytes 98336 | tf_op jit(solution)/shard_map/ppermute | solution.py:80
  315.6 1.8 fusion.1
  (129 shorter events, 18.1 us)
Async XLA Ops:
  6.5 105.6 %all-gather.5.cloned.1.call-start = ((), (), s32[]{:S(2)}) async-start(), calls=%async_computation | async-start | bytes 9437184 | tf_op jit(solution)/shard_map/all_gather | solution.py:370
  7.3 171.0 %all-gather.7.cloned.1.call-start = ((), (), s32[]{:S(2)}) async-start(), calls=%async_computation.1 | async-start | bytes 9437184 | tf_op jit(solution)/shard_map/all_gather | solution.py:371
  10.4 12.9 %collective-permute-start = (bf16[8,12288]{1,0:T(8,128)(2,1)}, bf16[8,12288]{1,0:T(8,128)(2,1)S(1)}, u32[]{:S(2)}, u32[]{:S(2)}) collective-permute-start(bf16[8,12288]{1,0:T(8,128)(2,1)} %param.17), channel_id=1, source_target_pairs={{0,8},{4,12},{8,0},{12,4},{1,9},{5,13},{9,1},{13,5},{2,10},{6,14},... | collective-permute-start | bytes 589832 | tf_op jit(solution)/shard_map/ppermute | solution.py:76
  18.2 20.7 %collective-permute-start.1 = (bf16[3,512,256]{2,1,0:T(8,128)(2,1)}, bf16[3,512,256]{2,1,0:T(8,128)(2,1)S(1)}, u32[]{:S(2)}, u32[]{:S(2)}) collective-permute-start(bf16[3,512,256]{2,1,0:T(8,128)(2,1)} %get-tuple-element.114), channel_id=1, source_target_pairs={{0,8},{4,12},{8,0},{12,4},{1,9},{5,13},{9,1},{13,5},{2,10},{6,14},... | collective-permute-start | bytes 2359304 | tf_op jit(solution)/shard_map/ppermute | solution.py:76
  18.2 35.1 %collective-permute-start.2 = (bf16[3,512,256]{2,1,0:T(8,128)(2,1)}, bf16[3,512,256]{2,1,0:T(8,128)(2,1)S(1)}, u32[]{:S(2)}, u32[]{:S(2)}) collective-permute-start(bf16[3,512,256]{2,1,0:T(8,128)(2,1)} %get-tuple-element.138), channel_id=1, source_target_pairs={{0,12},{4,8},{8,4},{12,0},{1,13},{5,9},{9,5},{13,1},{2,14},{6,10},... | collective-permute-start | bytes 2359304 | tf_op jit(solution)/shard_map/ppermute | solution.py:76
  38.9 18.5 %collective-permute-start.3 = (bf16[3,512,256]{2,1,0:T(8,128)(2,1)S(1)}, bf16[3,512,256]{2,1,0:T(8,128)(2,1)}, u32[]{:S(2)}, u32[]{:S(2)}) collective-permute-start(bf16[3,512,256]{2,1,0:T(8,128)(2,1)S(1)} %collective-permute-done.1.refs_2_), channel_id=1, source_target_pairs={{0,16},{16,0},{1,17},{17,1},{2,18},{18,2},{3,19},{19,3},{4,20},{20... | collective-permute-start | bytes 2359304 | tf_op jit(solution)/shard_map/ppermute | solution.py:84
  40.4 32.2 %collective-permute-start.4 = (bf16[3,512,256]{2,1,0:T(8,128)(2,1)}, bf16[3,512,256]{2,1,0:T(8,128)(2,1)S(1)}, u32[]{:S(2)}, u32[]{:S(2)}) collective-permute-start(bf16[3,512,256]{2,1,0:T(8,128)(2,1)} %get-tuple-element.128), channel_id=1, source_target_pairs={{0,8},{4,12},{8,0},{12,4},{1,9},{5,13},{9,1},{13,5},{2,10},{6,14},... | collective-permute-start | bytes 2359304 | tf_op jit(solution)/shard_map/ppermute | solution.py:76
  53.3 22.8 %copy-start.4 = (bf16[3,512,256]{2,1,0:T(8,128)(2,1)}, bf16[3,512,256]{2,1,0:T(8,128)(2,1)S(1)}, u32[]{:S(2)}) copy-start(bf16[3,512,256]{2,1,0:T(8,128)(2,1)S(1)} %collective-permute-done.2.refs_3_) | copy-start | bytes 2359300
  53.4 24.4 %collective-permute-start.5 = (bf16[3,512,256]{2,1,0:T(8,128)(2,1)S(1)}, bf16[3,512,256]{2,1,0:T(8,128)(2,1)}, u32[]{:S(2)}, u32[]{:S(2)}) collective-permute-start(bf16[3,512,256]{2,1,0:T(8,128)(2,1)S(1)} %collective-permute-done.2.refs_3_), channel_id=1, source_target_pairs={{0,16},{16,0},{1,17},{17,1},{2,18},{18,2},{3,19},{19,3},{4,20},{20... | collective-permute-start | bytes 2359304 | tf_op jit(solution)/shard_map/ppermute | solution.py:84
  55.4 20.7 %collective-permute-start.9 = (bf16[2,8,12288]{2,1,0:T(8,128)(2,1)}, bf16[2,8,12288]{2,1,0:T(8,128)(2,1)S(1)}, u32[]{:S(2)}, u32[]{:S(2)}) collective-permute-start(bf16[2,8,12288]{2,1,0:T(8,128)(2,1)} %get-tuple-element.141), channel_id=1, source_target_pairs={{0,4},{4,0},{8,12},{12,8},{1,5},{5,1},{9,13},{13,9},{2,6},{6,2},{1... | collective-permute-start | bytes 1179656 | tf_op jit(solution)/shard_map/ppermute | solution.py:76
  57.2 29.9 %collective-permute-start.6 = (bf16[3,512,256]{2,1,0:T(8,128)(2,1)}, bf16[3,512,256]{2,1,0:T(8,128)(2,1)S(1)}, u32[]{:S(2)}, u32[]{:S(2)}) collective-permute-start(bf16[3,512,256]{2,1,0:T(8,128)(2,1)} %get-tuple-element.162), channel_id=1, source_target_pairs={{0,12},{4,8},{8,4},{12,0},{1,13},{5,9},{9,5},{13,1},{2,14},{6,10},... | collective-permute-start | bytes 2359304 | tf_op jit(solution)/shard_map/ppermute | solution.py:76
  57.3 29.7 %collective-permute-start.7 = (bf16[3,512,256]{2,1,0:T(8,128)(2,1)}, bf16[3,512,256]{2,1,0:T(8,128)(2,1)}, u32[]{:S(2)}, u32[]{:S(2)}) collective-permute-start(bf16[3,512,256]{2,1,0:T(8,128)(2,1)} %get-tuple-element.138), channel_id=1, source_target_pairs={{0,4},{4,0},{8,12},{12,8},{1,5},{5,1},{9,13},{13,9},{2,6},{6,2},{1... | collective-permute-start | bytes 2359304 | tf_op jit(solution)/shard_map/ppermute | solution.py:76
  72.6 14.5 %collective-permute-start.8 = (bf16[3,512,256]{2,1,0:T(8,128)(2,1)}, bf16[3,512,256]{2,1,0:T(8,128)(2,1)}, u32[]{:S(2)}, u32[]{:S(2)}) collective-permute-start(bf16[3,512,256]{2,1,0:T(8,128)(2,1)} %get-tuple-element.140), channel_id=1, source_target_pairs={{0,4},{4,0},{8,12},{12,8},{1,5},{5,1},{9,13},{13,9},{2,6},{6,2},{1... | collective-permute-start | bytes 2359304 | tf_op jit(solution)/shard_map/ppermute | solution.py:76
  76.1 20.5 %collective-permute-start.10 = (bf16[3,512,256]{2,1,0:T(8,128)(2,1)S(1)}, bf16[3,512,256]{2,1,0:T(8,128)(2,1)}, u32[]{:S(2)}, u32[]{:S(2)}) collective-permute-start(bf16[3,512,256]{2,1,0:T(8,128)(2,1)S(1)} %collective-permute-done.4.refs_2_), channel_id=1, source_target_pairs={{0,16},{16,0},{1,17},{17,1},{2,18},{18,2},{3,19},{19,3},{4,20},{20... | collective-permute-start | bytes 2359304 | tf_op jit(solution)/shard_map/ppermute | solution.py:84
  77.7 28.5 %collective-permute-start.11 = (bf16[3,512,256]{2,1,0:T(8,128)(2,1)}, bf16[3,512,256]{2,1,0:T(8,128)(2,1)S(1)}, u32[]{:S(2)}, u32[]{:S(2)}) collective-permute-start(bf16[3,512,256]{2,1,0:T(8,128)(2,1)} %get-tuple-element.150), channel_id=1, source_target_pairs={{0,8},{4,12},{8,0},{12,4},{1,9},{5,13},{9,1},{13,5},{2,10},{6,14},... | collective-permute-start | bytes 2359304 | tf_op jit(solution)/shard_map/ppermute | solution.py:76
  87.1 13.2 %copy-start.2 = (bf16[3,512,256]{2,1,0:T(8,128)(2,1)}, bf16[3,512,256]{2,1,0:T(8,128)(2,1)S(1)}, u32[]{:S(2)}) copy-start(bf16[3,512,256]{2,1,0:T(8,128)(2,1)S(1)} %collective-permute-done.6.refs_3_) | copy-start | bytes 2359300
  87.1 37.0 %collective-permute-start.14 = (bf16[3,512,256]{2,1,0:T(8,128)(2,1)}, bf16[3,512,256]{2,1,0:T(8,128)(2,1)S(1)}, u32[]{:S(2)}, u32[]{:S(2)}) collective-permute-start(bf16[3,512,256]{2,1,0:T(8,128)(2,1)} %get-tuple-element.162), channel_id=1, source_target_pairs={{0,4},{4,0},{8,12},{12,8},{1,5},{5,1},{9,13},{13,9},{2,6},{6,2},{1... | collective-permute-start | bytes 2359304 | tf_op jit(solution)/shard_map/ppermute | solution.py:76
  89.7 34.9 %collective-permute-start.15 = (bf16[3,512,256]{2,1,0:T(8,128)(2,1)}, bf16[3,512,256]{2,1,0:T(8,128)(2,1)}, u32[]{:S(2)}, u32[]{:S(2)}) collective-permute-start(bf16[3,512,256]{2,1,0:T(8,128)(2,1)} %get-tuple-element.163), channel_id=1, source_target_pairs={{0,4},{4,0},{8,12},{12,8},{1,5},{5,1},{9,13},{13,9},{2,6},{6,2},{1... | collective-permute-start | bytes 2359304 | tf_op jit(solution)/shard_map/ppermute | solution.py:76
  89.8 34.8 %collective-permute-start.12 = (bf16[3,512,256]{2,1,0:T(8,128)(2,1)S(1)}, bf16[3,512,256]{2,1,0:T(8,128)(2,1)}, u32[]{:S(2)}, u32[]{:S(2)}) collective-permute-start(bf16[3,512,256]{2,1,0:T(8,128)(2,1)S(1)} %collective-permute-done.6.refs_3_), channel_id=1, source_target_pairs={{0,16},{16,0},{1,17},{17,1},{2,18},{18,2},{3,19},{19,3},{4,20},{20... | collective-permute-start | bytes 2359304 | tf_op jit(solution)/shard_map/ppermute | solution.py:84
  96.7 27.9 %collective-permute-start.13 = (bf16[3,512,256]{2,1,0:T(8,128)(2,1)}, bf16[3,512,256]{2,1,0:T(8,128)(2,1)S(1)}, u32[]{:S(2)}, u32[]{:S(2)}) collective-permute-start(bf16[3,512,256]{2,1,0:T(8,128)(2,1)} %get-tuple-element.171), channel_id=1, source_target_pairs={{0,12},{4,8},{8,4},{12,0},{1,13},{5,9},{9,5},{13,1},{2,14},{6,10},... | collective-permute-start | bytes 2359304 | tf_op jit(solution)/shard_map/ppermute | solution.py:76
  106.3 5.8 %copy-start.5 = (bf16[3,512,256]{2,1,0:T(8,128)(2,1)}, bf16[3,512,256]{2,1,0:T(8,128)(2,1)S(1)}, u32[]{:S(2)}) copy-start(bf16[3,512,256]{2,1,0:T(8,128)(2,1)S(1)} %collective-permute-done.11.refs_2_) | copy-start | bytes 2359300
  106.3 24.1 %collective-permute-start.18 = (bf16[3,512,256]{2,1,0:T(8,128)(2,1)S(1)}, bf16[3,512,256]{2,1,0:T(8,128)(2,1)}, u32[]{:S(2)}, u32[]{:S(2)}) collective-permute-start(bf16[3,512,256]{2,1,0:T(8,128)(2,1)S(1)} %collective-permute-done.11.refs_2_), channel_id=1, source_target_pairs={{0,16},{16,0},{1,17},{17,1},{2,18},{18,2},{3,19},{19,3},{4,20},{20... | collective-permute-start | bytes 2359304 | tf_op jit(solution)/shard_map/ppermute | solution.py:84
  124.0 7.0 %copy-start.6 = (bf16[3,512,256]{2,1,0:T(8,128)(2,1)}, bf16[3,512,256]{2,1,0:T(8,128)(2,1)S(1)}, u32[]{:S(2)}) copy-start(bf16[3,512,256]{2,1,0:T(8,128)(2,1)S(1)} %collective-permute-done.14.refs_0_) | copy-start | bytes 2359300
  124.0 20.9 %collective-permute-start.20 = (bf16[3,512,256]{2,1,0:T(8,128)(2,1)}, bf16[3,512,256]{2,1,0:T(8,128)(2,1)}, u32[]{:S(2)}, u32[]{:S(2)}) collective-permute-start(bf16[3,512,256]{2,1,0:T(8,128)(2,1)} %get-tuple-element.177), channel_id=1, source_target_pairs={{0,8},{4,12},{8,0},{12,4},{1,9},{5,13},{9,1},{13,5},{2,10},{6,14},... | collective-permute-start | bytes 2359304 | tf_op jit(solution)/shard_map/ppermute | solution.py:76
  124.6 17.3 %copy-start.7 = (bf16[3,512,256]{2,1,0:T(8,128)(2,1)}, bf16[3,512,256]{2,1,0:T(8,128)(2,1)S(1)}, u32[]{:S(2)}) copy-start(bf16[3,512,256]{2,1,0:T(8,128)(2,1)S(1)} %collective-permute-done.13.refs_3_) | copy-start | bytes 2359300
  124.6 28.9 %collective-permute-start.16 = (bf16[3,512,256]{2,1,0:T(8,128)(2,1)}, bf16[3,512,256]{2,1,0:T(8,128)(2,1)S(1)}, u32[]{:S(2)}, u32[]{:S(2)}) collective-permute-start(bf16[3,512,256]{2,1,0:T(8,128)(2,1)} %get-tuple-element.171), channel_id=1, source_target_pairs={{0,4},{4,0},{8,12},{12,8},{1,5},{5,1},{9,13},{13,9},{2,6},{6,2},{1... | collective-permute-start | bytes 2359304 | tf_op jit(solution)/shard_map/ppermute | solution.py:76
  124.7 29.0 %collective-permute-start.17 = (bf16[3,512,256]{2,1,0:T(8,128)(2,1)}, bf16[3,512,256]{2,1,0:T(8,128)(2,1)}, u32[]{:S(2)}, u32[]{:S(2)}) collective-permute-start(bf16[3,512,256]{2,1,0:T(8,128)(2,1)} %get-tuple-element.172), channel_id=1, source_target_pairs={{0,4},{4,0},{8,12},{12,8},{1,5},{5,1},{9,13},{13,9},{2,6},{6,2},{1... | collective-permute-start | bytes 2359304 | tf_op jit(solution)/shard_map/ppermute | solution.py:76
  125.2 28.5 %collective-permute-start.19 = (bf16[3,512,256]{2,1,0:T(8,128)(2,1)S(1)}, bf16[3,512,256]{2,1,0:T(8,128)(2,1)}, u32[]{:S(2)}, u32[]{:S(2)}) collective-permute-start(bf16[3,512,256]{2,1,0:T(8,128)(2,1)S(1)} %collective-permute-done.13.refs_3_), channel_id=1, source_target_pairs={{0,16},{16,0},{1,17},{17,1},{2,18},{18,2},{3,19},{19,3},{4,20},{20... | collective-permute-start | bytes 2359304 | tf_op jit(solution)/shard_map/ppermute | solution.py:84
  130.4 26.8 %collective-permute-start.23 = (bf16[3,512,256]{2,1,0:T(8,128)(2,1)}, bf16[3,512,256]{2,1,0:T(8,128)(2,1)}, u32[]{:S(2)}, u32[]{:S(2)}) collective-permute-start(bf16[3,512,256]{2,1,0:T(8,128)(2,1)} %get-tuple-element.189), channel_id=1, source_target_pairs={{0,12},{4,8},{8,4},{12,0},{1,13},{5,9},{9,5},{13,1},{2,14},{6,10},... | collective-permute-start | bytes 2359304 | tf_op jit(solution)/shard_map/ppermute | solution.py:76
  144.9 18.8 %collective-permute-start.21 = (bf16[3,512,256]{2,1,0:T(8,128)(2,1)}, bf16[3,512,256]{2,1,0:T(8,128)(2,1)}, u32[]{:S(2)}, u32[]{:S(2)}) collective-permute-start(bf16[3,512,256]{2,1,0:T(8,128)(2,1)} %collective-permute-done.20.refs_2_), channel_id=1, source_target_pairs={{0,16},{16,0},{1,17},{17,1},{2,18},{18,2},{3,19},{19,3},{4,20},{20... | collective-permute-start | bytes 2359304 | tf_op jit(solution)/shard_map/ppermute | solution.py:84
  153.5 10.9 %copy-start.8 = (bf16[3,512,256]{2,1,0:T(8,128)(2,1)}, bf16[3,512,256]{2,1,0:T(8,128)(2,1)S(1)}, u32[]{:S(2)}) copy-start(bf16[3,512,256]{2,1,0:T(8,128)(2,1)S(1)} %collective-permute-done.16.refs_0_) | copy-start | bytes 2359300
  153.5 23.3 %collective-permute-start.22 = (bf16[3,512,256]{2,1,0:T(8,128)(2,1)}, bf16[3,512,256]{2,1,0:T(8,128)(2,1)S(1)}, u32[]{:S(2)}, u32[]{:S(2)}) collective-permute-start(bf16[3,512,256]{2,1,0:T(8,128)(2,1)} %get-tuple-element.180), channel_id=1, source_target_pairs={{0,8},{4,12},{8,0},{12,4},{1,9},{5,13},{9,1},{13,5},{2,10},{6,14},... | collective-permute-start | bytes 2359304 | tf_op jit(solution)/shard_map/ppermute | solution.py:76
  157.2 20.3 %collective-permute-start.24 = (bf16[3,512,256]{2,1,0:T(8,128)(2,1)}, bf16[3,512,256]{2,1,0:T(8,128)(2,1)}, u32[]{:S(2)}, u32[]{:S(2)}) collective-permute-start(bf16[3,512,256]{2,1,0:T(8,128)(2,1)} %get-tuple-element.189), channel_id=1, source_target_pairs={{0,4},{4,0},{8,12},{12,8},{1,5},{5,1},{9,13},{13,9},{2,6},{6,2},{1... | collective-permute-start | bytes 2359304 | tf_op jit(solution)/shard_map/ppermute | solution.py:76
  160.1 32.0 %collective-permute-start.25 = (bf16[3,512,256]{2,1,0:T(8,128)(2,1)}, bf16[3,512,256]{2,1,0:T(8,128)(2,1)}, u32[]{:S(2)}, u32[]{:S(2)}) collective-permute-start(bf16[3,512,256]{2,1,0:T(8,128)(2,1)} %get-tuple-element.190), channel_id=1, source_target_pairs={{0,4},{4,0},{8,12},{12,8},{1,5},{5,1},{9,13},{13,9},{2,6},{6,2},{1... | collective-permute-start | bytes 2359304 | tf_op jit(solution)/shard_map/ppermute | solution.py:76
  160.1 32.0 %collective-permute-start.26 = (bf16[3,512,256]{2,1,0:T(8,128)(2,1)}, bf16[3,512,256]{2,1,0:T(8,128)(2,1)}, u32[]{:S(2)}, u32[]{:S(2)}) collective-permute-start(bf16[3,512,256]{2,1,0:T(8,128)(2,1)} %collective-permute-done.23.refs_3_), channel_id=1, source_target_pairs={{0,16},{16,0},{1,17},{17,1},{2,18},{18,2},{3,19},{19,3},{4,20},{20... | collective-permute-start | bytes 2359304 | tf_op jit(solution)/shard_map/ppermute | solution.py:84
  163.7 28.4 %collective-permute-start.27 = (bf16[3,512,256]{2,1,0:T(8,128)(2,1)}, bf16[3,512,256]{2,1,0:T(8,128)(2,1)S(1)}, u32[]{:S(2)}, u32[]{:S(2)}) collective-permute-start(bf16[3,512,256]{2,1,0:T(8,128)(2,1)} %get-tuple-element.199), channel_id=1, source_target_pairs={{0,12},{4,8},{8,4},{12,0},{1,13},{5,9},{9,5},{13,1},{2,14},{6,10},... | collective-permute-start | bytes 2359304 | tf_op jit(solution)/shard_map/ppermute | solution.py:76
  176.8 15.3 %copy-start.10 = (bf16[3,512,256]{2,1,0:T(8,128)(2,1)}, bf16[3,512,256]{2,1,0:T(8,128)(2,1)S(1)}, u32[]{:S(2)}) copy-start(bf16[3,512,256]{2,1,0:T(8,128)(2,1)S(1)} %collective-permute-done.22.refs_2_) | copy-start | bytes 2359300
  176.8 32.6 %collective-permute-start.33 = (bf16[3,512,256]{2,1,0:T(8,128)(2,1)S(1)}, bf16[3,512,256]{2,1,0:T(8,128)(2,1)}, u32[]{:S(2)}, u32[]{:S(2)}) collective-permute-start(bf16[3,512,256]{2,1,0:T(8,128)(2,1)S(1)} %collective-permute-done.22.refs_2_), channel_id=1, source_target_pairs={{0,16},{16,0},{1,17},{17,1},{2,18},{18,2},{3,19},{19,3},{4,20},{20... | collective-permute-start | bytes 2359304 | tf_op jit(solution)/shard_map/ppermute | solution.py:84
  177.5 32.7 %collective-permute-start.32 = (bf16[3,512,256]{2,1,0:T(8,128)(2,1)}, bf16[3,512,256]{2,1,0:T(8,128)(2,1)S(1)}, u32[]{:S(2)}, u32[]{:S(2)}) collective-permute-start(bf16[3,512,256]{2,1,0:T(8,128)(2,1)} %get-tuple-element.201), channel_id=1, source_target_pairs={{0,8},{4,12},{8,0},{12,4},{1,9},{5,13},{9,1},{13,5},{2,10},{6,14},... | collective-permute-start | bytes 2359304 | tf_op jit(solution)/shard_map/ppermute | solution.py:76
  192.2 17.3 %copy-start.12 = (bf16[3,512,256]{2,1,0:T(8,128)(2,1)}, bf16[3,512,256]{2,1,0:T(8,128)(2,1)S(1)}, u32[]{:S(2)}) copy-start(bf16[3,512,256]{2,1,0:T(8,128)(2,1)S(1)} %collective-permute-done.27.refs_3_) | copy-start | bytes 2359300
  192.2 37.0 %collective-permute-start.30 = (bf16[3,512,256]{2,1,0:T(8,128)(2,1)}, bf16[3,512,256]{2,1,0:T(8,128)(2,1)S(1)}, u32[]{:S(2)}, u32[]{:S(2)}) collective-permute-start(bf16[3,512,256]{2,1,0:T(8,128)(2,1)} %get-tuple-element.199), channel_id=1, source_target_pairs={{0,4},{4,0},{8,12},{12,8},{1,5},{5,1},{9,13},{13,9},{2,6},{6,2},{1... | collective-permute-start | bytes 2359304 | tf_op jit(solution)/shard_map/ppermute | solution.py:76
  193.9 37.0 %collective-permute-start.31 = (bf16[3,512,256]{2,1,0:T(8,128)(2,1)}, bf16[3,512,256]{2,1,0:T(8,128)(2,1)}, u32[]{:S(2)}, u32[]{:S(2)}) collective-permute-start(bf16[3,512,256]{2,1,0:T(8,128)(2,1)} %get-tuple-element.200), channel_id=1, source_target_pairs={{0,4},{4,0},{8,12},{12,8},{1,5},{5,1},{9,13},{13,9},{2,6},{6,2},{1... | collective-permute-start | bytes 2359304 | tf_op jit(solution)/shard_map/ppermute | solution.py:76
  193.9 37.0 %collective-permute-start.28 = (bf16[3,512,256]{2,1,0:T(8,128)(2,1)S(1)}, bf16[3,512,256]{2,1,0:T(8,128)(2,1)}, u32[]{:S(2)}, u32[]{:S(2)}) collective-permute-start(bf16[3,512,256]{2,1,0:T(8,128)(2,1)S(1)} %collective-permute-done.27.refs_3_), channel_id=1, source_target_pairs={{0,16},{16,0},{1,17},{17,1},{2,18},{18,2},{3,19},{19,3},{4,20},{20... | collective-permute-start | bytes 2359304 | tf_op jit(solution)/shard_map/ppermute | solution.py:84
  209.4 21.5 %collective-permute-start.29 = (bf16[3,512,256]{2,1,0:T(8,128)(2,1)}, bf16[3,512,256]{2,1,0:T(8,128)(2,1)}, u32[]{:S(2)}, u32[]{:S(2)}) collective-permute-start(bf16[3,512,256]{2,1,0:T(8,128)(2,1)} %get-tuple-element.206), channel_id=1, source_target_pairs={{0,12},{4,8},{8,4},{12,0},{1,13},{5,9},{9,5},{13,1},{2,14},{6,10},... | collective-permute-start | bytes 2359304 | tf_op jit(solution)/shard_map/ppermute | solution.py:76
  210.3 9.8 %copy-start.11 = (bf16[3,512,256]{2,1,0:T(8,128)(2,1)}, bf16[3,512,256]{2,1,0:T(8,128)(2,1)S(1)}, u32[]{:S(2)}) copy-start(bf16[3,512,256]{2,1,0:T(8,128)(2,1)S(1)} %collective-permute-done.32.refs_2_) | copy-start | bytes 2359300
  210.3 20.8 %collective-permute-start.34 = (bf16[3,512,256]{2,1,0:T(8,128)(2,1)S(1)}, bf16[3,512,256]{2,1,0:T(8,128)(2,1)}, u32[]{:S(2)}, u32[]{:S(2)}) collective-permute-start(bf16[3,512,256]{2,1,0:T(8,128)(2,1)S(1)} %collective-permute-done.32.refs_2_), channel_id=1, source_target_pairs={{0,16},{16,0},{1,17},{17,1},{2,18},{18,2},{3,19},{19,3},{4,20},{20... | collective-permute-start | bytes 2359304 | tf_op jit(solution)/shard_map/ppermute | solution.py:84
  229.2 20.6 %collective-permute-start.39 = (bf16[3,512,256]{2,1,0:T(8,128)(2,1)}, bf16[3,512,256]{2,1,0:T(8,128)(2,1)S(1)}, u32[]{:S(2)}, u32[]{:S(2)}) collective-permute-start(bf16[3,512,256]{2,1,0:T(8,128)(2,1)} %get-tuple-element.210), channel_id=1, source_target_pairs={{0,8},{4,12},{8,0},{12,4},{1,9},{5,13},{9,1},{13,5},{2,10},{6,14},... | collective-permute-start | bytes 2359304 | tf_op jit(solution)/shard_map/ppermute | solution.py:76
  231.1 19.6 %collective-permute-start.37 = (bf16[3,512,256]{2,1,0:T(8,128)(2,1)}, bf16[3,512,256]{2,1,0:T(8,128)(2,1)}, u32[]{:S(2)}, u32[]{:S(2)}) collective-permute-start(bf16[3,512,256]{2,1,0:T(8,128)(2,1)} %collective-permute-done.29.refs_3_), channel_id=1, source_target_pairs={{0,16},{16,0},{1,17},{17,1},{2,18},{18,2},{3,19},{19,3},{4,20},{20... | collective-permute-start | bytes 2359304 | tf_op jit(solution)/shard_map/ppermute | solution.py:84
  233.2 19.0 %collective-permute-start.35 = (bf16[3,512,256]{2,1,0:T(8,128)(2,1)}, bf16[3,512,256]{2,1,0:T(8,128)(2,1)}, u32[]{:S(2)}, u32[]{:S(2)}) collective-permute-start(bf16[3,512,256]{2,1,0:T(8,128)(2,1)} %get-tuple-element.206), channel_id=1, source_target_pairs={{0,4},{4,0},{8,12},{12,8},{1,5},{5,1},{9,13},{13,9},{2,6},{6,2},{1... | collective-permute-start | bytes 2359304 | tf_op jit(solution)/shard_map/ppermute | solution.py:76
  233.2 19.0 %collective-permute-start.36 = (bf16[3,512,256]{2,1,0:T(8,128)(2,1)}, bf16[3,512,256]{2,1,0:T(8,128)(2,1)}, u32[]{:S(2)}, u32[]{:S(2)}) collective-permute-start(bf16[3,512,256]{2,1,0:T(8,128)(2,1)} %get-tuple-element.207), channel_id=1, source_target_pairs={{0,4},{4,0},{8,12},{12,8},{1,5},{5,1},{9,13},{13,9},{2,6},{6,2},{1... | collective-permute-start | bytes 2359304 | tf_op jit(solution)/shard_map/ppermute | solution.py:76
  233.8 33.3 %collective-permute-start.38 = (bf16[3,512,256]{2,1,0:T(8,128)(2,1)}, bf16[3,512,256]{2,1,0:T(8,128)(2,1)S(1)}, u32[]{:S(2)}, u32[]{:S(2)}) collective-permute-start(bf16[3,512,256]{2,1,0:T(8,128)(2,1)} %get-tuple-element.216), channel_id=1, source_target_pairs={{0,12},{4,8},{8,4},{12,0},{1,13},{5,9},{9,5},{13,1},{2,14},{6,10},... | collective-permute-start | bytes 2359304 | tf_op jit(solution)/shard_map/ppermute | solution.py:76
  249.8 17.3 %copy-start.13 = (bf16[3,512,256]{2,1,0:T(8,128)(2,1)}, bf16[3,512,256]{2,1,0:T(8,128)(2,1)S(1)}, u32[]{:S(2)}) copy-start(bf16[3,512,256]{2,1,0:T(8,128)(2,1)S(1)} %collective-permute-done.39.refs_2_) | copy-start | bytes 2359300
  250.7 18.4 %collective-permute-start.40 = (bf16[3,512,256]{2,1,0:T(8,128)(2,1)S(1)}, bf16[3,512,256]{2,1,0:T(8,128)(2,1)S(1)}, u32[]{:S(2)}, u32[]{:S(2)}) collective-permute-start(bf16[3,512,256]{2,1,0:T(8,128)(2,1)S(1)} %collective-permute-done.39.refs_2_), channel_id=1, source_target_pairs={{0,16},{16,0},{1,17},{17,1},{2,18},{18,2},{3,19},{19,3},{4,20},{20... | collective-permute-start | bytes 2359304 | tf_op jit(solution)/shard_map/ppermute | solution.py:84
  252.3 19.3 %copy-start = (f32[1024,128]{1,0:T(8,128)S(1)}, f32[1024,128]{1,0:T(8,128)}, u32[]{:S(2)}) copy-start(f32[1024,128]{1,0:T(8,128)} %shard_map.97) | copy-start | bytes 1572868
  267.1 5.8 %copy-start.15 = (bf16[3,512,256]{2,1,0:T(8,128)(2,1)}, bf16[3,512,256]{2,1,0:T(8,128)(2,1)S(1)}, u32[]{:S(2)}) copy-start(bf16[3,512,256]{2,1,0:T(8,128)(2,1)S(1)} %collective-permute-done.38.refs_3_) | copy-start | bytes 2359300
  269.1 2.6 collective-permute-start.41
  269.1 3.7 %collective-permute-start.42 = (bf16[3,512,256]{2,1,0:T(8,128)(2,1)}, bf16[3,512,256]{2,1,0:T(8,128)(2,1)}, u32[]{:S(2)}, u32[]{:S(2)}) collective-permute-start(bf16[3,512,256]{2,1,0:T(8,128)(2,1)} %get-tuple-element.217), channel_id=1, source_target_pairs={{0,4},{4,0},{8,12},{12,8},{1,5},{5,1},{9,13},{13,9},{2,6},{6,2},{1... | collective-permute-start | bytes 2359304 | tf_op jit(solution)/shard_map/ppermute | solution.py:76
  269.7 19.4 %collective-permute-start.43 = (bf16[3,512,256]{2,1,0:T(8,128)(2,1)S(1)}, bf16[3,512,256]{2,1,0:T(8,128)(2,1)S(1)}, u32[]{:S(2)}, u32[]{:S(2)}) collective-permute-start(bf16[3,512,256]{2,1,0:T(8,128)(2,1)S(1)} %collective-permute-done.38.refs_3_), channel_id=1, source_target_pairs={{0,16},{16,0},{1,17},{17,1},{2,18},{18,2},{3,19},{19,3},{4,20},{20... | collective-permute-start | bytes 2359304 | tf_op jit(solution)/shard_map/ppermute | solution.py:84
  290.0 8.6 %copy-start.18 = (f32[1024,64]{1,0:T(8,128)S(1)}, f32[1024,64]{1,0:T(8,128)}, u32[]{:S(2)}) copy-start(f32[1024,64]{1,0:T(8,128)} %get-tuple-element.222) | copy-start | bytes 786436
  296.9 14.3 %copy-start.9 = (bf16[1,2,8,12288]{3,2,1,0:T(8,128)(2,1)S(1)}, bf16[1,2,8,12288]{3,2,1,0:T(8,128)(2,1)}, u32[]{:S(2)}) copy-start(bf16[1,2,8,12288]{3,2,1,0:T(8,128)(2,1)} %get-tuple-element.230) | copy-start | bytes 1179652
  296.9 14.3 %copy-start.20 = (bf16[2,8,12288]{2,1,0:T(8,128)(2,1)S(1)}, bf16[2,8,12288]{2,1,0:T(8,128)(2,1)}, u32[]{:S(2)}) copy-start(bf16[2,8,12288]{2,1,0:T(8,128)(2,1)} %copy-done.19) | copy-start | bytes 1179652
  302.0 1.4 collective-permute-start.44
  303.4 4.9 %collective-permute-start.45 = (f32[2,12288]{1,0:T(2,128)S(1)}, f32[2,12288]{1,0:T(2,128)S(1)}, u32[]{:S(2)}, u32[]{:S(2)}) collective-permute-start(f32[2,12288]{1,0:T(2,128)S(1)} %bitcast_add_fusion), channel_id=1, source_target_pairs={{0,1},{1,0},{2,3},{3,2},{4,5},{5,4},{6,7},{7,6},{8,9},{9,8},{10,11... | collective-permute-start | bytes 294920 | tf_op jit(solution)/shard_map/ppermute | solution.py:80
  308.4 7.2 %collective-permute-start.46 = (f32[2,12288]{1,0:T(2,128)S(1)}, f32[2,12288]{1,0:T(2,128)S(1)}, u32[]{:S(2)}, u32[]{:S(2)}) collective-permute-start(f32[2,12288]{1,0:T(2,128)S(1)} %add.75), channel_id=1, source_target_pairs={{0,2},{1,3},{2,0},{3,1},{4,6},{5,7},{6,4},{7,5},{8,10},{9,11},{10,... | collective-permute-start | bytes 294920 | tf_op jit(solution)/shard_map/ppermute | solution.py:80
  (7 other events, 23.9 us)
Sparse Core Ops, SparseCore 0:
  9.0 84.7 all-gather.4
  95.3 81.1 all-gather.6

commit v5 on v4

--- a/solution.py
+++ b/solution.py
@@ -31,7 +31,7 @@
     rank = left.shape[1]
     left_seq = left.reshape(-1, length, rank)
     right_seq = right.reshape(-1, length, rank)
-    return jnp.einsum("slr,slk->srk", left_seq, right_seq, precision=HIGHEST)
+    return jnp.einsum("slr,slk->srk", left_seq, right_seq, precision=lax.Precision.HIGH)
 
 
 def mask_tokens(out_grad, lengths):

time: 326 us -> 325 us (level)
  no operation moved by 1% of the time
where the time goes in v5:
time: 325 us; the launch traced here: 324 us
  Pallas kernels  162 us (50%)
  waiting for transfers between devices  89.6 us (28%)
  starting transfers between devices  39.1 us (12%)
  between operations  13.7 us (4%)
  local copies, waits for them, and re-layouts  8.61 us (3%)
  other arithmetic  6.07 us (2%)
  matrix products  4.39 us (1%)
    pallas_call x9, Pallas kernels, add_hidden_units(): pl.pallas_call(kernel, out_shape=out_shape, grid_spec=pltpu.PrefetchScala...  108 us
    ppermute x31, waiting for transfers between devices, permute_dp(): return lax.ppermute(value, DP, [(i, i ^ flip) for i in range(4)])  61.3 us
    pallas_call x7, Pallas kernels, cut(): pl.pallas_call(cut_kernel, out_shape=[jax.ShapeDtypeStruct((3, rows, chun...  25.8 us
    ppermute x14, waiting for transfers between devices, permute_parts(): return lax.ppermute(value, 'parts', [(0, 1), (1, 0)])  20 us
    ppermute x31, starting transfers between devices, permute_dp(): return lax.ppermute(value, DP, [(i, i ^ flip) for i in range(4)])  19.9 us
    pallas_call x2, Pallas kernels, small_call(): pl.pallas_call(kernel, out_shape=out_shape, grid_spec=pltpu.PrefetchScala...  19.7 us
    ppermute x14, starting transfers between devices, permute_parts(): return lax.ppermute(value, 'parts', [(0, 1), (1, 0)])  14.8 us
    pallas_call x1, Pallas kernels, direct(): pl.pallas_call(direct_kernel, out_shape=jax.ShapeDtypeStruct((tiles * til...  8.16 us
  transfers between devices with their start and end apart: 49, of which 20 were waited for; matrix products, arithmetic and copies ran while one was open for 4% of the time, Pallas kernels for 48%

profile of v5, /device:TPU:0, one launch (start us, length us, event | category | flops | bytes accessed | tf_op | source)
XLA Modules:
  0.0 323.8 jit_solution(4500110851926309563)
XLA Ops:
  8.0 2.3 broadcast_multiply_fusion
  10.4 3.0 collective-permute-start
  14.6 3.6 %shard_map.91 = (bf16[3,512,256]{2,1,0:T(8,128)(2,1)}, bf16[3,512,256]{2,1,0:T(8,128)(2,1)}, bf16[3,512,256]{2,1,0:T(8,128)(2,1)}) custom-call(s32[4]{0:T(128)} %get-tuple-element.237.at, bf16[1024,3584]{1,0:T(8,128)(2,1)} %w_gate.13, bf16[1024,3584]{1,0:T(8,128)(2,1)} %w_up.13, bf16[1024,3584]{1,0:T(8,128)(2,1)} %w_down.13, bf16[1024,3584]{1,0:T(8,128)(2,1)} %w_gate.13, ...), custom_call_target="tpu_custom_call" | custom-call | flops 1000 | bytes 1000 | tf_op jit(solution)/shard_map/pallas_call | solution.py:308
  18.2 0.8 collective-permute-start.2
  19.1 4.2 %shard_map.92 = (bf16[3,512,256]{2,1,0:T(8,128)(2,1)}, bf16[3,512,256]{2,1,0:T(8,128)(2,1)}, bf16[3,512,256]{2,1,0:T(8,128)(2,1)}) custom-call(s32[4]{0:T(128)} %get-tuple-element.236.at, bf16[1024,3584]{1,0:T(8,128)(2,1)} %w_gate.13, bf16[1024,3584]{1,0:T(8,128)(2,1)} %w_up.13, bf16[1024,3584]{1,0:T(8,128)(2,1)} %w_down.13, bf16[1024,3584]{1,0:T(8,128)(2,1)} %w_gate.13, ...), custom_call_target="tpu_custom_call" | custom-call | flops 1000 | bytes 1000 | tf_op jit(solution)/shard_map/pallas_call | solution.py:308
  23.3 0.9 fusion.8
  24.3 14.6 %collective-permute-done.1.refs_2_ = bf16[3,512,256]{2,1,0:T(8,128)(2,1)S(1)} collective-permute-done((bf16[3,512,256]{2,1,0:T(8,128)(2,1)}, bf16[3,512,256]{2,1,0:T(8,128)(2,1)S(1)}, u32[]{:S(2)}, u32[]{:S(2)}) %collective-permute-start.1) | collective-permute-done | bytes 786464 | tf_op jit(solution)/shard_map/ppermute | solution.py:76
  38.9 1.5 collective-permute-start.3
  40.9 3.7 %shard_map.93 = (bf16[3,512,256]{2,1,0:T(8,128)(2,1)}, bf16[3,512,256]{2,1,0:T(8,128)(2,1)}, bf16[3,512,256]{2,1,0:T(8,128)(2,1)}) custom-call(s32[4]{0:T(128)} %get-tuple-element.235.at, bf16[1024,3584]{1,0:T(8,128)(2,1)} %w_gate.13, bf16[1024,3584]{1,0:T(8,128)(2,1)} %w_up.13, bf16[1024,3584]{1,0:T(8,128)(2,1)} %w_down.13, bf16[1024,3584]{1,0:T(8,128)(2,1)} %w_gate.13, ...), custom_call_target="tpu_custom_call" | custom-call | flops 1000 | bytes 1000 | tf_op jit(solution)/shard_map/pallas_call | solution.py:308
  44.6 8.8 %collective-permute-done.2.refs_3_ = bf16[3,512,256]{2,1,0:T(8,128)(2,1)S(1)} collective-permute-done((bf16[3,512,256]{2,1,0:T(8,128)(2,1)}, bf16[3,512,256]{2,1,0:T(8,128)(2,1)S(1)}, u32[]{:S(2)}, u32[]{:S(2)}) %collective-permute-start.2) | collective-permute-done | bytes 786464 | tf_op jit(solution)/shard_map/ppermute | solution.py:76
  53.4 2.0 collective-permute-start.5
  55.4 1.8 collective-permute-start.9
  57.8 14.7 %collective-permute-done.4.refs_2_ = bf16[3,512,256]{2,1,0:T(8,128)(2,1)S(1)} collective-permute-done((bf16[3,512,256]{2,1,0:T(8,128)(2,1)}, bf16[3,512,256]{2,1,0:T(8,128)(2,1)S(1)}, u32[]{:S(2)}, u32[]{:S(2)}) %collective-permute-start.4) | collective-permute-done | bytes 786464 | tf_op jit(solution)/shard_map/ppermute | solution.py:76
  72.6 3.5 %shard_map.94 = (bf16[3,512,256]{2,1,0:T(8,128)(2,1)}, bf16[3,512,256]{2,1,0:T(8,128)(2,1)}, bf16[3,512,256]{2,1,0:T(8,128)(2,1)}) custom-call(s32[4]{0:T(128)} %get-tuple-element.234.at, bf16[1024,3584]{1,0:T(8,128)(2,1)} %w_gate.13, bf16[1024,3584]{1,0:T(8,128)(2,1)} %w_up.13, bf16[1024,3584]{1,0:T(8,128)(2,1)} %w_down.13, bf16[1024,3584]{1,0:T(8,128)(2,1)} %w_gate.13, ...), custom_call_target="tpu_custom_call" | custom-call | flops 1000 | bytes 1000 | tf_op jit(solution)/shard_map/pallas_call | solution.py:308
  76.1 1.6 collective-permute-start.10
  78.3 3.6 %shard_map.95 = (bf16[3,512,256]{2,1,0:T(8,128)(2,1)}, bf16[3,512,256]{2,1,0:T(8,128)(2,1)}, bf16[3,512,256]{2,1,0:T(8,128)(2,1)}) custom-call(s32[4]{0:T(128)} %get-tuple-element.233.at, bf16[1024,3584]{1,0:T(8,128)(2,1)} %w_gate.13, bf16[1024,3584]{1,0:T(8,128)(2,1)} %w_up.13, bf16[1024,3584]{1,0:T(8,128)(2,1)} %w_down.13, bf16[1024,3584]{1,0:T(8,128)(2,1)} %w_gate.13, ...), custom_call_target="tpu_custom_call" | custom-call | flops 1000 | bytes 1000 | tf_op jit(solution)/shard_map/pallas_call | solution.py:308
  81.9 5.2 %collective-permute-done.6.refs_3_ = bf16[3,512,256]{2,1,0:T(8,128)(2,1)S(1)} collective-permute-done((bf16[3,512,256]{2,1,0:T(8,128)(2,1)}, bf16[3,512,256]{2,1,0:T(8,128)(2,1)S(1)}, u32[]{:S(2)}, u32[]{:S(2)}) %collective-permute-start.6) | collective-permute-done | bytes 786464 | tf_op jit(solution)/shard_map/ppermute | solution.py:76
  87.1 2.6 collective-permute-start.14
  89.8 1.5 collective-permute-start.12
  91.3 5.3 %collective-permute-done.10.refs_4_ = bf16[3,512,256]{2,1,0:T(8,128)(2,1)} collective-permute-done((bf16[3,512,256]{2,1,0:T(8,128)(2,1)S(1)}, bf16[3,512,256]{2,1,0:T(8,128)(2,1)}, u32[]{:S(2)}, u32[]{:S(2)}) %collective-permute-start.10) | collective-permute-done | bytes 786464 | tf_op jit(solution)/shard_map/ppermute | solution.py:84
  96.7 3.6 %shard_map.96 = (bf16[3,512,256]{2,1,0:T(8,128)(2,1)}, bf16[3,512,256]{2,1,0:T(8,128)(2,1)}, bf16[3,512,256]{2,1,0:T(8,128)(2,1)}) custom-call(s32[4]{0:T(128)} %get-tuple-element.232.at, bf16[1024,3584]{1,0:T(8,128)(2,1)} %w_gate.13, bf16[1024,3584]{1,0:T(8,128)(2,1)} %w_up.13, bf16[1024,3584]{1,0:T(8,128)(2,1)} %w_down.13, bf16[1024,3584]{1,0:T(8,128)(2,1)} %w_gate.13, ...), custom_call_target="tpu_custom_call" | custom-call | flops 1000 | bytes 1000 | tf_op jit(solution)/shard_map/pallas_call | solution.py:308
  100.2 6.0 %collective-permute-done.11.refs_2_ = bf16[3,512,256]{2,1,0:T(8,128)(2,1)S(1)} collective-permute-done((bf16[3,512,256]{2,1,0:T(8,128)(2,1)}, bf16[3,512,256]{2,1,0:T(8,128)(2,1)S(1)}, u32[]{:S(2)}, u32[]{:S(2)}) %collective-permute-start.11) | collective-permute-done | bytes 786464 | tf_op jit(solution)/shard_map/ppermute | solution.py:76
  106.3 1.5 collective-permute-start.18
  108.5 3.6 %shard_map.99 = (bf16[3,512,256]{2,1,0:T(8,128)(2,1)}, bf16[3,512,256]{2,1,0:T(8,128)(2,1)}, bf16[3,512,256]{2,1,0:T(8,128)(2,1)}) custom-call(s32[4]{0:T(128)} %get-tuple-element.223.at, bf16[1024,3584]{1,0:T(8,128)(2,1)} %w_gate.13, bf16[1024,3584]{1,0:T(8,128)(2,1)} %w_up.13, bf16[1024,3584]{1,0:T(8,128)(2,1)} %w_down.13, bf16[1024,3584]{1,0:T(8,128)(2,1)} %w_gate.13, ...), custom_call_target="tpu_custom_call" | custom-call | flops 1000 | bytes 1000 | tf_op jit(solution)/shard_map/pallas_call | solution.py:308
  112.1 1.1 broadcast_in_dim.5.refs_7_
  113.2 10.8 %shard_map.98 = (f32[1024,192]{1,0:T(8,128)}, f32[1024,256]{1,0:T(8,128)}, f32[1024,256]{1,0:T(8,128)}) custom-call(s32[8]{0:T(128)} %stack.139.places, bf16[8,512,1024]{2,1,0:T(8,128)(2,1)} %bitcast.73, bf16[1024,3584]{1,0:T(8,128)(2,1)} %w_gate.13, bf16[1024,3584]{1,0:T(8,128)(2,1)} %w_up.13, ...), custom_call_target="tpu_custom_call", output_to_operand_aliasing={{0}: (11, {})} | custom-call | flops 1000 | bytes 1000 | tf_op jit(solution)/shard_map/pallas_call | solution.py:275
  125.2 5.2 %collective-permute-done.18.refs_4_ = bf16[3,512,256]{2,1,0:T(8,128)(2,1)} collective-permute-done((bf16[3,512,256]{2,1,0:T(8,128)(2,1)S(1)}, bf16[3,512,256]{2,1,0:T(8,128)(2,1)}, u32[]{:S(2)}, u32[]{:S(2)}) %collective-permute-start.18) | collective-permute-done | bytes 786464 | tf_op jit(solution)/shard_map/ppermute | solution.py:84
  131.0 10.9 %shard_map.100 = (f32[1024,192]{1,0:T(8,128)}, f32[1024,256]{1,0:T(8,128)}, f32[1024,256]{1,0:T(8,128)}) custom-call(s32[8]{0:T(128)} %stack.283.places, bf16[8,512,1024]{2,1,0:T(8,128)(2,1)} %bitcast.74, bf16[1024,3584]{1,0:T(8,128)(2,1)} %w_gate.13, bf16[1024,3584]{1,0:T(8,128)(2,1)} %w_up.13, ...), custom_call_target="tpu_custom_call", output_to_operand_aliasing={{0}: (11, {})} | custom-call | flops 1000 | bytes 1000 | tf_op jit(solution)/shard_map/pallas_call | solution.py:275
  141.9 3.0 collective-permute-done.20.refs_2_
  145.3 8.2 %shard_map.97 = f32[1024,128]{1,0:T(8,128)} custom-call(bf16[8,512,1024]{2,1,0:T(8,128)(2,1)} %bitcast.75, bf16[3,64,4096]{2,1,0:T(8,128)(2,1)} %bitcast.100), custom_call_target="tpu_custom_call" | custom-call | flops 1000 | bytes 1000 | tf_op jit(solution)/shard_map/pallas_call | solution.py:131
  153.6 3.6 %collective-permute-done.23.refs_3_ = bf16[3,512,256]{2,1,0:T(8,128)(2,1)} collective-permute-done((bf16[3,512,256]{2,1,0:T(8,128)(2,1)}, bf16[3,512,256]{2,1,0:T(8,128)(2,1)}, u32[]{:S(2)}, u32[]{:S(2)}) %collective-permute-start.23) | collective-permute-done | bytes 786464 | tf_op jit(solution)/shard_map/ppermute | solution.py:76
  157.2 2.9 collective-permute-start.24
  160.1 0.7 collective-permute-start.26
  160.9 2.8 collective-permute-done.21.refs_4_
  164.4 10.6 %shard_map.101 = (f32[1024,192]{1,0:T(8,128)}, f32[1024,256]{1,0:T(8,128)}, f32[1024,256]{1,0:T(8,128)}) custom-call(s32[8]{0:T(128)} %stack.138.places, bf16[8,512,1024]{2,1,0:T(8,128)(2,1)} %bitcast.76, bf16[1024,3584]{1,0:T(8,128)(2,1)} %w_gate.13, bf16[1024,3584]{1,0:T(8,128)(2,1)} %w_up.13, ...), custom_call_target="tpu_custom_call", output_to_operand_aliasing={{0}: (11, {})} | custom-call | flops 1000 | bytes 1000 | tf_op jit(solution)/shard_map/pallas_call | solution.py:275
  175.0 1.8 collective-permute-done.22.refs_2_
  178.2 13.9 %shard_map.102 = (f32[1024,192]{1,0:T(8,128)}, f32[1024,64]{1,0:T(8,128)}) custom-call(s32[8]{0:T(128)} %stack.139.places, bf16[8,512,1024]{2,1,0:T(8,128)(2,1)} %bitcast.82, bf16[1024,3584]{1,0:T(8,128)(2,1)} %w_down.13, bf16[3,512,256]{2,1,0:T(8,128)(2,1)} %collective-permute-done.7.refs_0_, ...), custom_call_target="tpu_custom_call", output_to_operand_aliasing={{0}: (13, {})} | custom-call | flops 1000 | bytes 1000 | tf_op jit(solution)/shard_map/pallas_call | solution.py:275
  192.2 1.7 collective-permute-start.30
  194.6 14.8 %shard_map.103.refs_9_ = f32[1024,192]{1,0:T(8,128)} custom-call(s32[8]{0:T(128)} %stack.286.places, bf16[8,512,1024]{2,1,0:T(8,128)(2,1)} %bitcast.77, bf16[8,512,1024]{2,1,0:T(8,128)(2,1)} %bitcast.83, bf16[1024,3584]{1,0:T(8,128)(2,1)} %w_gate.13, bf16[1024,3584]{1,0:T(8,128)(2,1)} %w_up.13, ...), custom_call_target="tpu_custom_call", output_to_operand_aliasing={{}: (13, {})} | custom-call | flops 1000 | bytes 1000 | tf_op jit(solution)/shard_map/pallas_call | solution.py:275
  209.4 0.8 collective-permute-start.29
  210.3 0.8 collective-permute-start.34
  211.0 9.1 %shard_map.104.refs_9_ = f32[1024,192]{1,0:T(8,128)} custom-call(s32[8]{0:T(128)} %stack.283.places, bf16[8,512,1024]{2,1,0:T(8,128)(2,1)} %bitcast.84, bf16[1024,3584]{1,0:T(8,128)(2,1)} %w_down.13, bf16[3,512,256]{2,1,0:T(8,128)(2,1)} %copy-done.6, bf16[3,512,256]{2,1,0:T(8,128)(2,1)} %collective-permute-done.15.refs_1_, ...), custom_call_target="tpu_custom_call", output_to_operand_aliasing={{}: (12, {})} | custom-call | flops 1000 | bytes 1000 | tf_op jit(solution)/shard_map/pallas_call | solution.py:275
  220.1 9.1 %shard_map.105.refs_7_ = f32[1024,192]{1,0:T(8,128)} custom-call(s32[8]{0:T(128)} %stack.138.places, bf16[8,512,1024]{2,1,0:T(8,128)(2,1)} %bitcast.85, bf16[1024,3584]{1,0:T(8,128)(2,1)} %w_down.13, bf16[3,512,256]{2,1,0:T(8,128)(2,1)} %copy-done.8, bf16[3,512,256]{2,1,0:T(8,128)(2,1)} %collective-permute-done.17.refs_1_, ...), custom_call_target="tpu_custom_call", output_to_operand_aliasing={{}: (12, {})} | custom-call | flops 1000 | bytes 1000 | tf_op jit(solution)/shard_map/pallas_call | solution.py:275
  229.2 1.7 collective-permute-start.39
  231.1 1.5 collective-permute-start.37
  233.9 14.6 %shard_map.106.refs_7_ = f32[1024,192]{1,0:T(8,128)} custom-call(s32[8]{0:T(128)} %stack.287.places, bf16[8,512,1024]{2,1,0:T(8,128)(2,1)} %bitcast.78, bf16[8,512,1024]{2,1,0:T(8,128)(2,1)} %bitcast.86, bf16[1024,3584]{1,0:T(8,128)(2,1)} %w_gate.13, bf16[1024,3584]{1,0:T(8,128)(2,1)} %w_up.13, ...), custom_call_target="tpu_custom_call", output_to_operand_aliasing={{}: (13, {})} | custom-call | flops 1000 | bytes 1000 | tf_op jit(solution)/shard_map/pallas_call | solution.py:275
  248.5 1.3 collective-permute-done.39.refs_2_
  249.8 0.9 collective-permute-done.37.refs_5_
  250.7 0.9 collective-permute-start.40
  252.3 14.8 %shard_map.107.sums_in = f32[1024,192]{1,0:T(8,128)} custom-call(s32[8]{0:T(128)} %stack.285.places, bf16[8,512,1024]{2,1,0:T(8,128)(2,1)} %bitcast.79, bf16[8,512,1024]{2,1,0:T(8,128)(2,1)} %bitcast.87, bf16[1024,3584]{1,0:T(8,128)(2,1)} %w_gate.13, bf16[1024,3584]{1,0:T(8,128)(2,1)} %w_up.13, ...), custom_call_target="tpu_custom_call", output_to_operand_aliasing={{}: (13, {})} | custom-call | flops 1000 | bytes 1000 | tf_op jit(solution)/shard_map/pallas_call | solution.py:275
  267.1 2.1 collective-permute-done.40.refs_4_
  271.8 1.1 collective-permute-done.42.refs_1_
  272.9 12.8 %shard_map.108 = (f32[1024,256]{1,0:T(8,128)}, f32[1024,256]{1,0:T(8,128)}, f32[1024,256]{1,0:T(8,128)}) custom-call(s32[8]{0:T(128)} %stack.284.places, bf16[8,512,1024]{2,1,0:T(8,128)(2,1)} %bitcast.80, bf16[8,512,1024]{2,1,0:T(8,128)(2,1)} %bitcast.88, bf16[1024,3584]{1,0:T(8,128)(2,1)} %w_gate.13, bf16[1024,3584]{1,0:T(8,128)(2,1)} %w_up.13, ...), custom_call_target="tpu_custom_call" | custom-call | flops 1000 | bytes 1000 | tf_op jit(solution)/shard_map/pallas_call | solution.py:197
  285.7 3.4 %collective-permute-done.43.piece = bf16[3,512,256]{2,1,0:T(8,128)(2,1)S(1)} collective-permute-done((bf16[3,512,256]{2,1,0:T(8,128)(2,1)S(1)}, bf16[3,512,256]{2,1,0:T(8,128)(2,1)S(1)}, u32[]{:S(2)}, u32[]{:S(2)}) %collective-permute-start.43) | collective-permute-done | bytes 786464 | tf_op jit(solution)/shard_map/ppermute | solution.py:84
  289.1 0.9 copy-done.17
  290.0 6.9 %shard_map.109 = f32[1024,192]{1,0:T(8,128)} custom-call(s32[2]{0:T(128)} %pad_add_fusion.7.places, bf16[8,512,1024]{2,1,0:T(8,128)(2,1)} %bitcast.81, bf16[8,512,1024]{2,1,0:T(8,128)(2,1)} %bitcast.89, f32[1024,256]{1,0:T(8,128)} %get-tuple-element.218.gate_in, f32[1024,256]{1,0:T(8,128)} %get-tuple-element.219.up_in, ...), custom_call_target="tpu_custom_call", output_to_operand_aliasing={{}: (8, {})} | custom-call | flops 1000 | bytes 1000 | tf_op jit(solution)/shard_map/pallas_call | solution.py:197
  296.9 1.6 fusion.9
  300.8 1.3 collective-permute-done.44
  302.1 1.6 collective-permute-start.45
  303.8 3.2 collective-permute-done.45
  307.1 2.8 collective-permute-start.46
  310.0 4.3 %collective-permute-done.46 = f32[2,12288]{1,0:T(2,128)S(1)} collective-permute-done((f32[2,12288]{1,0:T(2,128)S(1)}, f32[2,12288]{1,0:T(2,128)S(1)}, u32[]{:S(2)}, u32[]{:S(2)}) %collective-permute-start.46) | collective-permute-done | bytes 98336 | tf_op jit(solution)/shard_map/ppermute | solution.py:80
  314.4 1.8 fusion.1
  316.2 0.7 convolution_bitcast_fusion.3
  (129 shorter events, 17.7 us)
Async XLA Ops:
  6.5 105.6 %all-gather.5.cloned.1.call-start = ((), (), s32[]{:S(2)}) async-start(), calls=%async_computation | async-start | bytes 9437184 | tf_op jit(solution)/shard_map/all_gather | solution.py:370
  7.3 171.0 %all-gather.7.cloned.1.call-start = ((), (), s32[]{:S(2)}) async-start(), calls=%async_computation.1 | async-start | bytes 9437184 | tf_op jit(solution)/shard_map/all_gather | solution.py:371
  10.4 12.9 %collective-permute-start = (bf16[8,12288]{1,0:T(8,128)(2,1)}, bf16[8,12288]{1,0:T(8,128)(2,1)S(1)}, u32[]{:S(2)}, u32[]{:S(2)}) collective-permute-start(bf16[8,12288]{1,0:T(8,128)(2,1)} %param.17), channel_id=1, source_target_pairs={{0,8},{4,12},{8,0},{12,4},{1,9},{5,13},{9,1},{13,5},{2,10},{6,14},... | collective-permute-start | bytes 589832 | tf_op jit(solution)/shard_map/ppermute | solution.py:76
  18.2 20.7 %collective-permute-start.1 = (bf16[3,512,256]{2,1,0:T(8,128)(2,1)}, bf16[3,512,256]{2,1,0:T(8,128)(2,1)S(1)}, u32[]{:S(2)}, u32[]{:S(2)}) collective-permute-start(bf16[3,512,256]{2,1,0:T(8,128)(2,1)} %get-tuple-element.114), channel_id=1, source_target_pairs={{0,8},{4,12},{8,0},{12,4},{1,9},{5,13},{9,1},{13,5},{2,10},{6,14},... | collective-permute-start | bytes 2359304 | tf_op jit(solution)/shard_map/ppermute | solution.py:76
  18.2 35.1 %collective-permute-start.2 = (bf16[3,512,256]{2,1,0:T(8,128)(2,1)}, bf16[3,512,256]{2,1,0:T(8,128)(2,1)S(1)}, u32[]{:S(2)}, u32[]{:S(2)}) collective-permute-start(bf16[3,512,256]{2,1,0:T(8,128)(2,1)} %get-tuple-element.138), channel_id=1, source_target_pairs={{0,12},{4,8},{8,4},{12,0},{1,13},{5,9},{9,5},{13,1},{2,14},{6,10},... | collective-permute-start | bytes 2359304 | tf_op jit(solution)/shard_map/ppermute | solution.py:76
  38.9 18.5 %collective-permute-start.3 = (bf16[3,512,256]{2,1,0:T(8,128)(2,1)S(1)}, bf16[3,512,256]{2,1,0:T(8,128)(2,1)}, u32[]{:S(2)}, u32[]{:S(2)}) collective-permute-start(bf16[3,512,256]{2,1,0:T(8,128)(2,1)S(1)} %collective-permute-done.1.refs_2_), channel_id=1, source_target_pairs={{0,16},{16,0},{1,17},{17,1},{2,18},{18,2},{3,19},{19,3},{4,20},{20... | collective-permute-start | bytes 2359304 | tf_op jit(solution)/shard_map/ppermute | solution.py:84
  40.4 32.2 %collective-permute-start.4 = (bf16[3,512,256]{2,1,0:T(8,128)(2,1)}, bf16[3,512,256]{2,1,0:T(8,128)(2,1)S(1)}, u32[]{:S(2)}, u32[]{:S(2)}) collective-permute-start(bf16[3,512,256]{2,1,0:T(8,128)(2,1)} %get-tuple-element.128), channel_id=1, source_target_pairs={{0,8},{4,12},{8,0},{12,4},{1,9},{5,13},{9,1},{13,5},{2,10},{6,14},... | collective-permute-start | bytes 2359304 | tf_op jit(solution)/shard_map/ppermute | solution.py:76
  53.3 22.8 %copy-start.4 = (bf16[3,512,256]{2,1,0:T(8,128)(2,1)}, bf16[3,512,256]{2,1,0:T(8,128)(2,1)S(1)}, u32[]{:S(2)}) copy-start(bf16[3,512,256]{2,1,0:T(8,128)(2,1)S(1)} %collective-permute-done.2.refs_3_) | copy-start | bytes 2359300
  53.4 24.4 %collective-permute-start.5 = (bf16[3,512,256]{2,1,0:T(8,128)(2,1)S(1)}, bf16[3,512,256]{2,1,0:T(8,128)(2,1)}, u32[]{:S(2)}, u32[]{:S(2)}) collective-permute-start(bf16[3,512,256]{2,1,0:T(8,128)(2,1)S(1)} %collective-permute-done.2.refs_3_), channel_id=1, source_target_pairs={{0,16},{16,0},{1,17},{17,1},{2,18},{18,2},{3,19},{19,3},{4,20},{20... | collective-permute-start | bytes 2359304 | tf_op jit(solution)/shard_map/ppermute | solution.py:84
  55.4 20.7 %collective-permute-start.9 = (bf16[2,8,12288]{2,1,0:T(8,128)(2,1)}, bf16[2,8,12288]{2,1,0:T(8,128)(2,1)S(1)}, u32[]{:S(2)}, u32[]{:S(2)}) collective-permute-start(bf16[2,8,12288]{2,1,0:T(8,128)(2,1)} %get-tuple-element.141), channel_id=1, source_target_pairs={{0,4},{4,0},{8,12},{12,8},{1,5},{5,1},{9,13},{13,9},{2,6},{6,2},{1... | collective-permute-start | bytes 1179656 | tf_op jit(solution)/shard_map/ppermute | solution.py:76
  57.2 29.9 %collective-permute-start.6 = (bf16[3,512,256]{2,1,0:T(8,128)(2,1)}, bf16[3,512,256]{2,1,0:T(8,128)(2,1)S(1)}, u32[]{:S(2)}, u32[]{:S(2)}) collective-permute-start(bf16[3,512,256]{2,1,0:T(8,128)(2,1)} %get-tuple-element.162), channel_id=1, source_target_pairs={{0,12},{4,8},{8,4},{12,0},{1,13},{5,9},{9,5},{13,1},{2,14},{6,10},... | collective-permute-start | bytes 2359304 | tf_op jit(solution)/shard_map/ppermute | solution.py:76
  57.3 29.7 %collective-permute-start.7 = (bf16[3,512,256]{2,1,0:T(8,128)(2,1)}, bf16[3,512,256]{2,1,0:T(8,128)(2,1)}, u32[]{:S(2)}, u32[]{:S(2)}) collective-permute-start(bf16[3,512,256]{2,1,0:T(8,128)(2,1)} %get-tuple-element.138), channel_id=1, source_target_pairs={{0,4},{4,0},{8,12},{12,8},{1,5},{5,1},{9,13},{13,9},{2,6},{6,2},{1... | collective-permute-start | bytes 2359304 | tf_op jit(solution)/shard_map/ppermute | solution.py:76
  72.6 14.5 %collective-permute-start.8 = (bf16[3,512,256]{2,1,0:T(8,128)(2,1)}, bf16[3,512,256]{2,1,0:T(8,128)(2,1)}, u32[]{:S(2)}, u32[]{:S(2)}) collective-permute-start(bf16[3,512,256]{2,1,0:T(8,128)(2,1)} %get-tuple-element.140), channel_id=1, source_target_pairs={{0,4},{4,0},{8,12},{12,8},{1,5},{5,1},{9,13},{13,9},{2,6},{6,2},{1... | collective-permute-start | bytes 2359304 | tf_op jit(solution)/shard_map/ppermute | solution.py:76
  76.1 20.5 %collective-permute-start.10 = (bf16[3,512,256]{2,1,0:T(8,128)(2,1)S(1)}, bf16[3,512,256]{2,1,0:T(8,128)(2,1)}, u32[]{:S(2)}, u32[]{:S(2)}) collective-permute-start(bf16[3,512,256]{2,1,0:T(8,128)(2,1)S(1)} %collective-permute-done.4.refs_2_), channel_id=1, source_target_pairs={{0,16},{16,0},{1,17},{17,1},{2,18},{18,2},{3,19},{19,3},{4,20},{20... | collective-permute-start | bytes 2359304 | tf_op jit(solution)/shard_map/ppermute | solution.py:84
  77.7 28.5 %collective-permute-start.11 = (bf16[3,512,256]{2,1,0:T(8,128)(2,1)}, bf16[3,512,256]{2,1,0:T(8,128)(2,1)S(1)}, u32[]{:S(2)}, u32[]{:S(2)}) collective-permute-start(bf16[3,512,256]{2,1,0:T(8,128)(2,1)} %get-tuple-element.150), channel_id=1, source_target_pairs={{0,8},{4,12},{8,0},{12,4},{1,9},{5,13},{9,1},{13,5},{2,10},{6,14},... | collective-permute-start | bytes 2359304 | tf_op jit(solution)/shard_map/ppermute | solution.py:76
  87.1 13.2 %copy-start.2 = (bf16[3,512,256]{2,1,0:T(8,128)(2,1)}, bf16[3,512,256]{2,1,0:T(8,128)(2,1)S(1)}, u32[]{:S(2)}) copy-start(bf16[3,512,256]{2,1,0:T(8,128)(2,1)S(1)} %collective-permute-done.6.refs_3_) | copy-start | bytes 2359300
  87.1 37.0 %collective-permute-start.14 = (bf16[3,512,256]{2,1,0:T(8,128)(2,1)}, bf16[3,512,256]{2,1,0:T(8,128)(2,1)S(1)}, u32[]{:S(2)}, u32[]{:S(2)}) collective-permute-start(bf16[3,512,256]{2,1,0:T(8,128)(2,1)} %get-tuple-element.162), channel_id=1, source_target_pairs={{0,4},{4,0},{8,12},{12,8},{1,5},{5,1},{9,13},{13,9},{2,6},{6,2},{1... | collective-permute-start | bytes 2359304 | tf_op jit(solution)/shard_map/ppermute | solution.py:76
  89.7 34.9 %collective-permute-start.15 = (bf16[3,512,256]{2,1,0:T(8,128)(2,1)}, bf16[3,512,256]{2,1,0:T(8,128)(2,1)}, u32[]{:S(2)}, u32[]{:S(2)}) collective-permute-start(bf16[3,512,256]{2,1,0:T(8,128)(2,1)} %get-tuple-element.163), channel_id=1, source_target_pairs={{0,4},{4,0},{8,12},{12,8},{1,5},{5,1},{9,13},{13,9},{2,6},{6,2},{1... | collective-permute-start | bytes 2359304 | tf_op jit(solution)/shard_map/ppermute | solution.py:76
  89.8 34.8 %collective-permute-start.12 = (bf16[3,512,256]{2,1,0:T(8,128)(2,1)S(1)}, bf16[3,512,256]{2,1,0:T(8,128)(2,1)}, u32[]{:S(2)}, u32[]{:S(2)}) collective-permute-start(bf16[3,512,256]{2,1,0:T(8,128)(2,1)S(1)} %collective-permute-done.6.refs_3_), channel_id=1, source_target_pairs={{0,16},{16,0},{1,17},{17,1},{2,18},{18,2},{3,19},{19,3},{4,20},{20... | collective-permute-start | bytes 2359304 | tf_op jit(solution)/shard_map/ppermute | solution.py:84
  96.7 27.9 %collective-permute-start.13 = (bf16[3,512,256]{2,1,0:T(8,128)(2,1)}, bf16[3,512,256]{2,1,0:T(8,128)(2,1)S(1)}, u32[]{:S(2)}, u32[]{:S(2)}) collective-permute-start(bf16[3,512,256]{2,1,0:T(8,128)(2,1)} %get-tuple-element.171), channel_id=1, source_target_pairs={{0,12},{4,8},{8,4},{12,0},{1,13},{5,9},{9,5},{13,1},{2,14},{6,10},... | collective-permute-start | bytes 2359304 | tf_op jit(solution)/shard_map/ppermute | solution.py:76
  106.3 5.8 %copy-start.5 = (bf16[3,512,256]{2,1,0:T(8,128)(2,1)}, bf16[3,512,256]{2,1,0:T(8,128)(2,1)S(1)}, u32[]{:S(2)}) copy-start(bf16[3,512,256]{2,1,0:T(8,128)(2,1)S(1)} %collective-permute-done.11.refs_2_) | copy-start | bytes 2359300
  106.3 24.1 %collective-permute-start.18 = (bf16[3,512,256]{2,1,0:T(8,128)(2,1)S(1)}, bf16[3,512,256]{2,1,0:T(8,128)(2,1)}, u32[]{:S(2)}, u32[]{:S(2)}) collective-permute-start(bf16[3,512,256]{2,1,0:T(8,128)(2,1)S(1)} %collective-permute-done.11.refs_2_), channel_id=1, source_target_pairs={{0,16},{16,0},{1,17},{17,1},{2,18},{18,2},{3,19},{19,3},{4,20},{20... | collective-permute-start | bytes 2359304 | tf_op jit(solution)/shard_map/ppermute | solution.py:84
  124.0 7.0 %copy-start.6 = (bf16[3,512,256]{2,1,0:T(8,128)(2,1)}, bf16[3,512,256]{2,1,0:T(8,128)(2,1)S(1)}, u32[]{:S(2)}) copy-start(bf16[3,512,256]{2,1,0:T(8,128)(2,1)S(1)} %collective-permute-done.14.refs_0_) | copy-start | bytes 2359300
  124.0 20.9 %collective-permute-start.20 = (bf16[3,512,256]{2,1,0:T(8,128)(2,1)}, bf16[3,512,256]{2,1,0:T(8,128)(2,1)}, u32[]{:S(2)}, u32[]{:S(2)}) collective-permute-start(bf16[3,512,256]{2,1,0:T(8,128)(2,1)} %get-tuple-element.177), channel_id=1, source_target_pairs={{0,8},{4,12},{8,0},{12,4},{1,9},{5,13},{9,1},{13,5},{2,10},{6,14},... | collective-permute-start | bytes 2359304 | tf_op jit(solution)/shard_map/ppermute | solution.py:76
  124.6 17.3 %copy-start.7 = (bf16[3,512,256]{2,1,0:T(8,128)(2,1)}, bf16[3,512,256]{2,1,0:T(8,128)(2,1)S(1)}, u32[]{:S(2)}) copy-start(bf16[3,512,256]{2,1,0:T(8,128)(2,1)S(1)} %collective-permute-done.13.refs_3_) | copy-start | bytes 2359300
  124.6 28.9 %collective-permute-start.16 = (bf16[3,512,256]{2,1,0:T(8,128)(2,1)}, bf16[3,512,256]{2,1,0:T(8,128)(2,1)S(1)}, u32[]{:S(2)}, u32[]{:S(2)}) collective-permute-start(bf16[3,512,256]{2,1,0:T(8,128)(2,1)} %get-tuple-element.171), channel_id=1, source_target_pairs={{0,4},{4,0},{8,12},{12,8},{1,5},{5,1},{9,13},{13,9},{2,6},{6,2},{1... | collective-permute-start | bytes 2359304 | tf_op jit(solution)/shard_map/ppermute | solution.py:76
  124.7 29.0 %collective-permute-start.17 = (bf16[3,512,256]{2,1,0:T(8,128)(2,1)}, bf16[3,512,256]{2,1,0:T(8,128)(2,1)}, u32[]{:S(2)}, u32[]{:S(2)}) collective-permute-start(bf16[3,512,256]{2,1,0:T(8,128)(2,1)} %get-tuple-element.172), channel_id=1, source_target_pairs={{0,4},{4,0},{8,12},{12,8},{1,5},{5,1},{9,13},{13,9},{2,6},{6,2},{1... | collective-permute-start | bytes 2359304 | tf_op jit(solution)/shard_map/ppermute | solution.py:76
  125.2 28.5 %collective-permute-start.19 = (bf16[3,512,256]{2,1,0:T(8,128)(2,1)S(1)}, bf16[3,512,256]{2,1,0:T(8,128)(2,1)}, u32[]{:S(2)}, u32[]{:S(2)}) collective-permute-start(bf16[3,512,256]{2,1,0:T(8,128)(2,1)S(1)} %collective-permute-done.13.refs_3_), channel_id=1, source_target_pairs={{0,16},{16,0},{1,17},{17,1},{2,18},{18,2},{3,19},{19,3},{4,20},{20... | collective-permute-start | bytes 2359304 | tf_op jit(solution)/shard_map/ppermute | solution.py:84
  130.4 26.8 %collective-permute-start.23 = (bf16[3,512,256]{2,1,0:T(8,128)(2,1)}, bf16[3,512,256]{2,1,0:T(8,128)(2,1)}, u32[]{:S(2)}, u32[]{:S(2)}) collective-permute-start(bf16[3,512,256]{2,1,0:T(8,128)(2,1)} %get-tuple-element.189), channel_id=1, source_target_pairs={{0,12},{4,8},{8,4},{12,0},{1,13},{5,9},{9,5},{13,1},{2,14},{6,10},... | collective-permute-start | bytes 2359304 | tf_op jit(solution)/shard_map/ppermute | solution.py:76
  144.9 18.8 %collective-permute-start.21 = (bf16[3,512,256]{2,1,0:T(8,128)(2,1)}, bf16[3,512,256]{2,1,0:T(8,128)(2,1)}, u32[]{:S(2)}, u32[]{:S(2)}) collective-permute-start(bf16[3,512,256]{2,1,0:T(8,128)(2,1)} %collective-permute-done.20.refs_2_), channel_id=1, source_target_pairs={{0,16},{16,0},{1,17},{17,1},{2,18},{18,2},{3,19},{19,3},{4,20},{20... | collective-permute-start | bytes 2359304 | tf_op jit(solution)/shard_map/ppermute | solution.py:84
  153.5 10.9 %copy-start.8 = (bf16[3,512,256]{2,1,0:T(8,128)(2,1)}, bf16[3,512,256]{2,1,0:T(8,128)(2,1)S(1)}, u32[]{:S(2)}) copy-start(bf16[3,512,256]{2,1,0:T(8,128)(2,1)S(1)} %collective-permute-done.16.refs_0_) | copy-start | bytes 2359300
  153.5 23.3 %collective-permute-start.22 = (bf16[3,512,256]{2,1,0:T(8,128)(2,1)}, bf16[3,512,256]{2,1,0:T(8,128)(2,1)S(1)}, u32[]{:S(2)}, u32[]{:S(2)}) collective-permute-start(bf16[3,512,256]{2,1,0:T(8,128)(2,1)} %get-tuple-element.180), channel_id=1, source_target_pairs={{0,8},{4,12},{8,0},{12,4},{1,9},{5,13},{9,1},{13,5},{2,10},{6,14},... | collective-permute-start | bytes 2359304 | tf_op jit(solution)/shard_map/ppermute | solution.py:76
  157.2 20.3 %collective-permute-start.24 = (bf16[3,512,256]{2,1,0:T(8,128)(2,1)}, bf16[3,512,256]{2,1,0:T(8,128)(2,1)}, u32[]{:S(2)}, u32[]{:S(2)}) collective-permute-start(bf16[3,512,256]{2,1,0:T(8,128)(2,1)} %get-tuple-element.189), channel_id=1, source_target_pairs={{0,4},{4,0},{8,12},{12,8},{1,5},{5,1},{9,13},{13,9},{2,6},{6,2},{1... | collective-permute-start | bytes 2359304 | tf_op jit(solution)/shard_map/ppermute | solution.py:76
  160.1 32.0 %collective-permute-start.25 = (bf16[3,512,256]{2,1,0:T(8,128)(2,1)}, bf16[3,512,256]{2,1,0:T(8,128)(2,1)}, u32[]{:S(2)}, u32[]{:S(2)}) collective-permute-start(bf16[3,512,256]{2,1,0:T(8,128)(2,1)} %get-tuple-element.190), channel_id=1, source_target_pairs={{0,4},{4,0},{8,12},{12,8},{1,5},{5,1},{9,13},{13,9},{2,6},{6,2},{1... | collective-permute-start | bytes 2359304 | tf_op jit(solution)/shard_map/ppermute | solution.py:76
  160.1 32.0 %collective-permute-start.26 = (bf16[3,512,256]{2,1,0:T(8,128)(2,1)}, bf16[3,512,256]{2,1,0:T(8,128)(2,1)}, u32[]{:S(2)}, u32[]{:S(2)}) collective-permute-start(bf16[3,512,256]{2,1,0:T(8,128)(2,1)} %collective-permute-done.23.refs_3_), channel_id=1, source_target_pairs={{0,16},{16,0},{1,17},{17,1},{2,18},{18,2},{3,19},{19,3},{4,20},{20... | collective-permute-start | bytes 2359304 | tf_op jit(solution)/shard_map/ppermute | solution.py:84
  163.7 28.4 %collective-permute-start.27 = (bf16[3,512,256]{2,1,0:T(8,128)(2,1)}, bf16[3,512,256]{2,1,0:T(8,128)(2,1)S(1)}, u32[]{:S(2)}, u32[]{:S(2)}) collective-permute-start(bf16[3,512,256]{2,1,0:T(8,128)(2,1)} %get-tuple-element.199), channel_id=1, source_target_pairs={{0,12},{4,8},{8,4},{12,0},{1,13},{5,9},{9,5},{13,1},{2,14},{6,10},... | collective-permute-start | bytes 2359304 | tf_op jit(solution)/shard_map/ppermute | solution.py:76
  176.8 15.3 %copy-start.10 = (bf16[3,512,256]{2,1,0:T(8,128)(2,1)}, bf16[3,512,256]{2,1,0:T(8,128)(2,1)S(1)}, u32[]{:S(2)}) copy-start(bf16[3,512,256]{2,1,0:T(8,128)(2,1)S(1)} %collective-permute-done.22.refs_2_) | copy-start | bytes 2359300
  176.8 32.6 %collective-permute-start.33 = (bf16[3,512,256]{2,1,0:T(8,128)(2,1)S(1)}, bf16[3,512,256]{2,1,0:T(8,128)(2,1)}, u32[]{:S(2)}, u32[]{:S(2)}) collective-permute-start(bf16[3,512,256]{2,1,0:T(8,128)(2,1)S(1)} %collective-permute-done.22.refs_2_), channel_id=1, source_target_pairs={{0,16},{16,0},{1,17},{17,1},{2,18},{18,2},{3,19},{19,3},{4,20},{20... | collective-permute-start | bytes 2359304 | tf_op jit(solution)/shard_map/ppermute | solution.py:84
  177.5 32.7 %collective-permute-start.32 = (bf16[3,512,256]{2,1,0:T(8,128)(2,1)}, bf16[3,512,256]{2,1,0:T(8,128)(2,1)S(1)}, u32[]{:S(2)}, u32[]{:S(2)}) collective-permute-start(bf16[3,512,256]{2,1,0:T(8,128)(2,1)} %get-tuple-element.201), channel_id=1, source_target_pairs={{0,8},{4,12},{8,0},{12,4},{1,9},{5,13},{9,1},{13,5},{2,10},{6,14},... | collective-permute-start | bytes 2359304 | tf_op jit(solution)/shard_map/ppermute | solution.py:76
  192.2 17.3 %copy-start.12 = (bf16[3,512,256]{2,1,0:T(8,128)(2,1)}, bf16[3,512,256]{2,1,0:T(8,128)(2,1)S(1)}, u32[]{:S(2)}) copy-start(bf16[3,512,256]{2,1,0:T(8,128)(2,1)S(1)} %collective-permute-done.27.refs_3_) | copy-start | bytes 2359300
  192.2 37.0 %collective-permute-start.30 = (bf16[3,512,256]{2,1,0:T(8,128)(2,1)}, bf16[3,512,256]{2,1,0:T(8,128)(2,1)S(1)}, u32[]{:S(2)}, u32[]{:S(2)}) collective-permute-start(bf16[3,512,256]{2,1,0:T(8,128)(2,1)} %get-tuple-element.199), channel_id=1, source_target_pairs={{0,4},{4,0},{8,12},{12,8},{1,5},{5,1},{9,13},{13,9},{2,6},{6,2},{1... | collective-permute-start | bytes 2359304 | tf_op jit(solution)/shard_map/ppermute | solution.py:76
  193.9 37.0 %collective-permute-start.31 = (bf16[3,512,256]{2,1,0:T(8,128)(2,1)}, bf16[3,512,256]{2,1,0:T(8,128)(2,1)}, u32[]{:S(2)}, u32[]{:S(2)}) collective-permute-start(bf16[3,512,256]{2,1,0:T(8,128)(2,1)} %get-tuple-element.200), channel_id=1, source_target_pairs={{0,4},{4,0},{8,12},{12,8},{1,5},{5,1},{9,13},{13,9},{2,6},{6,2},{1... | collective-permute-start | bytes 2359304 | tf_op jit(solution)/shard_map/ppermute | solution.py:76
  193.9 37.0 %collective-permute-start.28 = (bf16[3,512,256]{2,1,0:T(8,128)(2,1)S(1)}, bf16[3,512,256]{2,1,0:T(8,128)(2,1)}, u32[]{:S(2)}, u32[]{:S(2)}) collective-permute-start(bf16[3,512,256]{2,1,0:T(8,128)(2,1)S(1)} %collective-permute-done.27.refs_3_), channel_id=1, source_target_pairs={{0,16},{16,0},{1,17},{17,1},{2,18},{18,2},{3,19},{19,3},{4,20},{20... | collective-permute-start | bytes 2359304 | tf_op jit(solution)/shard_map/ppermute | solution.py:84
  209.4 21.5 %collective-permute-start.29 = (bf16[3,512,256]{2,1,0:T(8,128)(2,1)}, bf16[3,512,256]{2,1,0:T(8,128)(2,1)}, u32[]{:S(2)}, u32[]{:S(2)}) collective-permute-start(bf16[3,512,256]{2,1,0:T(8,128)(2,1)} %get-tuple-element.206), channel_id=1, source_target_pairs={{0,12},{4,8},{8,4},{12,0},{1,13},{5,9},{9,5},{13,1},{2,14},{6,10},... | collective-permute-start | bytes 2359304 | tf_op jit(solution)/shard_map/ppermute | solution.py:76
  210.3 9.8 %copy-start.11 = (bf16[3,512,256]{2,1,0:T(8,128)(2,1)}, bf16[3,512,256]{2,1,0:T(8,128)(2,1)S(1)}, u32[]{:S(2)}) copy-start(bf16[3,512,256]{2,1,0:T(8,128)(2,1)S(1)} %collective-permute-done.32.refs_2_) | copy-start | bytes 2359300
  210.3 20.8 %collective-permute-start.34 = (bf16[3,512,256]{2,1,0:T(8,128)(2,1)S(1)}, bf16[3,512,256]{2,1,0:T(8,128)(2,1)}, u32[]{:S(2)}, u32[]{:S(2)}) collective-permute-start(bf16[3,512,256]{2,1,0:T(8,128)(2,1)S(1)} %collective-permute-done.32.refs_2_), channel_id=1, source_target_pairs={{0,16},{16,0},{1,17},{17,1},{2,18},{18,2},{3,19},{19,3},{4,20},{20... | collective-permute-start | bytes 2359304 | tf_op jit(solution)/shard_map/ppermute | solution.py:84
  229.2 20.6 %collective-permute-start.39 = (bf16[3,512,256]{2,1,0:T(8,128)(2,1)}, bf16[3,512,256]{2,1,0:T(8,128)(2,1)S(1)}, u32[]{:S(2)}, u32[]{:S(2)}) collective-permute-start(bf16[3,512,256]{2,1,0:T(8,128)(2,1)} %get-tuple-element.210), channel_id=1, source_target_pairs={{0,8},{4,12},{8,0},{12,4},{1,9},{5,13},{9,1},{13,5},{2,10},{6,14},... | collective-permute-start | bytes 2359304 | tf_op jit(solution)/shard_map/ppermute | solution.py:76
  231.1 19.6 %collective-permute-start.37 = (bf16[3,512,256]{2,1,0:T(8,128)(2,1)}, bf16[3,512,256]{2,1,0:T(8,128)(2,1)}, u32[]{:S(2)}, u32[]{:S(2)}) collective-permute-start(bf16[3,512,256]{2,1,0:T(8,128)(2,1)} %collective-permute-done.29.refs_3_), channel_id=1, source_target_pairs={{0,16},{16,0},{1,17},{17,1},{2,18},{18,2},{3,19},{19,3},{4,20},{20... | collective-permute-start | bytes 2359304 | tf_op jit(solution)/shard_map/ppermute | solution.py:84
  233.2 19.0 %collective-permute-start.35 = (bf16[3,512,256]{2,1,0:T(8,128)(2,1)}, bf16[3,512,256]{2,1,0:T(8,128)(2,1)}, u32[]{:S(2)}, u32[]{:S(2)}) collective-permute-start(bf16[3,512,256]{2,1,0:T(8,128)(2,1)} %get-tuple-element.206), channel_id=1, source_target_pairs={{0,4},{4,0},{8,12},{12,8},{1,5},{5,1},{9,13},{13,9},{2,6},{6,2},{1... | collective-permute-start | bytes 2359304 | tf_op jit(solution)/shard_map/ppermute | solution.py:76
  233.2 19.0 %collective-permute-start.36 = (bf16[3,512,256]{2,1,0:T(8,128)(2,1)}, bf16[3,512,256]{2,1,0:T(8,128)(2,1)}, u32[]{:S(2)}, u32[]{:S(2)}) collective-permute-start(bf16[3,512,256]{2,1,0:T(8,128)(2,1)} %get-tuple-element.207), channel_id=1, source_target_pairs={{0,4},{4,0},{8,12},{12,8},{1,5},{5,1},{9,13},{13,9},{2,6},{6,2},{1... | collective-permute-start | bytes 2359304 | tf_op jit(solution)/shard_map/ppermute | solution.py:76
  233.8 33.3 %collective-permute-start.38 = (bf16[3,512,256]{2,1,0:T(8,128)(2,1)}, bf16[3,512,256]{2,1,0:T(8,128)(2,1)S(1)}, u32[]{:S(2)}, u32[]{:S(2)}) collective-permute-start(bf16[3,512,256]{2,1,0:T(8,128)(2,1)} %get-tuple-element.216), channel_id=1, source_target_pairs={{0,12},{4,8},{8,4},{12,0},{1,13},{5,9},{9,5},{13,1},{2,14},{6,10},... | collective-permute-start | bytes 2359304 | tf_op jit(solution)/shard_map/ppermute | solution.py:76
  249.8 17.3 %copy-start.13 = (bf16[3,512,256]{2,1,0:T(8,128)(2,1)}, bf16[3,512,256]{2,1,0:T(8,128)(2,1)S(1)}, u32[]{:S(2)}) copy-start(bf16[3,512,256]{2,1,0:T(8,128)(2,1)S(1)} %collective-permute-done.39.refs_2_) | copy-start | bytes 2359300
  250.7 18.4 %collective-permute-start.40 = (bf16[3,512,256]{2,1,0:T(8,128)(2,1)S(1)}, bf16[3,512,256]{2,1,0:T(8,128)(2,1)S(1)}, u32[]{:S(2)}, u32[]{:S(2)}) collective-permute-start(bf16[3,512,256]{2,1,0:T(8,128)(2,1)S(1)} %collective-permute-done.39.refs_2_), channel_id=1, source_target_pairs={{0,16},{16,0},{1,17},{17,1},{2,18},{18,2},{3,19},{19,3},{4,20},{20... | collective-permute-start | bytes 2359304 | tf_op jit(solution)/shard_map/ppermute | solution.py:84
  252.3 19.3 %copy-start = (f32[1024,128]{1,0:T(8,128)S(1)}, f32[1024,128]{1,0:T(8,128)}, u32[]{:S(2)}) copy-start(f32[1024,128]{1,0:T(8,128)} %shard_map.97) | copy-start | bytes 1572868
  267.1 5.8 %copy-start.15 = (bf16[3,512,256]{2,1,0:T(8,128)(2,1)}, bf16[3,512,256]{2,1,0:T(8,128)(2,1)S(1)}, u32[]{:S(2)}) copy-start(bf16[3,512,256]{2,1,0:T(8,128)(2,1)S(1)} %collective-permute-done.38.refs_3_) | copy-start | bytes 2359300
  269.1 2.6 collective-permute-start.41
  269.1 3.7 %collective-permute-start.42 = (bf16[3,512,256]{2,1,0:T(8,128)(2,1)}, bf16[3,512,256]{2,1,0:T(8,128)(2,1)}, u32[]{:S(2)}, u32[]{:S(2)}) collective-permute-start(bf16[3,512,256]{2,1,0:T(8,128)(2,1)} %get-tuple-element.217), channel_id=1, source_target_pairs={{0,4},{4,0},{8,12},{12,8},{1,5},{5,1},{9,13},{13,9},{2,6},{6,2},{1... | collective-permute-start | bytes 2359304 | tf_op jit(solution)/shard_map/ppermute | solution.py:76
  269.7 19.4 %collective-permute-start.43 = (bf16[3,512,256]{2,1,0:T(8,128)(2,1)S(1)}, bf16[3,512,256]{2,1,0:T(8,128)(2,1)S(1)}, u32[]{:S(2)}, u32[]{:S(2)}) collective-permute-start(bf16[3,512,256]{2,1,0:T(8,128)(2,1)S(1)} %collective-permute-done.38.refs_3_), channel_id=1, source_target_pairs={{0,16},{16,0},{1,17},{17,1},{2,18},{18,2},{3,19},{19,3},{4,20},{20... | collective-permute-start | bytes 2359304 | tf_op jit(solution)/shard_map/ppermute | solution.py:84
  290.0 8.6 %copy-start.18 = (f32[1024,64]{1,0:T(8,128)S(1)}, f32[1024,64]{1,0:T(8,128)}, u32[]{:S(2)}) copy-start(f32[1024,64]{1,0:T(8,128)} %get-tuple-element.222) | copy-start | bytes 786436
  296.9 13.1 %copy-start.9 = (bf16[1,2,8,12288]{3,2,1,0:T(8,128)(2,1)S(1)}, bf16[1,2,8,12288]{3,2,1,0:T(8,128)(2,1)}, u32[]{:S(2)}) copy-start(bf16[1,2,8,12288]{3,2,1,0:T(8,128)(2,1)} %get-tuple-element.230) | copy-start | bytes 1179652
  296.9 13.1 %copy-start.20 = (bf16[2,8,12288]{2,1,0:T(8,128)(2,1)S(1)}, bf16[2,8,12288]{2,1,0:T(8,128)(2,1)}, u32[]{:S(2)}) copy-start(bf16[2,8,12288]{2,1,0:T(8,128)(2,1)} %copy-done.19) | copy-start | bytes 1179652
  300.7 1.4 collective-permute-start.44
  302.1 4.9 %collective-permute-start.45 = (f32[2,12288]{1,0:T(2,128)S(1)}, f32[2,12288]{1,0:T(2,128)S(1)}, u32[]{:S(2)}, u32[]{:S(2)}) collective-permute-start(f32[2,12288]{1,0:T(2,128)S(1)} %bitcast_add_fusion), channel_id=1, source_target_pairs={{0,1},{1,0},{2,3},{3,2},{4,5},{5,4},{6,7},{7,6},{8,9},{9,8},{10,11... | collective-permute-start | bytes 294920 | tf_op jit(solution)/shard_map/ppermute | solution.py:80
  307.1 7.2 %collective-permute-start.46 = (f32[2,12288]{1,0:T(2,128)S(1)}, f32[2,12288]{1,0:T(2,128)S(1)}, u32[]{:S(2)}, u32[]{:S(2)}) collective-permute-start(f32[2,12288]{1,0:T(2,128)S(1)} %add.75), channel_id=1, source_target_pairs={{0,2},{1,3},{2,0},{3,1},{4,6},{5,7},{6,4},{7,5},{8,10},{9,11},{10,... | collective-permute-start | bytes 294920 | tf_op jit(solution)/shard_map/ppermute | solution.py:80
  (7 other events, 23.9 us)
Sparse Core Ops, SparseCore 0:
  9.0 84.7 all-gather.4
  95.3 81.1 all-gather.6
